TPU v7x, 32 devices: a whole 2x2x4 slice. The times are simulated.
32 devices in a mesh: groups: 2 (over y), space: 4 (over x, core), chan: 4 (over z).
Axes of the slice: x: 2, y: 2, z: 4, core: 2. Of those that a mesh axis runs over, the one named last changes fastest.
Arguments:
- fields: bfloat16 [1024, 16, 256], P('chan', ('groups', 'space')), parts along dimension 1, may hold values from -6 to 6
- conv_weight: bfloat16 [27, 1024, 1024], P(None, 'chan', 'space'), may hold values from -0.0390625 to 0.0390625
Outputs:
- convolved: bfloat16 [1024, 16, 256], P('chan', ('groups', 'space')), parts along dimension 1
There are 2 independent parts, one for each index of `groups`. A program takes and returns all parts, laid end to end along the dimension named above; an argument that names none is the same for every part. Nothing has to cross between parts.
All inputs are finite; a program needn't handle non-finite values.
Results may differ from a plain program's by a relative error of at most 0.001.
Values may be sent and summed in bfloat16 or wider, within the bound.
No kernel may reach another device: no remote copies, remote signals or barrier semaphores. Data moves between devices by JAX's collectives and lax.ppermute only.
A program may use at most 128 MiB of HBM per device.

v0:
```python
import jax
import jax.numpy as jnp
from jax import lax
from jax.sharding import PartitionSpec as P

NY = 16
NZ = 16


def padded_2(block, sides, width):
    for axis, dim in sides:
        count = lax.axis_size(axis)
        forward = [(i, i + 1) for i in range(count - 1)]
        backward = [(target, source) for source, target in forward]
        low = lax.ppermute(
            lax.slice_in_dim(block, block.shape[dim] - width, None, axis=dim), axis, forward
        )
        high = lax.ppermute(lax.slice_in_dim(block, 0, width, axis=dim), axis, backward)
        block = jnp.concatenate([low, block, high], axis=dim)
    return block


def convolve_block(summed, block, weights):
    count = block.shape[0]
    depth = block.shape[1] - 2
    shaped = block.reshape(count, depth + 2, NY, NZ)
    padded = jnp.pad(shaped, ((0, 0), (0, 0), (1, 1), (1, 1)))
    for step_x in range(3):
        for step_y in range(3):
            for step_z in range(3):
                window = padded[
                    :, step_x : step_x + depth, step_y : step_y + NY, step_z : step_z + NZ
                ].reshape(count, depth * NY * NZ)
                summed = summed + jnp.dot(
                    weights[9 * step_x + 3 * step_y + step_z],
                    window,
                    preferred_element_type=jnp.float32,
                )
    return summed


def local(fields, conv_weight):
    depth = fields.shape[1]
    owned = conv_weight.shape[1]
    weights = lax.all_gather(conv_weight, "space", axis=2, tiled=True)
    empty = jnp.zeros((owned, depth * NY * NZ), jnp.float32)
    gathered = lax.all_gather(fields, "chan", axis=0, tiled=True)
    framed = padded_2(gathered, (("space", 1),), 1)
    summed = convolve_block(empty, framed, weights)
    return summed.reshape(owned, depth, NY * NZ).astype(jnp.bfloat16)


def solution(mesh):
    return jax.shard_map(
        local,
        mesh=mesh,
        in_specs=(P("chan", ("groups", "space"), None), P(None, "chan", "space")),
        out_specs=P("chan", ("groups", "space"), None),
        check_vma=False,
    )
```

profile of v0, /device:TPU:0, one launch (start us, length us, event | category | flops | bytes accessed | tf_op | source)
XLA Modules:
  0.0 168.5 jit_solution(9444668171630820183)
XLA Ops:
  6.5 0.0 all-gather.3.cloned.1.call-start
  6.5 1.8 %copy.4 = bf16[256,2,256]{0,2,1:T(8,128)(2,1)} copy(bf16[256,2,256]{2,1,0:T(2,128)(2,1)} %param.2) | data formatting | bytes 524288 | tf_op args[0]
  8.3 0.0 all-gather.3.cloned.1.call-update
  8.4 0.0 all-gather.5.cloned.1.call-start
  8.4 0.7 all-gather.5.cloned.1.call-update
  9.1 32.7 %all-gather.3.cloned.1.call-done = bf16[1024,2,256]{0,2,1:T(8,128)(2,1)} async-done(((bf16[256,2,256]{0,2,1:T(8,128)(2,1)}), bf16[1024,2,256]{0,2,1:T(8,128)(2,1)}) %all-gather.3.cloned.1.call-update) | async-done | bytes 1048592 | tf_op jit(solution)/shard_map/all_gather | solution.py:47
  41.8 1.3 fusion.13
  43.1 1.3 collective-permute-start.1
  44.4 3.1 %collective-permute-start = (bf16[1024,1,256]{0,2,1:T(8,128)(2,1)S(1)}, bf16[1024,1,256]{0,2,1:T(8,128)(2,1)S(1)}, u32[]{:S(2)}, u32[]{:S(2)}) collective-permute-start(bf16[1024,1,256]{0,2,1:T(8,128)(2,1)S(1)} %get-tuple-element.32), channel_id=1, source_target_pairs={{0,4},{4,8},{8,12},{1,5},{5,9},{9,13},{2,6},{6,10},{10,14},{3,7},{... | collective-permute-start | bytes 1572872 | tf_op jit(solution)/shard_map/ppermute | solution.py:15
  47.5 0.0 collective-permute-done.1
  47.5 1.5 collective-permute-done
  49.0 1.6 pad_maximum_fusion
  50.6 3.3 %pad_slice_fusion.1 = (bf16[1024,2,16,16]{0,3,2,1:T(8,128)(2,1)S(1)}, bf16[1024,2,16,16]{0,3,2,1:T(8,128)(2,1)}, bf16[1024,2,16,16]{0,3,2,1:T(8,128)(2,1)S(1)}, ...) fusion(bf16[1024,4,16,16]{0,3,2,1:T(8,128)(2,1)S(1)} %bitcast.181), kind=kLoop, calls=%fused_computation.1 | loop fusion | bytes 13631488 | tf_op jit(solution)/shard_map/slice | solution.py:31
  54.0 7.4 %pad_slice_fusion = (bf16[1024,2,16,16]{0,3,2,1:T(8,128)(2,1)}, bf16[1024,2,16,16]{0,3,2,1:T(8,128)(2,1)}, bf16[1024,2,16,16]{0,3,2,1:T(8,128)(2,1)}, bf16[1024,...) fusion(bf16[1024,4,16,16]{0,3,2,1:T(8,128)(2,1)S(1)} %bitcast.182), kind=kLoop, calls=%fused_computation | loop fusion | bytes 22020096 | tf_op jit(solution)/shard_map/slice | solution.py:31
  61.3 73.3 %all-gather.5.cloned.1.call-done = bf16[27,256,1024]{2,1,0:T(8,128)(2,1)} async-done(((bf16[27,256,256]{2,1,0:T(8,128)(2,1)}), bf16[27,256,1024]{2,1,0:T(8,128)(2,1)}) %all-gather.5.cloned.1.call-update) | async-done | bytes 14155792 | tf_op jit(solution)/shard_map/all_gather | solution.py:45
  134.7 2.0 %convolution_bitcast_fusion.8 = f32[256,512]{0,1:T(8,128)S(1)} fusion(bf16[1024,512]{0,1:T(8,128)(2,1)} %bitcast.210, bf16[27,256,1024]{2,1,0:T(8,128)(2,1)} %all-gather.5.cloned.1.call-done), kind=kOutput, calls=%fused_computation.59 | convolution fusion | flops 268435456 | bytes 2097152 | tf_op jit(solution)/shard_map/dot_general | solution.py:34
  136.7 2.6 %convolution_bitcast_fusion.9 = f32[256,512]{0,1:T(8,128)S(1)} fusion(bf16[1024,512]{0,1:T(8,128)(2,1)} %bitcast.209, bf16[27,256,1024]{2,1,0:T(8,128)(2,1)} %all-gather.5.cloned.1.call-done), kind=kOutput, calls=%fused_computation.60 | convolution fusion | flops 268435456 | bytes 2097152 | tf_op jit(solution)/shard_map/dot_general | solution.py:34
  139.3 2.6 %fusion.12 = f32[512,256]{1,0:T(8,128)S(1)} fusion(bf16[1024,512]{0,1:T(8,128)(2,1)} %bitcast.208, bf16[27,256,1024]{2,1,0:T(8,128)(2,1)} %all-gather.5.cloned.1.call-done), kind=kOutput, calls=%fused_computation.89 | convolution fusion | flops 268435456 | bytes 2097152 | tf_op jit(solution)/shard_map/dot_general | solution.py:34
  142.0 1.9 %convolution_add_fusion.15 = f32[512,256]{1,0:T(8,128)S(1)} fusion(f32[512,256]{1,0:T(8,128)S(1)} %fusion.12, bf16[1024,512]{0,1:T(8,128)(2,1)} %bitcast.190, bf16[27,256,1024]{2,1,0:T(8,128)(2,1)} %all-gather.5.cloned.1.call-done), kind=kOutput, calls=%fused_computation.41 | convolution fusion | flops 268566528 | bytes 2621440 | tf_op jit(solution)/shard_map/dot_general | solution.py:34
  143.9 1.9 %convolution_add_fusion.14 = f32[512,256]{1,0:T(8,128)S(1)} fusion(f32[512,256]{1,0:T(8,128)S(1)} %convolution_add_fusion.15, bf16[1024,512]{0,1:T(8,128)(2,1)} %bitcast.206, bf16[27,256,1024]{2,1,0:T(8,128)(2,1)} %all-gather.5.cloned.1.call-done), kind=kOutput, calls=%fused_computation.40 | convolution fusion | flops 268566528 | bytes 2621440 | tf_op jit(solution)/shard_map/dot_general | solution.py:34
  145.8 0.0 copy-start.9
  145.8 1.9 %convolution_add_fusion.13 = f32[512,256]{1,0:T(8,128)S(1)} fusion(f32[512,256]{1,0:T(8,128)S(1)} %convolution_add_fusion.14, bf16[1024,512]{0,1:T(8,128)(2,1)} %bitcast.205, bf16[27,256,1024]{2,1,0:T(8,128)(2,1)} %all-gather.5.cloned.1.call-done), kind=kOutput, calls=%fused_computation.39 | convolution fusion | flops 268566528 | bytes 2621440 | tf_op jit(solution)/shard_map/dot_general | solution.py:34
  147.8 1.8 %convolution_add_fusion.12 = f32[512,256]{1,0:T(8,128)S(1)} fusion(f32[512,256]{1,0:T(8,128)S(1)} %convolution_add_fusion.13, bf16[1024,512]{0,1:T(8,128)(2,1)} %bitcast.189, bf16[27,256,1024]{2,1,0:T(8,128)(2,1)S(1)} %copy-done), kind=kOutput, calls=%fused_computation.38 | convolution fusion | flops 268566528 | bytes 2621440 | tf_op jit(solution)/shard_map/dot_general | solution.py:34
  149.6 1.8 %convolution_add_fusion.11 = f32[512,256]{1,0:T(8,128)S(1)} fusion(f32[512,256]{1,0:T(8,128)S(1)} %convolution_add_fusion.12, bf16[1024,512]{0,1:T(8,128)(2,1)} %bitcast.204, bf16[27,256,1024]{2,1,0:T(8,128)(2,1)S(1)} %copy-done), kind=kOutput, calls=%fused_computation.37 | convolution fusion | flops 268566528 | bytes 2621440 | tf_op jit(solution)/shard_map/dot_general | solution.py:34
  151.4 0.0 copy-done.16
  151.4 0.5 convolution_add_fusion.10
  151.9 0.0 copy-start.7
  151.9 0.0 copy-done.15
  151.9 0.5 convolution_add_fusion.9
  152.4 0.5 convolution_add_fusion.8
  152.9 0.5 convolution_add_fusion.7
  153.4 0.5 convolution_add_fusion.6
  153.9 0.5 convolution_add_fusion.5
  154.4 0.5 convolution_add_fusion.4
  154.9 0.0 copy-done.3
  154.9 0.5 convolution_add_fusion.3
  155.4 0.5 convolution_add_fusion.2
  155.9 0.5 convolution_add_fusion.1
  156.4 0.5 fusion.10
  156.9 0.5 fusion.9
  157.4 0.5 fusion.8
  157.9 0.5 fusion.7
  158.4 0.5 fusion.6
  158.8 0.5 fusion.5
  159.3 0.5 fusion.4
  159.8 0.5 fusion.3
  160.3 0.5 fusion.11
  160.8 0.9 copy.5
  (29 shorter events, 0.1 us)
Async XLA Ops:
  6.5 35.3 %all-gather.3.cloned.1.call-start = ((), (), s32[]{:S(2)}) async-start(), calls=%async_computation | async-start | bytes 1310720 | tf_op jit(solution)/shard_map/all_gather | solution.py:47
  8.4 126.3 %all-gather.5.cloned.1.call-start = ((), (), s32[]{:S(2)}) async-start(), calls=%async_computation.1 | async-start | bytes 17694720 | tf_op jit(solution)/shard_map/all_gather | solution.py:45
  43.1 4.4 %collective-permute-start.1 = (bf16[1024,1,256]{0,2,1:T(8,128)(2,1)S(1)}, bf16[1024,1,256]{0,2,1:T(8,128)(2,1)S(1)}, u32[]{:S(2)}, u32[]{:S(2)}) collective-permute-start(bf16[1024,1,256]{0,2,1:T(8,128)(2,1)S(1)} %get-tuple-element.33), channel_id=1, source_target_pairs={{4,0},{8,4},{12,8},{5,1},{9,5},{13,9},{6,2},{10,6},{14,10},{7,3},{... | collective-permute-start | bytes 1572872 | tf_op jit(solution)/shard_map/ppermute | solution.py:18
  44.4 4.6 %collective-permute-start = (bf16[1024,1,256]{0,2,1:T(8,128)(2,1)S(1)}, bf16[1024,1,256]{0,2,1:T(8,128)(2,1)S(1)}, u32[]{:S(2)}, u32[]{:S(2)}) collective-permute-start(bf16[1024,1,256]{0,2,1:T(8,128)(2,1)S(1)} %get-tuple-element.32), channel_id=1, source_target_pairs={{0,4},{4,8},{8,12},{1,5},{5,9},{9,13},{2,6},{6,10},{10,14},{3,7},{... | collective-permute-start | bytes 1572872 | tf_op jit(solution)/shard_map/ppermute | solution.py:15
  134.7 13.1 %copy-start = (bf16[27,256,1024]{2,1,0:T(8,128)(2,1)S(1)}, bf16[27,256,1024]{2,1,0:T(8,128)(2,1)}, u32[]{:S(2)}) copy-start(bf16[27,256,1024]{2,1,0:T(8,128)(2,1)} %all-gather.5.cloned.1.call-done) | copy-start | bytes 42467332
  134.7 16.7 %copy-start.16 = (bf16[1024,2,16,16]{0,3,2,1:T(8,128)(2,1)S(1)}, bf16[1024,2,16,16]{0,3,2,1:T(8,128)(2,1)}, u32[]{:S(2)}) copy-start(bf16[1024,2,16,16]{0,3,2,1:T(8,128)(2,1)} %get-tuple-element.10) | copy-start | bytes 3145732
  134.7 17.2 %copy-start.15 = (bf16[1024,2,16,16]{0,3,2,1:T(8,128)(2,1)S(1)}, bf16[1024,2,16,16]{0,3,2,1:T(8,128)(2,1)}, u32[]{:S(2)}) copy-start(bf16[1024,2,16,16]{0,3,2,1:T(8,128)(2,1)} %get-tuple-element.11) | copy-start | bytes 3145732
  134.7 17.7 %copy-start.14 = (bf16[1024,2,16,16]{0,3,2,1:T(8,128)(2,1)S(1)}, bf16[1024,2,16,16]{0,3,2,1:T(8,128)(2,1)}, u32[]{:S(2)}) copy-start(bf16[1024,2,16,16]{0,3,2,1:T(8,128)(2,1)} %get-tuple-element.12) | copy-start | bytes 3145732
  134.7 18.2 %copy-start.13 = (bf16[1024,2,16,16]{0,3,2,1:T(8,128)(2,1)S(1)}, bf16[1024,2,16,16]{0,3,2,1:T(8,128)(2,1)}, u32[]{:S(2)}) copy-start(bf16[1024,2,16,16]{0,3,2,1:T(8,128)(2,1)} %get-tuple-element.13) | copy-start | bytes 3145732
  136.7 16.7 %copy-start.12 = (bf16[1024,2,16,16]{0,3,2,1:T(8,128)(2,1)S(1)}, bf16[1024,2,16,16]{0,3,2,1:T(8,128)(2,1)}, u32[]{:S(2)}) copy-start(bf16[1024,2,16,16]{0,3,2,1:T(8,128)(2,1)} %get-tuple-element.14) | copy-start | bytes 3145732
  139.3 14.6 %copy-start.11 = (bf16[1024,2,16,16]{0,3,2,1:T(8,128)(2,1)S(1)}, bf16[1024,2,16,16]{0,3,2,1:T(8,128)(2,1)}, u32[]{:S(2)}) copy-start(bf16[1024,2,16,16]{0,3,2,1:T(8,128)(2,1)} %get-tuple-element.15) | copy-start | bytes 3145732
  141.9 12.4 %copy-start.10 = (bf16[1024,2,16,16]{0,3,2,1:T(8,128)(2,1)S(1)}, bf16[1024,2,16,16]{0,3,2,1:T(8,128)(2,1)}, u32[]{:S(2)}) copy-start(bf16[1024,2,16,16]{0,3,2,1:T(8,128)(2,1)} %get-tuple-element.16) | copy-start | bytes 3145732
  143.9 11.0 %copy-start.3 = (bf16[1024,2,16,16]{0,3,2,1:T(8,128)(2,1)S(1)}, bf16[1024,2,16,16]{0,3,2,1:T(8,128)(2,1)}, u32[]{:S(2)}) copy-start(bf16[1024,2,16,16]{0,3,2,1:T(8,128)(2,1)} %get-tuple-element.29) | copy-start | bytes 3145732
  145.8 9.6 %copy-start.9 = (bf16[1024,2,16,16]{0,3,2,1:T(8,128)(2,1)S(1)}, bf16[1024,2,16,16]{0,3,2,1:T(8,128)(2,1)}, u32[]{:S(2)}) copy-start(bf16[1024,2,16,16]{0,3,2,1:T(8,128)(2,1)} %get-tuple-element.17) | copy-start | bytes 3145732
  147.8 8.1 %copy-start.8 = (bf16[1024,2,16,16]{0,3,2,1:T(8,128)(2,1)S(1)}, bf16[1024,2,16,16]{0,3,2,1:T(8,128)(2,1)}, u32[]{:S(2)}) copy-start(bf16[1024,2,16,16]{0,3,2,1:T(8,128)(2,1)} %get-tuple-element.18) | copy-start | bytes 3145732
  149.6 6.8 %copy-start.4 = (bf16[1024,2,16,16]{0,3,2,1:T(8,128)(2,1)S(1)}, bf16[1024,2,16,16]{0,3,2,1:T(8,128)(2,1)}, u32[]{:S(2)}) copy-start(bf16[1024,2,16,16]{0,3,2,1:T(8,128)(2,1)} %get-tuple-element.19) | copy-start | bytes 3145732
  151.9 5.0 %copy-start.7 = (bf16[1024,2,16,16]{0,3,2,1:T(8,128)(2,1)S(1)}, bf16[1024,2,16,16]{0,3,2,1:T(8,128)(2,1)}, u32[]{:S(2)}) copy-start(bf16[1024,2,16,16]{0,3,2,1:T(8,128)(2,1)} %get-tuple-element.22) | copy-start | bytes 3145732
  152.4 5.0 %copy-start.6 = (bf16[1024,2,16,16]{0,3,2,1:T(8,128)(2,1)S(1)}, bf16[1024,2,16,16]{0,3,2,1:T(8,128)(2,1)}, u32[]{:S(2)}) copy-start(bf16[1024,2,16,16]{0,3,2,1:T(8,128)(2,1)} %get-tuple-element.23) | copy-start | bytes 3145732
  152.9 5.0 %copy-start.2 = (bf16[1024,2,16,16]{0,3,2,1:T(8,128)(2,1)S(1)}, bf16[1024,2,16,16]{0,3,2,1:T(8,128)(2,1)}, u32[]{:S(2)}) copy-start(bf16[1024,2,16,16]{0,3,2,1:T(8,128)(2,1)} %get-tuple-element.25) | copy-start | bytes 3145732
  153.4 5.0 %copy-start.1 = (bf16[1024,2,16,16]{0,3,2,1:T(8,128)(2,1)S(1)}, bf16[1024,2,16,16]{0,3,2,1:T(8,128)(2,1)}, u32[]{:S(2)}) copy-start(bf16[1024,2,16,16]{0,3,2,1:T(8,128)(2,1)} %get-tuple-element.28) | copy-start | bytes 3145732
  155.4 4.9 %copy-start.5 = (bf16[1024,2,16,16]{0,3,2,1:T(8,128)(2,1)S(1)}, bf16[1024,2,16,16]{0,3,2,1:T(8,128)(2,1)}, u32[]{:S(2)}) copy-start(bf16[1024,2,16,16]{0,3,2,1:T(8,128)(2,1)} %get-tuple-element.5) | copy-start | bytes 3145732
Sparse Core Ops, SparseCore 0:
  8.9 32.8 all-gather.2
  43.4 91.2 all-gather.4
where the time goes:
time: 169 us
  waiting for transfers between devices  108 us (64%)
  matrix products  25.6 us (15%)
  local copies, waits for them, and re-layouts  14.7 us (9%)
  between operations  13.9 us (8%)
  starting transfers between devices  4.4 us (3%)
    all_gather x1, waiting for transfers between devices, local(): weights = lax.all_gather(conv_weight, 'space', axis=2, tiled=True)  73.3 us
    all_gather x1, waiting for transfers between devices, local(): gathered = lax.all_gather(fields, 'chan', axis=0, tiled=True)  32.7 us
    dot_general x27, matrix products, convolve_block(): jnp.dot(weights[9 * step_x + 3 * step_y + step_z], window, preferred_elem...  25.6 us
    slice x2, local copies, waits for them, and re-layouts, convolve_block(): padded[:, step_x:step_x + depth, step_y:step_y + NY, step_z:step_z + NZ]  10.7 us
  transfers between devices with their start and end apart: 4, of which 3 were waited for; matrix products, arithmetic and copies ran while one was open for 8% of the time, Pallas kernels for 0%

commit v1 on v0

v1 whole, which is shorter than its diff:
```python
import functools

import jax
import jax.numpy as jnp
from jax import lax
from jax.experimental import pallas as pl
from jax.experimental.pallas import tpu as pltpu
from jax.sharding import PartitionSpec as P

NY = 16
NZ = 16
CUTS = (0, 9, 16)
VMEM_LIMIT = 48 * 2**20


def bit_count(n):
    return n.bit_length() - 1


def reversed_bits(value, bits):
    out = 0
    for bit in range(bits):
        out = out | (((value >> bit) & 1) << (bits - 1 - bit))
    return out


def transpose_kernel(cuts, fields_ref, *out_refs):
    for plane in range(fields_ref.shape[1]):
        turned = fields_ref[:, plane, :].T
        for out_ref, low, high in zip(out_refs, cuts, cuts[1:]):
            out_ref[plane] = turned[low * NZ : high * NZ]


def by_cell(fields, cuts):
    count, depth, _ = fields.shape
    return pl.pallas_call(
        functools.partial(transpose_kernel, cuts),
        out_shape=[
            jax.ShapeDtypeStruct((depth, (high - low) * NZ, count), fields.dtype)
            for low, high in zip(cuts, cuts[1:])
        ],
        name="by_cell",
    )(fields)


def shifted(value, step):
    rows = value.shape[0]
    z = lax.broadcasted_iota(jnp.int32, value.shape, 0) % NZ
    inside = (z != NZ - 1) if step > 0 else (z != 0)
    rolled = pltpu.roll(value.astype(jnp.float32), (-step) % rows, 0)
    return jnp.where(inside, rolled, 0.0).astype(value.dtype)


def partial_kernel(plan, place_ref, *refs):
    ns, nc, cuts, index = plan
    repeats = nc // ns
    bits = bit_count(ns)
    low, high = cuts[index], cuts[index + 1]
    first = max(low - 1, 0)
    last = high if high == NY else high - 1
    top = first - 1
    part_refs = refs[: nc * (2 if index else 1)]
    weight_ref, mate_ref, keep_ref, window_ref = refs[len(part_refs) :]
    older_refs, newer_refs = part_refs[:-nc], part_refs[-nc:]
    depth = newer_refs[0].shape[0]
    count = newer_refs[0].shape[2]
    taken = repeats * count
    planes = ns * depth
    space, chan = place_ref[0], place_ref[1]
    zeros = jnp.zeros(window_ref.shape[1:], window_ref.dtype)
    window_ref[0] = zeros
    window_ref[planes + 1] = zeros
    edge = jnp.zeros((planes, NZ, window_ref.shape[2]), window_ref.dtype)
    if top < 0:
        window_ref[1 : planes + 1, 0:NZ, :] = edge
    if last == NY:
        window_ref[1 : planes + 1, (NY - top) * NZ : (NY - top + 1) * NZ, :] = edge

    def put(values, row, plane, turn):
        rows = values.shape[0]
        for step in range(3):
            piece = values if step == 1 else shifted(values, step - 1)
            for slot in range(repeats):
                begin = step * taken + slot * count

                def store():
                    window_ref[
                        plane, (row - top) * NZ : (row - top) * NZ + rows, begin : begin + count
                    ] = piece

                if repeats == 1:
                    store()
                else:
                    pl.when(turn == slot)(store)

    for round_index in range(nc):
        mask, jump = round_index % ns, round_index // ns
        source = reversed_bits((chan % ns) ^ mask, bits)
        turn = (jump + chan // ns) % repeats
        for plane in range(depth):
            where = 1 + source * depth + plane
            if index:
                begin = max(top, 0)
                older = older_refs[round_index]
                put(older[plane, (begin - cuts[index - 1]) * NZ :, :], begin, where, turn)
            put(newer_refs[round_index][plane], low, where, turn)

    half = ns // 2
    cells = (last - first) * NZ
    for position in range(ns):
        order = position % half
        owner = space ^ (2 * (half - 1 - order) + (1 if position < half else 0))
        total = None
        for pair in range(9):
            a, b = divmod(pair, 3)
            left = window_ref[
                pl.ds(depth * owner + a, depth), b * NZ : b * NZ + cells, :
            ].reshape(depth * cells, 3 * taken)
            right = jnp.concatenate([weight_ref[3 * pair + c] for c in range(3)], axis=1)
            product = lax.dot_general(
                left, right, (((1,), (1,)), ((), ())), preferred_element_type=jnp.float32
            )
            total = product if total is None else total + product
        target = mate_ref if position < half else keep_ref
        target[order * depth : (order + 1) * depth] = total.reshape(depth, cells, -1)


def partial_sums(place, older, newer, weights, plan):
    ns, nc, cuts, index = plan
    low, high = cuts[index], cuts[index + 1]
    first = max(low - 1, 0)
    last = high if high == NY else high - 1
    depth, _, count = newer[0].shape
    owned, taken = weights.shape[1:]
    cells = (last - first) * NZ
    in_vmem = pl.BlockSpec(memory_space=pltpu.VMEM)
    parts = [*older, *newer]
    flops = 2 * 27 * ns * depth * cells * owned * taken
    return pl.pallas_call(
        functools.partial(partial_kernel, plan),
        out_shape=[jax.ShapeDtypeStruct((ns // 2 * depth, cells, owned), jnp.float32)] * 2,
        in_specs=[pl.BlockSpec(memory_space=pltpu.SMEM)] + [in_vmem] * (len(parts) + 1),
        out_specs=[in_vmem] * 2,
        scratch_shapes=[
            pltpu.VMEM((ns * depth + 2, cells + 2 * NZ, 3 * taken), newer[0].dtype)
        ],
        compiler_params=pltpu.CompilerParams(vmem_limit_bytes=VMEM_LIMIT),
        cost_estimate=pl.CostEstimate(
            flops=flops, bytes_accessed=2 * weights.size, transcendentals=0
        ),
        name="partial_sums",
    )(place, *parts, weights)


def finish_kernel(counts, *refs):
    out_ref = refs[-1]
    for plane in range(out_ref.shape[1]):
        at = 0
        begin = 0
        for count in counts:
            pieces = refs[at : at + count]
            at += count
            total = pieces[0][plane]
            for piece in pieces[1:]:
                total = total + piece[plane]
            turned = total.T.astype(out_ref.dtype)
            out_ref[:, plane, begin : begin + turned.shape[1]] = turned
            begin += turned.shape[1]


def finish(groups, dtype):
    depth, _, owned = groups[0][0].shape
    cells = sum(pieces[0].shape[1] for pieces in groups)
    return pl.pallas_call(
        functools.partial(finish_kernel, [len(pieces) for pieces in groups]),
        out_shape=jax.ShapeDtypeStruct((owned, depth, cells), dtype),
        name="finish",
    )(*[piece for pieces in groups for piece in pieces])


def swapped(value, bit, ns):
    return lax.ppermute(value, "space", [(i, i ^ (1 << bit)) for i in range(ns)])


def local(fields, conv_weight):
    ns, nc = lax.axis_size("space"), lax.axis_size("chan")
    repeats = nc // ns
    bits = bit_count(ns)
    depth = fields.shape[1]
    place = jnp.stack([lax.axis_index("space"), lax.axis_index("chan")]).astype(jnp.int32)
    blocks = by_cell(fields, CUTS)
    received = []
    for index, block in enumerate(blocks):
        arrived = []
        for round_index in range(nc):
            mask, jump = round_index % ns, round_index // ns
            pairs = []
            for s in range(ns):
                for z in range(nc):
                    source = reversed_bits((z % ns) ^ mask, bits)
                    turn = (jump + z // ns) % repeats
                    pairs.append((source * nc + s * repeats + turn, s * nc + z))
            operand = block
            if index:
                operand, received[-1][round_index] = lax.optimization_barrier(
                    (block, received[-1][round_index])
                )
            arrived.append(lax.ppermute(operand, ("space", "chan"), pairs))
        received.append(arrived)
    groups = []
    for index, newer in enumerate(received):
        older = received[index - 1] if index else []
        mate, keep = partial_sums(place, older, newer, conv_weight, (ns, nc, CUTS, index))
        held = [keep]
        sent = [mate]
        for step, bit in enumerate([0, *range(bits - 1, 0, -1)]):
            arrived = [swapped(value, bit, ns) for value in sent]
            if step == bits - 1:
                held.extend(arrived)
                break
            total = sum(arrived, start=sum(held[1:], start=held[0]))
            middle = total.shape[0] // 2
            sent, held = [total[:middle]], [total[middle:]]
        groups.append(held)
    return finish(groups, fields.dtype)


def solution(mesh):
    return jax.shard_map(
        local,
        mesh=mesh,
        in_specs=(P("chan", ("groups", "space"), None), P(None, "chan", "space")),
        out_specs=P("chan", ("groups", "space"), None),
        check_vma=False,
    )
```

time: 169 us -> 62.3 us (0.37)
  waiting for transfers between devices: 108 us -> 17.6 us
  matrix products: 25.6 us -> 0 us
  starting transfers between devices: 4.4 us -> 25.8 us
  Pallas kernels: 0 us -> 14.2 us
  between operations: 13.9 us -> 0.07 us
  local copies, waits for them, and re-layouts: 14.7 us -> 4.16 us
    all_gather x2 -> x0, waiting for transfers between devices: 106 us -> none  [the longest x1 73.3 us: local(): weights = lax.all_gather(conv_weight, 'space', axis=2, tiled=True)]
    dot_general x27 -> x0, matrix products: 25.6 us -> none  [convolve_block(): jnp.dot(weights[9 * step_x + 3 * step_y + step_z], window, preferred_elem...]
    ppermute x2 -> x12, starting transfers between devices: 4.36 us -> 25.8 us  [the longest x8 21.2 us: local(): arrived.append(lax.ppermute(operand, ('space', 'chan'), pairs))]
    ppermute x2 -> x12, waiting for transfers between devices: 1.48 us -> 17.6 us  [the longest x4 12.5 us: swapped(): return lax.ppermute(value, 'space', [(i, i ^ 1 << bit) for i in range(ns)])]
    pallas_call x0 -> x4, Pallas kernels: none -> 14.2 us  [the longest x2 9.46 us: partial_sums(): pl.pallas_call(functools.partial(partial_kernel, plan), out_shape=[jax.Sh...]
    slice x3 -> x2, local copies, waits for them, and re-layouts: 12 us -> 1.46 us  [local(): sent, held = ([total[:middle]], [total[middle:]])]
  transfers between devices with their start and end apart: 4 -> 12, of which waited for: 3 -> 5; matrix products, arithmetic and copies ran while one was open for 8% -> 3% of each run, Pallas kernels for 0% -> 15%
where the time goes in v1:
time: 62.3 us; the launch traced here: 62 us
  starting transfers between devices  25.8 us (41%)
  waiting for transfers between devices  17.6 us (28%)
  Pallas kernels  14.2 us (23%)
  local copies, waits for them, and re-layouts  4.16 us (7%)
    ppermute x8, starting transfers between devices, local(): arrived.append(lax.ppermute(operand, ('space', 'chan'), pairs))  21.2 us
    ppermute x4, waiting for transfers between devices, swapped(): return lax.ppermute(value, 'space', [(i, i ^ 1 << bit) for i in range(ns)])  12.5 us
    pallas_call x2, Pallas kernels, partial_sums(): pl.pallas_call(functools.partial(partial_kernel, plan), out_shape=[jax.Sh...  9.46 us
    ppermute x8, waiting for transfers between devices, local(): arrived.append(lax.ppermute(operand, ('space', 'chan'), pairs))  5.03 us
    ppermute x4, starting transfers between devices, swapped(): return lax.ppermute(value, 'space', [(i, i ^ 1 << bit) for i in range(ns)])  4.54 us
    unnamed x6, local copies, waits for them, and re-layouts  2.7 us
    pallas_call x1, Pallas kernels, finish(): pl.pallas_call(functools.partial(finish_kernel, [len(pieces) for pieces i...  2.47 us
    pallas_call x1, Pallas kernels, by_cell(): pl.pallas_call(functools.partial(transpose_kernel, cuts), out_shape=[jax....  2.27 us
  transfers between devices with their start and end apart: 12, of which 5 were waited for; matrix products, arithmetic and copies ran while one was open for 3% of the time, Pallas kernels for 15%

profile of v1, /device:TPU:0, one launch (start us, length us, event | category | flops | bytes accessed | tf_op | source)
XLA Modules:
  0.0 62.0 jit_solution(2160446720838286087)
XLA Ops:
  0.0 2.3 %by_cell.1 = (bf16[2,144,256]{2,1,0:T(8,128)(2,1)}, bf16[2,112,256]{2,1,0:T(8,128)(2,1)}) custom-call(bf16[256,2,256]{2,1,0:T(2,128)(2,1)} %fields_ref.1), custom_call_target="tpu_custom_call" | custom-call | tf_op jit(solution)/shard_map/by_cell/pallas_call | solution.py:36
  2.3 4.0 %collective-permute-start.2 = (bf16[2,144,256]{2,1,0:T(8,128)(2,1)}, bf16[2,144,256]{2,1,0:T(8,128)(2,1)S(1)}, u32[]{:S(2)}, u32[]{:S(2)}) collective-permute-start(bf16[2,144,256]{2,1,0:T(8,128)(2,1)} %get-tuple-element.20), channel_id=1, source_target_pairs={{4,0},{12,1},{0,2},{8,3},{5,4},{13,5},{1,6},{9,7},{6,8},{14,9},{2,... | collective-permute-start | bytes 442376 | tf_op jit(solution)/shard_map/ppermute | solution.py:208
  6.3 3.7 %collective-permute-start.3 = (bf16[2,144,256]{2,1,0:T(8,128)(2,1)}, bf16[2,144,256]{2,1,0:T(8,128)(2,1)S(1)}, u32[]{:S(2)}, u32[]{:S(2)}) collective-permute-start(bf16[2,144,256]{2,1,0:T(8,128)(2,1)} %get-tuple-element.20), channel_id=1, source_target_pairs={{12,0},{4,1},{8,2},{0,3},{13,4},{5,5},{9,6},{1,7},{14,8},{6,9},{10... | collective-permute-start | bytes 442376 | tf_op jit(solution)/shard_map/ppermute | solution.py:208
  10.0 0.1 collective-permute-start.1
  10.2 1.6 %collective-permute-start = (bf16[2,144,256]{2,1,0:T(8,128)(2,1)}, bf16[2,144,256]{2,1,0:T(8,128)(2,1)S(1)}, u32[]{:S(2)}, u32[]{:S(2)}) collective-permute-start(bf16[2,144,256]{2,1,0:T(8,128)(2,1)} %get-tuple-element.20), channel_id=1, source_target_pairs={{0,0},{8,1},{4,2},{12,3},{1,4},{9,5},{5,6},{13,7},{2,8},{10,9},{6,... | collective-permute-start | bytes 442376 | tf_op jit(solution)/shard_map/ppermute | solution.py:208
  11.7 0.1 pad_add_fusion.place_ref
  11.8 0.0 collective-permute-done.2.refs_2_
  11.8 2.5 %collective-permute-done.3.refs_3_ = bf16[2,144,256]{2,1,0:T(8,128)(2,1)S(1)} collective-permute-done((bf16[2,144,256]{2,1,0:T(8,128)(2,1)}, bf16[2,144,256]{2,1,0:T(8,128)(2,1)S(1)}, u32[]{:S(2)}, u32[]{:S(2)}) %collective-permute-start.3) | collective-permute-done | bytes 147488 | tf_op jit(solution)/shard_map/ppermute | solution.py:208
  14.3 2.5 %collective-permute-done.1.refs_1_ = bf16[2,144,256]{2,1,0:T(8,128)(2,1)S(1)} collective-permute-done((bf16[2,144,256]{2,1,0:T(8,128)(2,1)}, bf16[2,144,256]{2,1,0:T(8,128)(2,1)S(1)}, u32[]{:S(2)}, u32[]{:S(2)}) %collective-permute-start.1) | collective-permute-done | bytes 147488 | tf_op jit(solution)/shard_map/ppermute | solution.py:208
  16.8 0.0 collective-permute-done.refs_0_
  16.8 4.5 %collective-permute-start.8 = (bf16[2,112,256]{2,1,0:T(8,128)(2,1)}, bf16[2,112,256]{2,1,0:T(8,128)(2,1)S(1)}, u32[]{:S(2)}, u32[]{:S(2)}) collective-permute-start(bf16[2,112,256]{2,1,0:T(8,128)(2,1)} %get-tuple-element.30), channel_id=1, source_target_pairs={{4,0},{12,1},{0,2},{8,3},{5,4},{13,5},{1,6},{9,7},{6,8},{14,9},{2,... | collective-permute-start | bytes 344072 | tf_op jit(solution)/shard_map/ppermute | solution.py:208
  21.3 3.1 %collective-permute-start.9 = (bf16[2,112,256]{2,1,0:T(8,128)(2,1)}, bf16[2,112,256]{2,1,0:T(8,128)(2,1)S(1)}, u32[]{:S(2)}, u32[]{:S(2)}) collective-permute-start(bf16[2,112,256]{2,1,0:T(8,128)(2,1)} %get-tuple-element.30), channel_id=1, source_target_pairs={{12,0},{4,1},{8,2},{0,3},{13,4},{5,5},{9,6},{1,7},{14,8},{6,9},{10... | collective-permute-start | bytes 344072 | tf_op jit(solution)/shard_map/ppermute | solution.py:208
  24.4 2.6 %collective-permute-start.7 = (bf16[2,112,256]{2,1,0:T(8,128)(2,1)}, bf16[2,112,256]{2,1,0:T(8,128)(2,1)S(1)}, u32[]{:S(2)}, u32[]{:S(2)}) collective-permute-start(bf16[2,112,256]{2,1,0:T(8,128)(2,1)} %get-tuple-element.30), channel_id=1, source_target_pairs={{8,0},{0,1},{12,2},{4,3},{9,4},{1,5},{13,6},{5,7},{10,8},{2,9},{14... | collective-permute-start | bytes 344072 | tf_op jit(solution)/shard_map/ppermute | solution.py:208
  27.1 1.5 %collective-permute-start.6 = (bf16[2,112,256]{2,1,0:T(8,128)(2,1)}, bf16[2,112,256]{2,1,0:T(8,128)(2,1)S(1)}, u32[]{:S(2)}, u32[]{:S(2)}) collective-permute-start(bf16[2,112,256]{2,1,0:T(8,128)(2,1)} %get-tuple-element.30), channel_id=1, source_target_pairs={{0,0},{8,1},{4,2},{12,3},{1,4},{9,5},{5,6},{13,7},{2,8},{10,9},{6,... | collective-permute-start | bytes 344072 | tf_op jit(solution)/shard_map/ppermute | solution.py:208
  28.6 0.0 copy-start
  28.6 2.0 %copy-done = bf16[27,256,256]{2,1,0:T(8,128)(2,1)S(1)} copy-done((bf16[27,256,256]{2,1,0:T(8,128)(2,1)S(1)}, bf16[27,256,256]{2,1,0:T(8,128)(2,1)}, u32[]{:S(2)}) %copy-start) | copy-done | bytes 3538968
  30.6 4.8 %partial_sums.2 = (f32[4,128,256]{2,1,0:T(8,128)S(1)}, f32[4,128,256]{2,1,0:T(8,128)S(1)}) custom-call(s32[2]{0:T(128)S(1)} %pad_add_fusion.place_ref, bf16[2,144,256]{2,1,0:T(8,128)(2,1)S(1)} %collective-permute-done.refs_0_, bf16[2,144,256]{2,1,0:T(8,128)(2,1)S(1)} %collective-permute-done.1.refs_1_, ...), custom_call_target="tpu_custom_call" | custom-call | flops 3623878656 | bytes 3538944 | tf_op jit(solution)/shard_map/partial_sums/pallas_call | solution.py:139
  35.4 3.5 %collective-permute-start.4 = (f32[4,128,256]{2,1,0:T(8,128)S(1)}, f32[4,128,256]{2,1,0:T(8,128)S(1)}, u32[]{:S(2)}, u32[]{:S(2)}) collective-permute-start(f32[4,128,256]{2,1,0:T(8,128)S(1)} %get-tuple-element.26), channel_id=1, source_target_pairs={{0,4},{4,0},{8,12},{12,8},{1,5},{5,1},{9,13},{13,9},{2,6},{6,2},{1... | collective-permute-start | bytes 1572872 | tf_op jit(solution)/shard_map/ppermute | solution.py:182
  38.9 0.0 collective-permute-done.8.refs_6_
  38.9 0.0 collective-permute-done.9.refs_7_
  38.9 0.0 collective-permute-done.7.refs_5_
  38.9 0.0 collective-permute-done.6.refs_4_
  38.9 4.7 %partial_sums.3 = (f32[4,128,256]{2,1,0:T(8,128)S(1)}, f32[4,128,256]{2,1,0:T(8,128)S(1)}) custom-call(s32[2]{0:T(128)S(1)} %pad_add_fusion.place_ref, bf16[2,144,256]{2,1,0:T(8,128)(2,1)S(1)} %collective-permute-done.refs_0_, bf16[2,144,256]{2,1,0:T(8,128)(2,1)S(1)} %collective-permute-done.1.refs_1_, ...), custom_call_target="tpu_custom_call" | custom-call | flops 3623878656 | bytes 3538944 | tf_op jit(solution)/shard_map/partial_sums/pallas_call | solution.py:139
  43.6 0.1 collective-permute-start.10
  43.7 0.0 collective-permute-done.4
  43.7 0.1 add.6
  43.8 0.7 %fusion.1 = (f32[2,128,256]{2,1,0:T(8,128)S(1)}, f32[2,128,256]{2,1,0:T(8,128)}) fusion(f32[4,128,256]{2,1,0:T(8,128)S(1)} %add.6), kind=kLoop, calls=%fused_computation.2 | loop fusion | bytes 1048576 | tf_op jit(solution)/shard_map/slice | solution.py:223
  44.5 0.0 collective-permute-start.5
  44.5 1.1 %collective-permute-done.10 = f32[4,128,256]{2,1,0:T(8,128)S(1)} collective-permute-done((f32[4,128,256]{2,1,0:T(8,128)S(1)}, f32[4,128,256]{2,1,0:T(8,128)S(1)}, u32[]{:S(2)}, u32[]{:S(2)}) %collective-permute-start.10) | collective-permute-done | bytes 524320 | tf_op jit(solution)/shard_map/ppermute | solution.py:182
  45.6 0.1 add.7
  45.6 0.7 %fusion = (f32[2,128,256]{2,1,0:T(8,128)S(1)}, f32[2,128,256]{2,1,0:T(8,128)}) fusion(f32[4,128,256]{2,1,0:T(8,128)S(1)} %add.7), kind=kLoop, calls=%fused_computation.1 | loop fusion | bytes 1048576 | tf_op jit(solution)/shard_map/slice | solution.py:223
  46.4 1.0 %collective-permute-start.11 = (f32[2,128,256]{2,1,0:T(8,128)S(1)}, f32[2,128,256]{2,1,0:T(8,128)S(1)}, u32[]{:S(2)}, u32[]{:S(2)}) collective-permute-start(f32[2,128,256]{2,1,0:T(8,128)S(1)} %get-tuple-element.33), channel_id=1, source_target_pairs={{0,8},{4,12},{8,0},{12,4},{1,9},{5,13},{9,1},{13,5},{2,10},{6,14},... | collective-permute-start | bytes 786440 | tf_op jit(solution)/shard_map/ppermute | solution.py:182
  47.3 6.3 %collective-permute-done.5.refs_1_ = f32[2,128,256]{2,1,0:T(8,128)S(1)} collective-permute-done((f32[2,128,256]{2,1,0:T(8,128)S(1)}, f32[2,128,256]{2,1,0:T(8,128)S(1)}, u32[]{:S(2)}, u32[]{:S(2)}) %collective-permute-start.5) | collective-permute-done | bytes 262176 | tf_op jit(solution)/shard_map/ppermute | solution.py:182
  53.6 0.0 copy-start.1
  53.6 5.2 %collective-permute-done.11.refs_3_ = f32[2,128,256]{2,1,0:T(8,128)S(1)} collective-permute-done((f32[2,128,256]{2,1,0:T(8,128)S(1)}, f32[2,128,256]{2,1,0:T(8,128)S(1)}, u32[]{:S(2)}, u32[]{:S(2)}) %collective-permute-start.11) | collective-permute-done | bytes 262176 | tf_op jit(solution)/shard_map/ppermute | solution.py:182
  58.8 0.0 copy-start.2
  58.8 0.0 copy-done.1
  58.8 0.7 %copy-done.2 = f32[2,128,256]{2,1,0:T(8,128)} copy-done((f32[2,128,256]{2,1,0:T(8,128)}, f32[2,128,256]{2,1,0:T(8,128)S(1)}, u32[]{:S(2)}) %copy-start.2) | copy-done | bytes 262168
  59.5 2.5 %finish.1 = bf16[256,2,256]{2,1,0:T(2,128)(2,1)} custom-call(f32[2,128,256]{2,1,0:T(8,128)} %get-tuple-element.36.refs_0_, f32[2,128,256]{2,1,0:T(8,128)} %copy-done.1, f32[2,128,256]{2,1,0:T(8,128)} %get-tuple-element.34.refs_2_, f32[2,128,256]{2,1,0:T(8,128)} %copy-done.2), custom_call_target="tpu_custom_call" | custom-call | tf_op jit(solution)/shard_map/finish/pallas_call | solution.py:174
Async XLA Ops:
  2.3 9.5 %collective-permute-start.2 = (bf16[2,144,256]{2,1,0:T(8,128)(2,1)}, bf16[2,144,256]{2,1,0:T(8,128)(2,1)S(1)}, u32[]{:S(2)}, u32[]{:S(2)}) collective-permute-start(bf16[2,144,256]{2,1,0:T(8,128)(2,1)} %get-tuple-element.20), channel_id=1, source_target_pairs={{4,0},{12,1},{0,2},{8,3},{5,4},{13,5},{1,6},{9,7},{6,8},{14,9},{2,... | collective-permute-start | bytes 442376 | tf_op jit(solution)/shard_map/ppermute | solution.py:208
  6.3 8.0 %collective-permute-start.3 = (bf16[2,144,256]{2,1,0:T(8,128)(2,1)}, bf16[2,144,256]{2,1,0:T(8,128)(2,1)S(1)}, u32[]{:S(2)}, u32[]{:S(2)}) collective-permute-start(bf16[2,144,256]{2,1,0:T(8,128)(2,1)} %get-tuple-element.20), channel_id=1, source_target_pairs={{12,0},{4,1},{8,2},{0,3},{13,4},{5,5},{9,6},{1,7},{14,8},{6,9},{10... | collective-permute-start | bytes 442376 | tf_op jit(solution)/shard_map/ppermute | solution.py:208
  10.0 6.8 %collective-permute-start.1 = (bf16[2,144,256]{2,1,0:T(8,128)(2,1)}, bf16[2,144,256]{2,1,0:T(8,128)(2,1)S(1)}, u32[]{:S(2)}, u32[]{:S(2)}) collective-permute-start(bf16[2,144,256]{2,1,0:T(8,128)(2,1)} %get-tuple-element.20), channel_id=1, source_target_pairs={{8,0},{0,1},{12,2},{4,3},{9,4},{1,5},{13,6},{5,7},{10,8},{2,9},{14... | collective-permute-start | bytes 442376 | tf_op jit(solution)/shard_map/ppermute | solution.py:208
  10.2 6.7 %collective-permute-start = (bf16[2,144,256]{2,1,0:T(8,128)(2,1)}, bf16[2,144,256]{2,1,0:T(8,128)(2,1)S(1)}, u32[]{:S(2)}, u32[]{:S(2)}) collective-permute-start(bf16[2,144,256]{2,1,0:T(8,128)(2,1)} %get-tuple-element.20), channel_id=1, source_target_pairs={{0,0},{8,1},{4,2},{12,3},{1,4},{9,5},{5,6},{13,7},{2,8},{10,9},{6,... | collective-permute-start | bytes 442376 | tf_op jit(solution)/shard_map/ppermute | solution.py:208
  16.8 22.1 %collective-permute-start.8 = (bf16[2,112,256]{2,1,0:T(8,128)(2,1)}, bf16[2,112,256]{2,1,0:T(8,128)(2,1)S(1)}, u32[]{:S(2)}, u32[]{:S(2)}) collective-permute-start(bf16[2,112,256]{2,1,0:T(8,128)(2,1)} %get-tuple-element.30), channel_id=1, source_target_pairs={{4,0},{12,1},{0,2},{8,3},{5,4},{13,5},{1,6},{9,7},{6,8},{14,9},{2,... | collective-permute-start | bytes 344072 | tf_op jit(solution)/shard_map/ppermute | solution.py:208
  21.3 17.6 %collective-permute-start.9 = (bf16[2,112,256]{2,1,0:T(8,128)(2,1)}, bf16[2,112,256]{2,1,0:T(8,128)(2,1)S(1)}, u32[]{:S(2)}, u32[]{:S(2)}) collective-permute-start(bf16[2,112,256]{2,1,0:T(8,128)(2,1)} %get-tuple-element.30), channel_id=1, source_target_pairs={{12,0},{4,1},{8,2},{0,3},{13,4},{5,5},{9,6},{1,7},{14,8},{6,9},{10... | collective-permute-start | bytes 344072 | tf_op jit(solution)/shard_map/ppermute | solution.py:208
  24.4 14.5 %collective-permute-start.7 = (bf16[2,112,256]{2,1,0:T(8,128)(2,1)}, bf16[2,112,256]{2,1,0:T(8,128)(2,1)S(1)}, u32[]{:S(2)}, u32[]{:S(2)}) collective-permute-start(bf16[2,112,256]{2,1,0:T(8,128)(2,1)} %get-tuple-element.30), channel_id=1, source_target_pairs={{8,0},{0,1},{12,2},{4,3},{9,4},{1,5},{13,6},{5,7},{10,8},{2,9},{14... | collective-permute-start | bytes 344072 | tf_op jit(solution)/shard_map/ppermute | solution.py:208
  27.1 11.8 %collective-permute-start.6 = (bf16[2,112,256]{2,1,0:T(8,128)(2,1)}, bf16[2,112,256]{2,1,0:T(8,128)(2,1)S(1)}, u32[]{:S(2)}, u32[]{:S(2)}) collective-permute-start(bf16[2,112,256]{2,1,0:T(8,128)(2,1)} %get-tuple-element.30), channel_id=1, source_target_pairs={{0,0},{8,1},{4,2},{12,3},{1,4},{9,5},{5,6},{13,7},{2,8},{10,9},{6,... | collective-permute-start | bytes 344072 | tf_op jit(solution)/shard_map/ppermute | solution.py:208
  28.6 2.0 %copy-start = (bf16[27,256,256]{2,1,0:T(8,128)(2,1)S(1)}, bf16[27,256,256]{2,1,0:T(8,128)(2,1)}, u32[]{:S(2)}) copy-start(bf16[27,256,256]{2,1,0:T(8,128)(2,1)} %refs_8_.1) | copy-start | bytes 10616836
  35.4 8.3 %collective-permute-start.4 = (f32[4,128,256]{2,1,0:T(8,128)S(1)}, f32[4,128,256]{2,1,0:T(8,128)S(1)}, u32[]{:S(2)}, u32[]{:S(2)}) collective-permute-start(f32[4,128,256]{2,1,0:T(8,128)S(1)} %get-tuple-element.26), channel_id=1, source_target_pairs={{0,4},{4,0},{8,12},{12,8},{1,5},{5,1},{9,13},{13,9},{2,6},{6,2},{1... | collective-permute-start | bytes 1572872 | tf_op jit(solution)/shard_map/ppermute | solution.py:182
  43.6 2.0 %collective-permute-start.10 = (f32[4,128,256]{2,1,0:T(8,128)S(1)}, f32[4,128,256]{2,1,0:T(8,128)S(1)}, u32[]{:S(2)}, u32[]{:S(2)}) collective-permute-start(f32[4,128,256]{2,1,0:T(8,128)S(1)} %get-tuple-element.32), channel_id=1, source_target_pairs={{0,4},{4,0},{8,12},{12,8},{1,5},{5,1},{9,13},{13,9},{2,6},{6,2},{1... | collective-permute-start | bytes 1572872 | tf_op jit(solution)/shard_map/ppermute | solution.py:182
  44.5 9.1 %collective-permute-start.5 = (f32[2,128,256]{2,1,0:T(8,128)S(1)}, f32[2,128,256]{2,1,0:T(8,128)S(1)}, u32[]{:S(2)}, u32[]{:S(2)}) collective-permute-start(f32[2,128,256]{2,1,0:T(8,128)S(1)} %get-tuple-element.35), channel_id=1, source_target_pairs={{0,8},{4,12},{8,0},{12,4},{1,9},{5,13},{9,1},{13,5},{2,10},{6,14},... | collective-permute-start | bytes 786440 | tf_op jit(solution)/shard_map/ppermute | solution.py:182
  46.4 12.4 %collective-permute-start.11 = (f32[2,128,256]{2,1,0:T(8,128)S(1)}, f32[2,128,256]{2,1,0:T(8,128)S(1)}, u32[]{:S(2)}, u32[]{:S(2)}) collective-permute-start(f32[2,128,256]{2,1,0:T(8,128)S(1)} %get-tuple-element.33), channel_id=1, source_target_pairs={{0,8},{4,12},{8,0},{12,4},{1,9},{5,13},{9,1},{13,5},{2,10},{6,14},... | collective-permute-start | bytes 786440 | tf_op jit(solution)/shard_map/ppermute | solution.py:182
  53.6 5.2 %copy-start.1 = (f32[2,128,256]{2,1,0:T(8,128)}, f32[2,128,256]{2,1,0:T(8,128)S(1)}, u32[]{:S(2)}) copy-start(f32[2,128,256]{2,1,0:T(8,128)S(1)} %collective-permute-done.5.refs_1_) | copy-start | bytes 786436
  58.8 0.7 %copy-start.2 = (f32[2,128,256]{2,1,0:T(8,128)}, f32[2,128,256]{2,1,0:T(8,128)S(1)}, u32[]{:S(2)}) copy-start(f32[2,128,256]{2,1,0:T(8,128)S(1)} %collective-permute-done.11.refs_3_) | copy-start | bytes 786436

commit v2 on v1

--- a/solution.py
+++ b/solution.py
@@ -10,7 +10,8 @@
 NY = 16
 NZ = 16
 CUTS = (0, 9, 16)
-VMEM_LIMIT = 48 * 2**20
+VMEM_LIMIT = 16 * 2**20
+IN_VMEM = pl.BlockSpec(memory_space=pltpu.VMEM)
 
 
 def bit_count(n):
@@ -25,8 +26,9 @@
 
 
 def transpose_kernel(cuts, fields_ref, *out_refs):
+    fields = fields_ref[...].astype(jnp.float32)
     for plane in range(fields_ref.shape[1]):
-        turned = fields_ref[:, plane, :].T
+        turned = fields[:, plane, :].T.astype(fields_ref.dtype)
         for out_ref, low, high in zip(out_refs, cuts, cuts[1:]):
             out_ref[plane] = turned[low * NZ : high * NZ]
 
@@ -39,8 +41,26 @@
             jax.ShapeDtypeStruct((depth, (high - low) * NZ, count), fields.dtype)
             for low, high in zip(cuts, cuts[1:])
         ],
+        in_specs=[IN_VMEM],
+        out_specs=[IN_VMEM] * (len(cuts) - 1),
+        compiler_params=pltpu.CompilerParams(vmem_limit_bytes=VMEM_LIMIT // 2),
         name="by_cell",
     )(fields)
+
+
+def hold_kernel(block_ref, weight_ref, token_ref):
+    token_ref[...] = jnp.zeros(token_ref.shape, token_ref.dtype)
+
+
+def hold(block, weights):
+    return pl.pallas_call(
+        hold_kernel,
+        out_shape=jax.ShapeDtypeStruct((8, 128), jnp.float32),
+        in_specs=[pl.BlockSpec(memory_space=pl.ANY), IN_VMEM],
+        out_specs=IN_VMEM,
+        compiler_params=pltpu.CompilerParams(vmem_limit_bytes=VMEM_LIMIT // 2),
+        name="hold",
+    )(block, weights)
 
 
 def shifted(value, step):
@@ -51,7 +71,7 @@
     return jnp.where(inside, rolled, 0.0).astype(value.dtype)
 
 
-def partial_kernel(plan, place_ref, *refs):
+def partial_kernel(plan, token_ref, *refs):
     ns, nc, cuts, index = plan
     repeats = nc // ns
     bits = bit_count(ns)
@@ -66,7 +86,7 @@
     count = newer_refs[0].shape[2]
     taken = repeats * count
     planes = ns * depth
-    space, chan = place_ref[0], place_ref[1]
+    space, chan = lax.axis_index("space"), lax.axis_index("chan")
     zeros = jnp.zeros(window_ref.shape[1:], window_ref.dtype)
     window_ref[0] = zeros
     window_ref[planes + 1] = zeros
@@ -107,25 +127,31 @@
 
     half = ns // 2
     cells = (last - first) * NZ
-    for position in range(ns):
-        order = position % half
-        owner = space ^ (2 * (half - 1 - order) + (1 if position < half else 0))
+    for order in range(half):
+        owners = [space ^ (2 * (half - 1 - order) + core) for core in (1, 0)]
         total = None
         for pair in range(9):
             a, b = divmod(pair, 3)
-            left = window_ref[
-                pl.ds(depth * owner + a, depth), b * NZ : b * NZ + cells, :
-            ].reshape(depth * cells, 3 * taken)
+            left = jnp.concatenate(
+                [
+                    window_ref[
+                        pl.ds(depth * owner + a, depth), b * NZ : b * NZ + cells, :
+                    ].reshape(depth * cells, 3 * taken)
+                    for owner in owners
+                ],
+                axis=0,
+            )
             right = jnp.concatenate([weight_ref[3 * pair + c] for c in range(3)], axis=1)
             product = lax.dot_general(
                 left, right, (((1,), (1,)), ((), ())), preferred_element_type=jnp.float32
             )
             total = product if total is None else total + product
-        target = mate_ref if position < half else keep_ref
-        target[order * depth : (order + 1) * depth] = total.reshape(depth, cells, -1)
-
-
-def partial_sums(place, older, newer, weights, plan):
+        total = total.reshape(2, depth, cells, -1)
+        mate_ref[order * depth : (order + 1) * depth] = total[0]
+        keep_ref[order * depth : (order + 1) * depth] = total[1]
+
+
+def partial_sums(token, older, newer, weights, plan):
     ns, nc, cuts, index = plan
     low, high = cuts[index], cuts[index + 1]
     first = max(low - 1, 0)
@@ -139,7 +165,7 @@
     return pl.pallas_call(
         functools.partial(partial_kernel, plan),
         out_shape=[jax.ShapeDtypeStruct((ns // 2 * depth, cells, owned), jnp.float32)] * 2,
-        in_specs=[pl.BlockSpec(memory_space=pltpu.SMEM)] + [in_vmem] * (len(parts) + 1),
+        in_specs=[pl.BlockSpec(memory_space=pl.ANY)] + [in_vmem] * (len(parts) + 1),
         out_specs=[in_vmem] * 2,
         scratch_shapes=[
             pltpu.VMEM((ns * depth + 2, cells + 2 * NZ, 3 * taken), newer[0].dtype)
@@ -149,11 +175,11 @@
             flops=flops, bytes_accessed=2 * weights.size, transcendentals=0
         ),
         name="partial_sums",
-    )(place, *parts, weights)
+    )(token, *parts, weights)
 
 
 def finish_kernel(counts, *refs):
-    out_ref = refs[-1]
+    *refs, out_ref, turned_ref = refs
     for plane in range(out_ref.shape[1]):
         at = 0
         begin = 0
@@ -163,19 +189,24 @@
             total = pieces[0][plane]
             for piece in pieces[1:]:
                 total = total + piece[plane]
-            turned = total.T.astype(out_ref.dtype)
-            out_ref[:, plane, begin : begin + turned.shape[1]] = turned
-            begin += turned.shape[1]
+            turned_ref[:, plane, begin : begin + total.shape[0]] = total.T
+            begin += total.shape[0]
+    out_ref[...] = turned_ref[...].astype(out_ref.dtype)
 
 
 def finish(groups, dtype):
     depth, _, owned = groups[0][0].shape
     cells = sum(pieces[0].shape[1] for pieces in groups)
+    flat = [piece for pieces in groups for piece in pieces]
     return pl.pallas_call(
         functools.partial(finish_kernel, [len(pieces) for pieces in groups]),
         out_shape=jax.ShapeDtypeStruct((owned, depth, cells), dtype),
+        in_specs=[IN_VMEM] * len(flat),
+        out_specs=IN_VMEM,
+        scratch_shapes=[pltpu.VMEM((owned, depth, cells), jnp.float32)],
+        compiler_params=pltpu.CompilerParams(vmem_limit_bytes=VMEM_LIMIT // 2),
         name="finish",
-    )(*[piece for pieces in groups for piece in pieces])
+    )(*flat)
 
 
 def swapped(value, bit, ns):
@@ -187,8 +218,8 @@
     repeats = nc // ns
     bits = bit_count(ns)
     depth = fields.shape[1]
-    place = jnp.stack([lax.axis_index("space"), lax.axis_index("chan")]).astype(jnp.int32)
     blocks = by_cell(fields, CUTS)
+    token = hold(blocks[0], conv_weight)
     received = []
     for index, block in enumerate(blocks):
         arrived = []
@@ -200,17 +231,13 @@
                     source = reversed_bits((z % ns) ^ mask, bits)
                     turn = (jump + z // ns) % repeats
                     pairs.append((source * nc + s * repeats + turn, s * nc + z))
-            operand = block
-            if index:
-                operand, received[-1][round_index] = lax.optimization_barrier(
-                    (block, received[-1][round_index])
-                )
-            arrived.append(lax.ppermute(operand, ("space", "chan"), pairs))
+            arrived.append(lax.ppermute(block, ("space", "chan"), pairs))
         received.append(arrived)
     groups = []
     for index, newer in enumerate(received):
         older = received[index - 1] if index else []
-        mate, keep = partial_sums(place, older, newer, conv_weight, (ns, nc, CUTS, index))
+        mate, keep = partial_sums(token, older, newer, conv_weight, (ns, nc, CUTS, index))
+        token, mate = lax.optimization_barrier((token, mate))
         held = [keep]
         sent = [mate]
         for step, bit in enumerate([0, *range(bits - 1, 0, -1)]):

time: 62.3 us -> 51.8 us (0.83)
  waiting for transfers between devices: 17.6 us -> 10.7 us
  Pallas kernels: 14.2 us -> 10.1 us
  starting transfers between devices: 25.8 us -> 27.5 us
  local copies, waits for them, and re-layouts: 4.16 us -> 3.02 us
    ppermute x8, waiting for transfers between devices: 5.03 us -> 0.02 us  [local(): arrived.append(lax.ppermute(block, ('space', 'chan'), pairs))]
    pallas_call x1, Pallas kernels: 2.27 us -> 0.34 us  [by_cell(): pl.pallas_call(functools.partial(transpose_kernel, cuts), out_shape=[jax....]
    ppermute x4, waiting for transfers between devices: 12.5 us -> 10.7 us  [swapped(): return lax.ppermute(value, 'space', [(i, i ^ 1 << bit) for i in range(ns)])]
    ppermute x4, starting transfers between devices: 4.54 us -> 6.18 us  [swapped(): return lax.ppermute(value, 'space', [(i, i ^ 1 << bit) for i in range(ns)])]
    slice x2, local copies, waits for them, and re-layouts: 1.46 us -> 0.07 us  [local(): sent, held = ([total[:middle]], [total[middle:]])]
    pallas_call x1, Pallas kernels: 2.47 us -> 1.34 us  [finish(): pl.pallas_call(functools.partial(finish_kernel, [len(pieces) for pieces i...]
    pallas_call x2, Pallas kernels: 9.46 us -> 8.37 us  [partial_sums(): pl.pallas_call(functools.partial(partial_kernel, plan), out_shape=[jax.Sh...]
  transfers between devices with their start and end apart: 12 -> 12, of which waited for: 5 -> 2; matrix products, arithmetic and copies ran while one was open for 3% -> 0% of each run, Pallas kernels for 15% -> 16%
where the time goes in v2:
time: 51.8 us; the launch traced here: 51.5 us
  starting transfers between devices  27.5 us (53%)
  waiting for transfers between devices  10.7 us (21%)
  Pallas kernels  10.1 us (19%)
  local copies, waits for them, and re-layouts  3.02 us (6%)
    ppermute x8, starting transfers between devices, local(): arrived.append(lax.ppermute(block, ('space', 'chan'), pairs))  21.3 us
    ppermute x4, waiting for transfers between devices, swapped(): return lax.ppermute(value, 'space', [(i, i ^ 1 << bit) for i in range(ns)])  10.7 us
    pallas_call x2, Pallas kernels, partial_sums(): pl.pallas_call(functools.partial(partial_kernel, plan), out_shape=[jax.Sh...  8.37 us
    ppermute x4, starting transfers between devices, swapped(): return lax.ppermute(value, 'space', [(i, i ^ 1 << bit) for i in range(ns)])  6.18 us
    unnamed x6, local copies, waits for them, and re-layouts  2.95 us
    pallas_call x1, Pallas kernels, finish(): pl.pallas_call(functools.partial(finish_kernel, [len(pieces) for pieces i...  1.34 us
  transfers between devices with their start and end apart: 12, of which 2 were waited for; matrix products, arithmetic and copies ran while one was open for 0% of the time, Pallas kernels for 16%

profile of v2, /device:TPU:0, one launch (start us, length us, event | category | flops | bytes accessed | tf_op | source)
XLA Modules:
  0.0 51.5 jit_solution(8512130752587596492)
XLA Ops:
  0.0 0.0 copy-start.2
  0.0 0.9 %copy-done.2 = bf16[256,2,256]{2,1,0:T(2,128)(2,1)S(1)} copy-done((bf16[256,2,256]{2,1,0:T(2,128)(2,1)S(1)}, bf16[256,2,256]{2,1,0:T(2,128)(2,1)}, u32[]{:S(2)}) %copy-start.2) | copy-done | bytes 262168
  1.0 0.3 by_cell.1
  1.3 0.7 %collective-permute-start = (bf16[2,144,256]{2,1,0:T(8,128)(2,1)S(1)}, bf16[2,144,256]{2,1,0:T(8,128)(2,1)S(1)}, u32[]{:S(2)}, u32[]{:S(2)}) collective-permute-start(bf16[2,144,256]{2,1,0:T(8,128)(2,1)S(1)} %get-tuple-element.14.block_ref), channel_id=1, source_target_pairs={{0,0},{8,1},{4,2},{12,3},{1,4},{9,5},{5,6},{13,7},{2,8},{10,9},{6,... | collective-permute-start | bytes 442376 | tf_op jit(solution)/shard_map/ppermute | solution.py:234
  2.0 4.3 %collective-permute-start.1 = (bf16[2,144,256]{2,1,0:T(8,128)(2,1)S(1)}, bf16[2,144,256]{2,1,0:T(8,128)(2,1)S(1)}, u32[]{:S(2)}, u32[]{:S(2)}) collective-permute-start(bf16[2,144,256]{2,1,0:T(8,128)(2,1)S(1)} %get-tuple-element.14.block_ref), channel_id=1, source_target_pairs={{8,0},{0,1},{12,2},{4,3},{9,4},{1,5},{13,6},{5,7},{10,8},{2,9},{14... | collective-permute-start | bytes 442376 | tf_op jit(solution)/shard_map/ppermute | solution.py:234
  6.3 2.4 %collective-permute-start.2 = (bf16[2,144,256]{2,1,0:T(8,128)(2,1)S(1)}, bf16[2,144,256]{2,1,0:T(8,128)(2,1)S(1)}, u32[]{:S(2)}, u32[]{:S(2)}) collective-permute-start(bf16[2,144,256]{2,1,0:T(8,128)(2,1)S(1)} %get-tuple-element.14.block_ref), channel_id=1, source_target_pairs={{4,0},{12,1},{0,2},{8,3},{5,4},{13,5},{1,6},{9,7},{6,8},{14,9},{2,... | collective-permute-start | bytes 442376 | tf_op jit(solution)/shard_map/ppermute | solution.py:234
  8.7 4.5 %collective-permute-start.3 = (bf16[2,144,256]{2,1,0:T(8,128)(2,1)S(1)}, bf16[2,144,256]{2,1,0:T(8,128)(2,1)S(1)}, u32[]{:S(2)}, u32[]{:S(2)}) collective-permute-start(bf16[2,144,256]{2,1,0:T(8,128)(2,1)S(1)} %get-tuple-element.14.block_ref), channel_id=1, source_target_pairs={{12,0},{4,1},{8,2},{0,3},{13,4},{5,5},{9,6},{1,7},{14,8},{6,9},{10... | collective-permute-start | bytes 442376 | tf_op jit(solution)/shard_map/ppermute | solution.py:234
  13.2 0.7 %collective-permute-start.6 = (bf16[2,112,256]{2,1,0:T(8,128)(2,1)S(1)}, bf16[2,112,256]{2,1,0:T(8,128)(2,1)S(1)}, u32[]{:S(2)}, u32[]{:S(2)}) collective-permute-start(bf16[2,112,256]{2,1,0:T(8,128)(2,1)S(1)} %get-tuple-element.19), channel_id=1, source_target_pairs={{0,0},{8,1},{4,2},{12,3},{1,4},{9,5},{5,6},{13,7},{2,8},{10,9},{6,... | collective-permute-start | bytes 344072 | tf_op jit(solution)/shard_map/ppermute | solution.py:234
  13.9 0.0 copy-start
  13.9 2.0 %copy-done = bf16[27,256,256]{2,1,0:T(8,128)(2,1)S(1)} copy-done((bf16[27,256,256]{2,1,0:T(8,128)(2,1)S(1)}, bf16[27,256,256]{2,1,0:T(8,128)(2,1)}, u32[]{:S(2)}) %copy-start) | copy-done | bytes 3538968
  15.9 0.0 copy-start.1
  15.9 0.0 collective-permute-done.refs_0_
  15.9 3.2 %collective-permute-start.7 = (bf16[2,112,256]{2,1,0:T(8,128)(2,1)S(1)}, bf16[2,112,256]{2,1,0:T(8,128)(2,1)S(1)}, u32[]{:S(2)}, u32[]{:S(2)}) collective-permute-start(bf16[2,112,256]{2,1,0:T(8,128)(2,1)S(1)} %get-tuple-element.19), channel_id=1, source_target_pairs={{8,0},{0,1},{12,2},{4,3},{9,4},{1,5},{13,6},{5,7},{10,8},{2,9},{14... | collective-permute-start | bytes 344072 | tf_op jit(solution)/shard_map/ppermute | solution.py:234
  19.1 0.0 collective-permute-done.1.refs_1_
  19.1 3.6 %collective-permute-start.8 = (bf16[2,112,256]{2,1,0:T(8,128)(2,1)S(1)}, bf16[2,112,256]{2,1,0:T(8,128)(2,1)S(1)}, u32[]{:S(2)}, u32[]{:S(2)}) collective-permute-start(bf16[2,112,256]{2,1,0:T(8,128)(2,1)S(1)} %get-tuple-element.19), channel_id=1, source_target_pairs={{4,0},{12,1},{0,2},{8,3},{5,4},{13,5},{1,6},{9,7},{6,8},{14,9},{2,... | collective-permute-start | bytes 344072 | tf_op jit(solution)/shard_map/ppermute | solution.py:234
  22.7 0.0 collective-permute-done.2.refs_2_
  22.7 1.9 %collective-permute-start.9 = (bf16[2,112,256]{2,1,0:T(8,128)(2,1)S(1)}, bf16[2,112,256]{2,1,0:T(8,128)(2,1)S(1)}, u32[]{:S(2)}, u32[]{:S(2)}) collective-permute-start(bf16[2,112,256]{2,1,0:T(8,128)(2,1)S(1)} %get-tuple-element.19), channel_id=1, source_target_pairs={{12,0},{4,1},{8,2},{0,3},{13,4},{5,5},{9,6},{1,7},{14,8},{6,9},{10... | collective-permute-start | bytes 344072 | tf_op jit(solution)/shard_map/ppermute | solution.py:234
  24.7 0.0 collective-permute-done.3.refs_3_
  24.7 0.0 copy-done.1
  24.7 4.2 %partial_sums.2 = (f32[4,128,256]{2,1,0:T(8,128)S(1)}, f32[4,128,256]{2,1,0:T(8,128)S(1)}) custom-call(f32[8,128]{1,0:T(8,128)S(1)} %hold.1.token_ref, bf16[2,144,256]{2,1,0:T(8,128)(2,1)S(1)} %collective-permute-done.refs_0_, bf16[2,144,256]{2,1,0:T(8,128)(2,1)S(1)} %collective-permute-done.1.refs_1_, ...), custom_call_target="tpu_custom_call" | custom-call | flops 3623878656 | bytes 3538944 | tf_op jit(solution)/shard_map/partial_sums/pallas_call | solution.py:165
  28.9 1.2 %collective-permute-start.4 = (f32[4,128,256]{2,1,0:T(8,128)S(1)}, f32[4,128,256]{2,1,0:T(8,128)S(1)}, u32[]{:S(2)}, u32[]{:S(2)}) collective-permute-start(f32[4,128,256]{2,1,0:T(8,128)S(1)} %get-tuple-element.17), channel_id=1, source_target_pairs={{0,4},{4,0},{8,12},{12,8},{1,5},{5,1},{9,13},{13,9},{2,6},{6,2},{1... | collective-permute-start | bytes 1572872 | tf_op jit(solution)/shard_map/ppermute | solution.py:213
  30.1 0.0 collective-permute-done.6.refs_4_
  30.1 0.0 collective-permute-done.7.refs_5_
  30.1 0.0 collective-permute-done.8.refs_6_
  30.2 0.0 collective-permute-done.9.refs_7_
  30.2 4.1 %partial_sums.3 = (f32[4,128,256]{2,1,0:T(8,128)S(1)}, f32[4,128,256]{2,1,0:T(8,128)S(1)}) custom-call(f32[8,128]{1,0:T(8,128)S(1)} %hold.1.token_ref, bf16[2,144,256]{2,1,0:T(8,128)(2,1)S(1)} %collective-permute-done.refs_0_, bf16[2,144,256]{2,1,0:T(8,128)(2,1)S(1)} %collective-permute-done.1.refs_1_, ...), custom_call_target="tpu_custom_call" | custom-call | flops 3623878656 | bytes 3538944 | tf_op jit(solution)/shard_map/partial_sums/pallas_call | solution.py:165
  34.3 0.1 collective-permute-start.10
  34.4 0.0 collective-permute-done.4
  34.4 0.1 add.6
  34.5 3.1 %collective-permute-start.5 = (f32[2,128,256]{2,1,0:T(8,128)S(1)}, f32[2,128,256]{2,1,0:T(8,128)S(1)}, u32[]{:S(2)}, u32[]{:S(2)}) collective-permute-start(f32[2,128,256]{2,1,0:T(8,128)S(1)} %get-tuple-element.25), channel_id=1, source_target_pairs={{0,8},{4,12},{8,0},{12,4},{1,9},{5,13},{9,1},{13,5},{2,10},{6,14},... | collective-permute-start | bytes 786440 | tf_op jit(solution)/shard_map/ppermute | solution.py:213
  37.6 0.0 collective-permute-done.10
  37.6 0.1 add.7
  37.7 1.8 %collective-permute-start.11 = (f32[2,128,256]{2,1,0:T(8,128)S(1)}, f32[2,128,256]{2,1,0:T(8,128)S(1)}, u32[]{:S(2)}, u32[]{:S(2)}) collective-permute-start(f32[2,128,256]{2,1,0:T(8,128)S(1)} %get-tuple-element.23), channel_id=1, source_target_pairs={{0,8},{4,12},{8,0},{12,4},{1,9},{5,13},{9,1},{13,5},{2,10},{6,14},... | collective-permute-start | bytes 786440 | tf_op jit(solution)/shard_map/ppermute | solution.py:213
  39.5 5.3 %collective-permute-done.5.refs_1_ = f32[2,128,256]{2,1,0:T(8,128)S(1)} collective-permute-done((f32[2,128,256]{2,1,0:T(8,128)S(1)}, f32[2,128,256]{2,1,0:T(8,128)S(1)}, u32[]{:S(2)}, u32[]{:S(2)}) %collective-permute-start.5) | collective-permute-done | bytes 262176 | tf_op jit(solution)/shard_map/ppermute | solution.py:213
  44.8 5.4 %collective-permute-done.11.refs_3_ = f32[2,128,256]{2,1,0:T(8,128)S(1)} collective-permute-done((f32[2,128,256]{2,1,0:T(8,128)S(1)}, f32[2,128,256]{2,1,0:T(8,128)S(1)}, u32[]{:S(2)}, u32[]{:S(2)}) %collective-permute-start.11) | collective-permute-done | bytes 262176 | tf_op jit(solution)/shard_map/ppermute | solution.py:213
  50.2 1.3 %finish.1 = bf16[256,2,256]{2,1,0:T(2,128)(2,1)} custom-call(f32[2,128,256]{2,1,0:T(8,128)S(1)} %get-tuple-element.26.refs_0_, f32[2,128,256]{2,1,0:T(8,128)S(1)} %collective-permute-done.5.refs_1_, f32[2,128,256]{2,1,0:T(8,128)S(1)} %get-tuple-element.24.refs_2_, f32[2,128,256]{2,1,0:T(8,128)S(1)} %collective-permute-done.11.refs_3_), custom_call_target="tpu_custom_call" | custom-call | tf_op jit(solution)/shard_map/finish/pallas_call | solution.py:201
  (3 shorter events, 0.1 us)
Async XLA Ops:
  0.0 0.9 %copy-start.2 = (bf16[256,2,256]{2,1,0:T(2,128)(2,1)S(1)}, bf16[256,2,256]{2,1,0:T(2,128)(2,1)}, u32[]{:S(2)}) copy-start(bf16[256,2,256]{2,1,0:T(2,128)(2,1)} %fields_ref.1) | copy-start | bytes 786436
  1.3 14.6 %collective-permute-start = (bf16[2,144,256]{2,1,0:T(8,128)(2,1)S(1)}, bf16[2,144,256]{2,1,0:T(8,128)(2,1)S(1)}, u32[]{:S(2)}, u32[]{:S(2)}) collective-permute-start(bf16[2,144,256]{2,1,0:T(8,128)(2,1)S(1)} %get-tuple-element.14.block_ref), channel_id=1, source_target_pairs={{0,0},{8,1},{4,2},{12,3},{1,4},{9,5},{5,6},{13,7},{2,8},{10,9},{6,... | collective-permute-start | bytes 442376 | tf_op jit(solution)/shard_map/ppermute | solution.py:234
  2.0 17.2 %collective-permute-start.1 = (bf16[2,144,256]{2,1,0:T(8,128)(2,1)S(1)}, bf16[2,144,256]{2,1,0:T(8,128)(2,1)S(1)}, u32[]{:S(2)}, u32[]{:S(2)}) collective-permute-start(bf16[2,144,256]{2,1,0:T(8,128)(2,1)S(1)} %get-tuple-element.14.block_ref), channel_id=1, source_target_pairs={{8,0},{0,1},{12,2},{4,3},{9,4},{1,5},{13,6},{5,7},{10,8},{2,9},{14... | collective-permute-start | bytes 442376 | tf_op jit(solution)/shard_map/ppermute | solution.py:234
  6.3 16.4 %collective-permute-start.2 = (bf16[2,144,256]{2,1,0:T(8,128)(2,1)S(1)}, bf16[2,144,256]{2,1,0:T(8,128)(2,1)S(1)}, u32[]{:S(2)}, u32[]{:S(2)}) collective-permute-start(bf16[2,144,256]{2,1,0:T(8,128)(2,1)S(1)} %get-tuple-element.14.block_ref), channel_id=1, source_target_pairs={{4,0},{12,1},{0,2},{8,3},{5,4},{13,5},{1,6},{9,7},{6,8},{14,9},{2,... | collective-permute-start | bytes 442376 | tf_op jit(solution)/shard_map/ppermute | solution.py:234
  8.7 16.0 %collective-permute-start.3 = (bf16[2,144,256]{2,1,0:T(8,128)(2,1)S(1)}, bf16[2,144,256]{2,1,0:T(8,128)(2,1)S(1)}, u32[]{:S(2)}, u32[]{:S(2)}) collective-permute-start(bf16[2,144,256]{2,1,0:T(8,128)(2,1)S(1)} %get-tuple-element.14.block_ref), channel_id=1, source_target_pairs={{12,0},{4,1},{8,2},{0,3},{13,4},{5,5},{9,6},{1,7},{14,8},{6,9},{10... | collective-permute-start | bytes 442376 | tf_op jit(solution)/shard_map/ppermute | solution.py:234
  13.2 16.9 %collective-permute-start.6 = (bf16[2,112,256]{2,1,0:T(8,128)(2,1)S(1)}, bf16[2,112,256]{2,1,0:T(8,128)(2,1)S(1)}, u32[]{:S(2)}, u32[]{:S(2)}) collective-permute-start(bf16[2,112,256]{2,1,0:T(8,128)(2,1)S(1)} %get-tuple-element.19), channel_id=1, source_target_pairs={{0,0},{8,1},{4,2},{12,3},{1,4},{9,5},{5,6},{13,7},{2,8},{10,9},{6,... | collective-permute-start | bytes 344072 | tf_op jit(solution)/shard_map/ppermute | solution.py:234
  13.9 2.0 %copy-start = (bf16[27,256,256]{2,1,0:T(8,128)(2,1)S(1)}, bf16[27,256,256]{2,1,0:T(8,128)(2,1)}, u32[]{:S(2)}) copy-start(bf16[27,256,256]{2,1,0:T(8,128)(2,1)} %refs_8_.1) | copy-start | bytes 10616836
  15.9 8.8 %copy-start.1 = (bf16[27,256,256]{2,1,0:T(8,128)(2,1)S(1)}, bf16[27,256,256]{2,1,0:T(8,128)(2,1)}, u32[]{:S(2)}) copy-start(bf16[27,256,256]{2,1,0:T(8,128)(2,1)} %refs_8_.1) | copy-start | bytes 10616836
  15.9 14.3 %collective-permute-start.7 = (bf16[2,112,256]{2,1,0:T(8,128)(2,1)S(1)}, bf16[2,112,256]{2,1,0:T(8,128)(2,1)S(1)}, u32[]{:S(2)}, u32[]{:S(2)}) collective-permute-start(bf16[2,112,256]{2,1,0:T(8,128)(2,1)S(1)} %get-tuple-element.19), channel_id=1, source_target_pairs={{8,0},{0,1},{12,2},{4,3},{9,4},{1,5},{13,6},{5,7},{10,8},{2,9},{14... | collective-permute-start | bytes 344072 | tf_op jit(solution)/shard_map/ppermute | solution.py:234
  19.1 11.0 %collective-permute-start.8 = (bf16[2,112,256]{2,1,0:T(8,128)(2,1)S(1)}, bf16[2,112,256]{2,1,0:T(8,128)(2,1)S(1)}, u32[]{:S(2)}, u32[]{:S(2)}) collective-permute-start(bf16[2,112,256]{2,1,0:T(8,128)(2,1)S(1)} %get-tuple-element.19), channel_id=1, source_target_pairs={{4,0},{12,1},{0,2},{8,3},{5,4},{13,5},{1,6},{9,7},{6,8},{14,9},{2,... | collective-permute-start | bytes 344072 | tf_op jit(solution)/shard_map/ppermute | solution.py:234
  22.7 7.4 %collective-permute-start.9 = (bf16[2,112,256]{2,1,0:T(8,128)(2,1)S(1)}, bf16[2,112,256]{2,1,0:T(8,128)(2,1)S(1)}, u32[]{:S(2)}, u32[]{:S(2)}) collective-permute-start(bf16[2,112,256]{2,1,0:T(8,128)(2,1)S(1)} %get-tuple-element.19), channel_id=1, source_target_pairs={{12,0},{4,1},{8,2},{0,3},{13,4},{5,5},{9,6},{1,7},{14,8},{6,9},{10... | collective-permute-start | bytes 344072 | tf_op jit(solution)/shard_map/ppermute | solution.py:234
  28.9 5.5 %collective-permute-start.4 = (f32[4,128,256]{2,1,0:T(8,128)S(1)}, f32[4,128,256]{2,1,0:T(8,128)S(1)}, u32[]{:S(2)}, u32[]{:S(2)}) collective-permute-start(f32[4,128,256]{2,1,0:T(8,128)S(1)} %get-tuple-element.17), channel_id=1, source_target_pairs={{0,4},{4,0},{8,12},{12,8},{1,5},{5,1},{9,13},{13,9},{2,6},{6,2},{1... | collective-permute-start | bytes 1572872 | tf_op jit(solution)/shard_map/ppermute | solution.py:213
  34.3 3.3 %collective-permute-start.10 = (f32[4,128,256]{2,1,0:T(8,128)S(1)}, f32[4,128,256]{2,1,0:T(8,128)S(1)}, u32[]{:S(2)}, u32[]{:S(2)}) collective-permute-start(f32[4,128,256]{2,1,0:T(8,128)S(1)} %get-tuple-element.22), channel_id=1, source_target_pairs={{0,4},{4,0},{8,12},{12,8},{1,5},{5,1},{9,13},{13,9},{2,6},{6,2},{1... | collective-permute-start | bytes 1572872 | tf_op jit(solution)/shard_map/ppermute | solution.py:213
  34.5 10.3 %collective-permute-start.5 = (f32[2,128,256]{2,1,0:T(8,128)S(1)}, f32[2,128,256]{2,1,0:T(8,128)S(1)}, u32[]{:S(2)}, u32[]{:S(2)}) collective-permute-start(f32[2,128,256]{2,1,0:T(8,128)S(1)} %get-tuple-element.25), channel_id=1, source_target_pairs={{0,8},{4,12},{8,0},{12,4},{1,9},{5,13},{9,1},{13,5},{2,10},{6,14},... | collective-permute-start | bytes 786440 | tf_op jit(solution)/shard_map/ppermute | solution.py:213
  37.7 12.5 %collective-permute-start.11 = (f32[2,128,256]{2,1,0:T(8,128)S(1)}, f32[2,128,256]{2,1,0:T(8,128)S(1)}, u32[]{:S(2)}, u32[]{:S(2)}) collective-permute-start(f32[2,128,256]{2,1,0:T(8,128)S(1)} %get-tuple-element.23), channel_id=1, source_target_pairs={{0,8},{4,12},{8,0},{12,4},{1,9},{5,13},{9,1},{13,5},{2,10},{6,14},... | collective-permute-start | bytes 786440 | tf_op jit(solution)/shard_map/ppermute | solution.py:213

commit v3 on v2

--- a/solution.py
+++ b/solution.py
@@ -10,6 +10,8 @@
 NY = 16
 NZ = 16
 CUTS = (0, 9, 16)
+HEAD = 16
+LOWEST, SPAN = 14.0, 29.0
 VMEM_LIMIT = 16 * 2**20
 IN_VMEM = pl.BlockSpec(memory_space=pltpu.VMEM)
 
@@ -71,7 +73,7 @@
     return jnp.where(inside, rolled, 0.0).astype(value.dtype)
 
 
-def partial_kernel(plan, token_ref, *refs):
+def fill_window(plan, part_refs, window_ref):
     ns, nc, cuts, index = plan
     repeats = nc // ns
     bits = bit_count(ns)
@@ -79,14 +81,12 @@
     first = max(low - 1, 0)
     last = high if high == NY else high - 1
     top = first - 1
-    part_refs = refs[: nc * (2 if index else 1)]
-    weight_ref, mate_ref, keep_ref, window_ref = refs[len(part_refs) :]
     older_refs, newer_refs = part_refs[:-nc], part_refs[-nc:]
     depth = newer_refs[0].shape[0]
     count = newer_refs[0].shape[2]
     taken = repeats * count
     planes = ns * depth
-    space, chan = lax.axis_index("space"), lax.axis_index("chan")
+    chan = lax.axis_index("chan")
     zeros = jnp.zeros(window_ref.shape[1:], window_ref.dtype)
     window_ref[0] = zeros
     window_ref[planes + 1] = zeros
@@ -125,10 +125,15 @@
                 put(older[plane, (begin - cuts[index - 1]) * NZ :, :], begin, where, turn)
             put(newer_refs[round_index][plane], low, where, turn)
 
-    half = ns // 2
-    cells = (last - first) * NZ
-    for order in range(half):
-        owners = [space ^ (2 * (half - 1 - order) + core) for core in (1, 0)]
+def add_up(plan, far, weight_ref, window_ref, mate_ref, keep_ref):
+    ns, nc, cuts, index = plan
+    depth = (window_ref.shape[0] - 2) // ns
+    cells = window_ref.shape[1] - 2 * NZ
+    space = lax.axis_index("space")
+    groups = ns // 4
+    for order in range(groups):
+        mask = 2 * (groups - 1 - order + (groups if far else 0))
+        owners = [space ^ (mask + 1), space ^ mask]
         total = None
         for pair in range(9):
             a, b = divmod(pair, 3)
@@ -136,7 +141,7 @@
                 [
                     window_ref[
                         pl.ds(depth * owner + a, depth), b * NZ : b * NZ + cells, :
-                    ].reshape(depth * cells, 3 * taken)
+                    ].reshape(depth * cells, -1)
                     for owner in owners
                 ],
                 axis=0,
@@ -146,57 +151,90 @@
                 left, right, (((1,), (1,)), ((), ())), preferred_element_type=jnp.float32
             )
             total = product if total is None else total + product
-        total = total.reshape(2, depth, cells, -1)
-        mate_ref[order * depth : (order + 1) * depth] = total[0]
-        keep_ref[order * depth : (order + 1) * depth] = total[1]
-
-
-def partial_sums(token, older, newer, weights, plan):
+        begin, rows = HEAD + order * depth * cells, depth * cells
+        mate_ref[begin : begin + rows] = total[:rows]
+        keep_ref[begin : begin + rows] = total[rows:]
+    for ref in (mate_ref, keep_ref):
+        peak = jnp.max(jnp.abs(ref[HEAD:]), axis=0, keepdims=True)
+        ref[:HEAD] = jnp.broadcast_to(peak, (HEAD, ref.shape[1]))
+
+
+def first_kernel(plan, token_ref, weight_ref, *refs):
+    *part_refs, mate_ref, keep_ref, window_ref = refs
+    fill_window(plan, part_refs, window_ref)
+    add_up(plan, True, weight_ref, window_ref, mate_ref, keep_ref)
+
+
+def second_kernel(plan, token_ref, weight_ref, window_ref, mate_ref, keep_ref):
+    add_up(plan, False, weight_ref, window_ref, mate_ref, keep_ref)
+
+
+def both_kernel(plan, token_ref, weight_ref, *refs):
+    *part_refs, far_mate, far_keep, near_mate, near_keep, window_ref = refs
+    fill_window(plan, part_refs, window_ref)
+    add_up(plan, True, weight_ref, window_ref, far_mate, far_keep)
+    add_up(plan, False, weight_ref, window_ref, near_mate, near_keep)
+
+
+def partial_sums(token, older, newer, weights, plan, at_once):
     ns, nc, cuts, index = plan
     low, high = cuts[index], cuts[index + 1]
     first = max(low - 1, 0)
     last = high if high == NY else high - 1
-    depth, _, count = newer[0].shape
+    depth = newer[0].shape[0]
     owned, taken = weights.shape[1:]
     cells = (last - first) * NZ
-    in_vmem = pl.BlockSpec(memory_space=pltpu.VMEM)
+    sums = jax.ShapeDtypeStruct((HEAD + ns // 4 * depth * cells, owned), jnp.float32)
+    window = (ns * depth + 2, cells + 2 * NZ, 3 * taken)
+
+    def call(kernel, inputs, out_shape, scratch_shapes):
+        return pl.pallas_call(
+            functools.partial(kernel, plan),
+            out_shape=out_shape,
+            in_specs=[pl.BlockSpec(memory_space=pl.ANY)] + [IN_VMEM] * (1 + len(inputs)),
+            out_specs=[IN_VMEM] * len(out_shape),
+            scratch_shapes=scratch_shapes,
+            compiler_params=pltpu.CompilerParams(vmem_limit_bytes=VMEM_LIMIT),
+            cost_estimate=pl.CostEstimate(
+                flops=27 * len(out_shape) // 2 * ns * depth * cells * owned * taken,
+                bytes_accessed=2 * weights.size,
+                transcendentals=0,
+            ),
+            name="partial_sums",
+        )(token, weights, *inputs)
+
     parts = [*older, *newer]
-    flops = 2 * 27 * ns * depth * cells * owned * taken
-    return pl.pallas_call(
-        functools.partial(partial_kernel, plan),
-        out_shape=[jax.ShapeDtypeStruct((ns // 2 * depth, cells, owned), jnp.float32)] * 2,
-        in_specs=[pl.BlockSpec(memory_space=pl.ANY)] + [in_vmem] * (len(parts) + 1),
-        out_specs=[in_vmem] * 2,
-        scratch_shapes=[
-            pltpu.VMEM((ns * depth + 2, cells + 2 * NZ, 3 * taken), newer[0].dtype)
-        ],
-        compiler_params=pltpu.CompilerParams(vmem_limit_bytes=VMEM_LIMIT),
-        cost_estimate=pl.CostEstimate(
-            flops=flops, bytes_accessed=2 * weights.size, transcendentals=0
-        ),
-        name="partial_sums",
-    )(token, *parts, weights)
+    if at_once:
+        far_mate, far_keep, near_mate, near_keep = call(
+            both_kernel, parts, [sums] * 4, [pltpu.VMEM(window, weights.dtype)]
+        )
+    else:
+        far_mate, far_keep, filled = call(
+            first_kernel, parts, [sums] * 2 + [jax.ShapeDtypeStruct(window, weights.dtype)], []
+        )
+        near_mate, near_keep = call(second_kernel, [filled], [sums] * 2, [])
+    return (far_mate, far_keep), (near_mate, near_keep)
 
 
 def finish_kernel(counts, *refs):
     *refs, out_ref, turned_ref = refs
-    for plane in range(out_ref.shape[1]):
-        at = 0
-        begin = 0
-        for count in counts:
-            pieces = refs[at : at + count]
-            at += count
-            total = pieces[0][plane]
+    at = begin = 0
+    for count in counts:
+        pieces = refs[at : at + count]
+        at += count
+        cells = pieces[0].shape[0] // out_ref.shape[1]
+        for plane in range(out_ref.shape[1]):
+            total = pieces[0][plane * cells : (plane + 1) * cells]
             for piece in pieces[1:]:
-                total = total + piece[plane]
-            turned_ref[:, plane, begin : begin + total.shape[0]] = total.T
-            begin += total.shape[0]
+                total = total + piece[plane * cells : (plane + 1) * cells]
+            turned_ref[:, plane, begin : begin + cells] = total.T
+        begin += cells
     out_ref[...] = turned_ref[...].astype(out_ref.dtype)
 
 
-def finish(groups, dtype):
-    depth, _, owned = groups[0][0].shape
-    cells = sum(pieces[0].shape[1] for pieces in groups)
+def finish(groups, depth, dtype):
+    owned = groups[0][0].shape[1]
+    cells = sum(pieces[0].shape[0] for pieces in groups) // depth
     flat = [piece for pieces in groups for piece in pieces]
     return pl.pallas_call(
         functools.partial(finish_kernel, [len(pieces) for pieces in groups]),
@@ -207,6 +245,28 @@
         compiler_params=pltpu.CompilerParams(vmem_limit_bytes=VMEM_LIMIT // 2),
         name="finish",
     )(*flat)
+
+
+def level(head):
+    exponent, fraction = head[:1].astype(jnp.float32), head[HEAD // 2 : HEAD // 2 + 1]
+    return fraction.astype(jnp.float32) * jnp.exp2(exponent)
+
+
+def coded(sums):
+    bound = jnp.maximum(sums[:HEAD], 1e-30)
+    exponent = jnp.floor(jnp.log2(bound))
+    fraction = bound * jnp.exp2(-exponent) * (1 + 2.0**-10)
+    row = lax.broadcasted_iota(jnp.int32, bound.shape, 0)
+    head = jnp.where(row < HEAD // 2, exponent, fraction).astype(jnp.float16)
+    values = sums[HEAD:]
+    power = jnp.exp2(jnp.minimum(jnp.abs(values) / level(head), 1.0) * SPAN - LOWEST)
+    return jnp.concatenate([head, jnp.where(values < 0, -power, power).astype(jnp.float16)])
+
+
+def decoded(sent):
+    values = sent[HEAD:].astype(jnp.float32)
+    size = (jnp.log2(jnp.abs(values)) + LOWEST) * (level(sent[:HEAD]) / SPAN)
+    return jnp.where(values < 0, -size, size)
 
 
 def swapped(value, bit, ns):
@@ -236,20 +296,17 @@
     groups = []
     for index, newer in enumerate(received):
         older = received[index - 1] if index else []
-        mate, keep = partial_sums(token, older, newer, conv_weight, (ns, nc, CUTS, index))
-        token, mate = lax.optimization_barrier((token, mate))
-        held = [keep]
-        sent = [mate]
-        for step, bit in enumerate([0, *range(bits - 1, 0, -1)]):
-            arrived = [swapped(value, bit, ns) for value in sent]
-            if step == bits - 1:
-                held.extend(arrived)
-                break
-            total = sum(arrived, start=sum(held[1:], start=held[0]))
-            middle = total.shape[0] // 2
-            sent, held = [total[:middle]], [total[middle:]]
-        groups.append(held)
-    return finish(groups, fields.dtype)
+        plan = (ns, nc, CUTS, index)
+        far, near = partial_sums(token, older, newer, conv_weight, plan, index == 0)
+        token, mate = lax.optimization_barrier((token, far[0]))
+        far = (mate, far[1])
+        far, near = [keep + swapped(mate, 0, ns) for mate, keep in (far, near)]
+        for bit in range(bits - 1, 1, -1):
+            total = near + swapped(far, bit, ns)
+            middle = HEAD + (total.shape[0] - HEAD) // 2
+            far, near = total[:middle], jnp.concatenate([total[:HEAD], total[middle:]])
+        groups.append([near[HEAD:], decoded(swapped(coded(far), 1, ns))])
+    return finish(groups, fields.shape[1], fields.dtype)
 
 
 def solution(mesh):

time: 51.8 us -> 47.7 us (0.921)
  waiting for transfers between devices: 10.7 us -> 6.8 us
  starting transfers between devices: 27.5 us -> 26.4 us
  other arithmetic: 0.14 us -> 0.77 us
    ppermute x4 -> x6, waiting for transfers between devices: 10.7 us -> 6.78 us  [swapped(): return lax.ppermute(value, 'space', [(i, i ^ 1 << bit) for i in range(ns)])]
    ppermute x4 -> x6, starting transfers between devices: 6.18 us -> 5.12 us  [swapped(): return lax.ppermute(value, 'space', [(i, i ^ 1 << bit) for i in range(ns)])]
    pallas_call x2 -> x3, Pallas kernels: 8.37 us -> 8.62 us  [call(): pl.pallas_call(functools.partial(kernel, plan), out_shape=out_shape, in_s...]
  transfers between devices with their start and end apart: 12 -> 14, of which waited for: 2 -> 2; matrix products, arithmetic and copies ran while one was open for 0% -> 1% of each run, Pallas kernels for 16% -> 18%
where the time goes in v3:
time: 47.7 us; the launch traced here: 47.4 us
  starting transfers between devices  26.4 us (55%)
  Pallas kernels  10.3 us (22%)
  waiting for transfers between devices  6.8 us (14%)
  local copies, waits for them, and re-layouts  2.95 us (6%)
  other arithmetic  0.77 us (2%)
    ppermute x8, starting transfers between devices, local(): arrived.append(lax.ppermute(block, ('space', 'chan'), pairs))  21.3 us
    pallas_call x3, Pallas kernels, call(): pl.pallas_call(functools.partial(kernel, plan), out_shape=out_shape, in_s...  8.62 us
    ppermute x6, waiting for transfers between devices, swapped(): return lax.ppermute(value, 'space', [(i, i ^ 1 << bit) for i in range(ns)])  6.78 us
    ppermute x6, starting transfers between devices, swapped(): return lax.ppermute(value, 'space', [(i, i ^ 1 << bit) for i in range(ns)])  5.12 us
    unnamed x6, local copies, waits for them, and re-layouts  2.95 us
    pallas_call x1, Pallas kernels, finish(): pl.pallas_call(functools.partial(finish_kernel, [len(pieces) for pieces i...  1.33 us
  transfers between devices with their start and end apart: 14, of which 2 were waited for; matrix products, arithmetic and copies ran while one was open for 1% of the time, Pallas kernels for 18%

profile of v3, /device:TPU:0, one launch (start us, length us, event | category | flops | bytes accessed | tf_op | source)
XLA Modules:
  0.0 47.4 jit_solution(6953212571737959540)
XLA Ops:
  0.0 0.0 copy-start.2
  0.0 0.9 %copy-done.2 = bf16[256,2,256]{2,1,0:T(2,128)(2,1)S(1)} copy-done((bf16[256,2,256]{2,1,0:T(2,128)(2,1)S(1)}, bf16[256,2,256]{2,1,0:T(2,128)(2,1)}, u32[]{:S(2)}) %copy-start.2) | copy-done | bytes 262168
  1.0 0.3 by_cell.1
  1.3 0.7 %collective-permute-start = (bf16[2,144,256]{2,1,0:T(8,128)(2,1)S(1)}, bf16[2,144,256]{2,1,0:T(8,128)(2,1)S(1)}, u32[]{:S(2)}, u32[]{:S(2)}) collective-permute-start(bf16[2,144,256]{2,1,0:T(8,128)(2,1)S(1)} %get-tuple-element.19.block_ref), channel_id=1, source_target_pairs={{0,0},{8,1},{4,2},{12,3},{1,4},{9,5},{5,6},{13,7},{2,8},{10,9},{6,... | collective-permute-start | bytes 442376 | tf_op jit(solution)/shard_map/ppermute | solution.py:294
  2.0 4.3 %collective-permute-start.1 = (bf16[2,144,256]{2,1,0:T(8,128)(2,1)S(1)}, bf16[2,144,256]{2,1,0:T(8,128)(2,1)S(1)}, u32[]{:S(2)}, u32[]{:S(2)}) collective-permute-start(bf16[2,144,256]{2,1,0:T(8,128)(2,1)S(1)} %get-tuple-element.19.block_ref), channel_id=1, source_target_pairs={{8,0},{0,1},{12,2},{4,3},{9,4},{1,5},{13,6},{5,7},{10,8},{2,9},{14... | collective-permute-start | bytes 442376 | tf_op jit(solution)/shard_map/ppermute | solution.py:294
  6.3 2.4 %collective-permute-start.2 = (bf16[2,144,256]{2,1,0:T(8,128)(2,1)S(1)}, bf16[2,144,256]{2,1,0:T(8,128)(2,1)S(1)}, u32[]{:S(2)}, u32[]{:S(2)}) collective-permute-start(bf16[2,144,256]{2,1,0:T(8,128)(2,1)S(1)} %get-tuple-element.19.block_ref), channel_id=1, source_target_pairs={{4,0},{12,1},{0,2},{8,3},{5,4},{13,5},{1,6},{9,7},{6,8},{14,9},{2,... | collective-permute-start | bytes 442376 | tf_op jit(solution)/shard_map/ppermute | solution.py:294
  8.7 4.5 %collective-permute-start.3 = (bf16[2,144,256]{2,1,0:T(8,128)(2,1)S(1)}, bf16[2,144,256]{2,1,0:T(8,128)(2,1)S(1)}, u32[]{:S(2)}, u32[]{:S(2)}) collective-permute-start(bf16[2,144,256]{2,1,0:T(8,128)(2,1)S(1)} %get-tuple-element.19.block_ref), channel_id=1, source_target_pairs={{12,0},{4,1},{8,2},{0,3},{13,4},{5,5},{9,6},{1,7},{14,8},{6,9},{10... | collective-permute-start | bytes 442376 | tf_op jit(solution)/shard_map/ppermute | solution.py:294
  13.2 0.7 %collective-permute-start.7 = (bf16[2,112,256]{2,1,0:T(8,128)(2,1)S(1)}, bf16[2,112,256]{2,1,0:T(8,128)(2,1)S(1)}, u32[]{:S(2)}, u32[]{:S(2)}) collective-permute-start(bf16[2,112,256]{2,1,0:T(8,128)(2,1)S(1)} %get-tuple-element.26), channel_id=1, source_target_pairs={{0,0},{8,1},{4,2},{12,3},{1,4},{9,5},{5,6},{13,7},{2,8},{10,9},{6,... | collective-permute-start | bytes 344072 | tf_op jit(solution)/shard_map/ppermute | solution.py:294
  13.9 0.0 copy-start
  13.9 2.0 %copy-done = bf16[27,256,256]{2,1,0:T(8,128)(2,1)S(1)} copy-done((bf16[27,256,256]{2,1,0:T(8,128)(2,1)S(1)}, bf16[27,256,256]{2,1,0:T(8,128)(2,1)}, u32[]{:S(2)}) %copy-start) | copy-done | bytes 3538968
  15.9 0.0 copy-start.1
  15.9 0.0 collective-permute-done.refs_0_
  15.9 3.2 %collective-permute-start.8 = (bf16[2,112,256]{2,1,0:T(8,128)(2,1)S(1)}, bf16[2,112,256]{2,1,0:T(8,128)(2,1)S(1)}, u32[]{:S(2)}, u32[]{:S(2)}) collective-permute-start(bf16[2,112,256]{2,1,0:T(8,128)(2,1)S(1)} %get-tuple-element.26), channel_id=1, source_target_pairs={{8,0},{0,1},{12,2},{4,3},{9,4},{1,5},{13,6},{5,7},{10,8},{2,9},{14... | collective-permute-start | bytes 344072 | tf_op jit(solution)/shard_map/ppermute | solution.py:294
  19.1 0.0 collective-permute-done.1.refs_1_
  19.1 3.6 %collective-permute-start.9 = (bf16[2,112,256]{2,1,0:T(8,128)(2,1)S(1)}, bf16[2,112,256]{2,1,0:T(8,128)(2,1)S(1)}, u32[]{:S(2)}, u32[]{:S(2)}) collective-permute-start(bf16[2,112,256]{2,1,0:T(8,128)(2,1)S(1)} %get-tuple-element.26), channel_id=1, source_target_pairs={{4,0},{12,1},{0,2},{8,3},{5,4},{13,5},{1,6},{9,7},{6,8},{14,9},{2,... | collective-permute-start | bytes 344072 | tf_op jit(solution)/shard_map/ppermute | solution.py:294
  22.7 0.0 collective-permute-done.2.refs_2_
  22.7 1.9 %collective-permute-start.10 = (bf16[2,112,256]{2,1,0:T(8,128)(2,1)S(1)}, bf16[2,112,256]{2,1,0:T(8,128)(2,1)S(1)}, u32[]{:S(2)}, u32[]{:S(2)}) collective-permute-start(bf16[2,112,256]{2,1,0:T(8,128)(2,1)S(1)} %get-tuple-element.26), channel_id=1, source_target_pairs={{12,0},{4,1},{8,2},{0,3},{13,4},{5,5},{9,6},{1,7},{14,8},{6,9},{10... | collective-permute-start | bytes 344072 | tf_op jit(solution)/shard_map/ppermute | solution.py:294
  24.7 0.0 collective-permute-done.3.refs_3_
  24.7 0.0 copy-done.1
  24.7 4.3 %partial_sums.3 = (f32[272,256]{1,0:T(8,128)S(1)}, f32[272,256]{1,0:T(8,128)S(1)}, f32[272,256]{1,0:T(8,128)S(1)}, f32[272,256]{1,0:T(8,128)S(1)}) custom-call(f32[8,128]{1,0:T(8,128)S(1)} %hold.1.token_ref, bf16[27,256,256]{2,1,0:T(8,128)(2,1)S(1)} %copy-done.1, bf16[2,144,256]{2,1,0:T(8,128)(2,1)S(1)} %collective-permute-done.refs_0_, ...), custom_call_target="tpu_custom_call" | custom-call | flops 3623878656 | bytes 3538944 | tf_op jit(solution)/shard_map/partial_sums/pallas_call | solution.py:191
  28.9 1.2 %collective-permute-start.5 = (f32[272,256]{1,0:T(8,128)S(1)}, f32[272,256]{1,0:T(8,128)S(1)}, u32[]{:S(2)}, u32[]{:S(2)}) collective-permute-start(f32[272,256]{1,0:T(8,128)S(1)} %get-tuple-element.24), channel_id=1, source_target_pairs={{0,4},{4,0},{8,12},{12,8},{1,5},{5,1},{9,13},{13,9},{2,6},{6,2},{1... | collective-permute-start | bytes 835592 | tf_op jit(solution)/shard_map/ppermute | solution.py:273
  30.2 0.0 collective-permute-done.7.refs_4_
  30.2 0.0 collective-permute-done.8.refs_5_
  30.2 0.0 collective-permute-done.9.refs_6_
  30.2 0.0 collective-permute-done.10.refs_7_
  30.2 2.3 %partial_sums.4 = (f32[272,256]{1,0:T(8,128)S(1)}, f32[272,256]{1,0:T(8,128)S(1)}, bf16[10,160,768]{2,1,0:T(8,128)(2,1)S(1)}) custom-call(f32[8,128]{1,0:T(8,128)S(1)} %hold.1.token_ref, bf16[27,256,256]{2,1,0:T(8,128)(2,1)S(1)} %copy-done.1, bf16[2,144,256]{2,1,0:T(8,128)(2,1)S(1)} %collective-permute-done.refs_0_, ...), custom_call_target="tpu_custom_call" | custom-call | flops 2684354560 | bytes 3538944 | tf_op jit(solution)/shard_map/partial_sums/pallas_call | solution.py:191
  32.5 0.1 collective-permute-start.12
  32.6 0.5 %collective-permute-start.4 = (f32[272,256]{1,0:T(8,128)S(1)}, f32[272,256]{1,0:T(8,128)S(1)}, u32[]{:S(2)}, u32[]{:S(2)}) collective-permute-start(f32[272,256]{1,0:T(8,128)S(1)} %get-tuple-element.21), channel_id=1, source_target_pairs={{0,4},{4,0},{8,12},{12,8},{1,5},{5,1},{9,13},{13,9},{2,6},{6,2},{1... | collective-permute-start | bytes 835592 | tf_op jit(solution)/shard_map/ppermute | solution.py:273
  33.1 2.0 %partial_sums.5 = (f32[272,256]{1,0:T(8,128)S(1)}, f32[272,256]{1,0:T(8,128)S(1)}) custom-call(f32[8,128]{1,0:T(8,128)S(1)} %hold.1.token_ref, bf16[27,256,256]{2,1,0:T(8,128)(2,1)S(1)} %copy-done.1, bf16[10,160,768]{2,1,0:T(8,128)(2,1)S(1)} %get-tuple-element.27.window_ref), custom_call_target="tpu_custom_call" | custom-call | flops 1811939328 | bytes 3538944 | tf_op jit(solution)/shard_map/partial_sums/pallas_call | solution.py:191
  35.1 0.2 collective-permute-start.11
  35.3 0.0 collective-permute-done.5
  35.3 0.0 collective-permute-done.12
  35.4 0.1 select_convert_fusion
  35.5 0.1 fusion.8
  35.7 3.1 %collective-permute-start.6 = (f16[272,256]{1,0:T(8,128)(2,1)S(1)}, f16[272,256]{1,0:T(8,128)(2,1)S(1)}, u32[]{:S(2)}, u32[]{:S(2)}) collective-permute-start(f16[272,256]{1,0:T(8,128)(2,1)S(1)} %pad_maximum_fusion), channel_id=1, source_target_pairs={{0,8},{4,12},{8,0},{12,4},{1,9},{5,13},{9,1},{13,5},{2,10},{6,14},... | collective-permute-start | bytes 417800 | tf_op jit(solution)/shard_map/ppermute | solution.py:273
  38.8 0.1 fusion.9
  38.9 0.1 collective-permute-start.13
  39.0 0.0 collective-permute-done.4
  39.1 0.0 collective-permute-done.11
  39.1 4.2 %collective-permute-done.6 = f16[272,256]{1,0:T(8,128)(2,1)S(1)} collective-permute-done((f16[272,256]{1,0:T(8,128)(2,1)S(1)}, f16[272,256]{1,0:T(8,128)(2,1)S(1)}, u32[]{:S(2)}, u32[]{:S(2)}) %collective-permute-start.6) | collective-permute-done | bytes 139296 | tf_op jit(solution)/shard_map/ppermute | solution.py:273
  43.3 0.1 negate_select_fusion.2.refs_1_
  43.4 2.6 %collective-permute-done.13 = f16[272,256]{1,0:T(8,128)(2,1)S(1)} collective-permute-done((f16[272,256]{1,0:T(8,128)(2,1)S(1)}, f16[272,256]{1,0:T(8,128)(2,1)S(1)}, u32[]{:S(2)}, u32[]{:S(2)}) %collective-permute-start.13) | collective-permute-done | bytes 139296 | tf_op jit(solution)/shard_map/ppermute | solution.py:273
  46.0 0.1 negate_select_fusion.refs_3_
  46.1 1.3 %finish.1 = bf16[256,2,256]{2,1,0:T(2,128)(2,1)} custom-call(f32[256,256]{1,0:T(8,128)S(1)} %slice_add_fusion.1.refs_0_, f32[256,256]{1,0:T(8,128)S(1)} %negate_select_fusion.2.refs_1_, f32[256,256]{1,0:T(8,128)S(1)} %slice_add_fusion.refs_2_, f32[256,256]{1,0:T(8,128)S(1)} %negate_select_fusion.refs_3_), custom_call_target="tpu_custom_call" | custom-call | tf_op jit(solution)/shard_map/finish/pallas_call | solution.py:239
  (12 shorter events, 0.3 us)
Async XLA Ops:
  0.0 0.9 %copy-start.2 = (bf16[256,2,256]{2,1,0:T(2,128)(2,1)S(1)}, bf16[256,2,256]{2,1,0:T(2,128)(2,1)}, u32[]{:S(2)}) copy-start(bf16[256,2,256]{2,1,0:T(2,128)(2,1)} %fields_ref.1) | copy-start | bytes 786436
  1.3 14.6 %collective-permute-start = (bf16[2,144,256]{2,1,0:T(8,128)(2,1)S(1)}, bf16[2,144,256]{2,1,0:T(8,128)(2,1)S(1)}, u32[]{:S(2)}, u32[]{:S(2)}) collective-permute-start(bf16[2,144,256]{2,1,0:T(8,128)(2,1)S(1)} %get-tuple-element.19.block_ref), channel_id=1, source_target_pairs={{0,0},{8,1},{4,2},{12,3},{1,4},{9,5},{5,6},{13,7},{2,8},{10,9},{6,... | collective-permute-start | bytes 442376 | tf_op jit(solution)/shard_map/ppermute | solution.py:294
  2.0 17.2 %collective-permute-start.1 = (bf16[2,144,256]{2,1,0:T(8,128)(2,1)S(1)}, bf16[2,144,256]{2,1,0:T(8,128)(2,1)S(1)}, u32[]{:S(2)}, u32[]{:S(2)}) collective-permute-start(bf16[2,144,256]{2,1,0:T(8,128)(2,1)S(1)} %get-tuple-element.19.block_ref), channel_id=1, source_target_pairs={{8,0},{0,1},{12,2},{4,3},{9,4},{1,5},{13,6},{5,7},{10,8},{2,9},{14... | collective-permute-start | bytes 442376 | tf_op jit(solution)/shard_map/ppermute | solution.py:294
  6.3 16.4 %collective-permute-start.2 = (bf16[2,144,256]{2,1,0:T(8,128)(2,1)S(1)}, bf16[2,144,256]{2,1,0:T(8,128)(2,1)S(1)}, u32[]{:S(2)}, u32[]{:S(2)}) collective-permute-start(bf16[2,144,256]{2,1,0:T(8,128)(2,1)S(1)} %get-tuple-element.19.block_ref), channel_id=1, source_target_pairs={{4,0},{12,1},{0,2},{8,3},{5,4},{13,5},{1,6},{9,7},{6,8},{14,9},{2,... | collective-permute-start | bytes 442376 | tf_op jit(solution)/shard_map/ppermute | solution.py:294
  8.7 16.0 %collective-permute-start.3 = (bf16[2,144,256]{2,1,0:T(8,128)(2,1)S(1)}, bf16[2,144,256]{2,1,0:T(8,128)(2,1)S(1)}, u32[]{:S(2)}, u32[]{:S(2)}) collective-permute-start(bf16[2,144,256]{2,1,0:T(8,128)(2,1)S(1)} %get-tuple-element.19.block_ref), channel_id=1, source_target_pairs={{12,0},{4,1},{8,2},{0,3},{13,4},{5,5},{9,6},{1,7},{14,8},{6,9},{10... | collective-permute-start | bytes 442376 | tf_op jit(solution)/shard_map/ppermute | solution.py:294
  13.2 17.0 %collective-permute-start.7 = (bf16[2,112,256]{2,1,0:T(8,128)(2,1)S(1)}, bf16[2,112,256]{2,1,0:T(8,128)(2,1)S(1)}, u32[]{:S(2)}, u32[]{:S(2)}) collective-permute-start(bf16[2,112,256]{2,1,0:T(8,128)(2,1)S(1)} %get-tuple-element.26), channel_id=1, source_target_pairs={{0,0},{8,1},{4,2},{12,3},{1,4},{9,5},{5,6},{13,7},{2,8},{10,9},{6,... | collective-permute-start | bytes 344072 | tf_op jit(solution)/shard_map/ppermute | solution.py:294
  13.9 2.0 %copy-start = (bf16[27,256,256]{2,1,0:T(8,128)(2,1)S(1)}, bf16[27,256,256]{2,1,0:T(8,128)(2,1)}, u32[]{:S(2)}) copy-start(bf16[27,256,256]{2,1,0:T(8,128)(2,1)} %weight_ref.7) | copy-start | bytes 10616836
  15.9 8.8 %copy-start.1 = (bf16[27,256,256]{2,1,0:T(8,128)(2,1)S(1)}, bf16[27,256,256]{2,1,0:T(8,128)(2,1)}, u32[]{:S(2)}) copy-start(bf16[27,256,256]{2,1,0:T(8,128)(2,1)} %weight_ref.7) | copy-start | bytes 10616836
  15.9 14.3 %collective-permute-start.8 = (bf16[2,112,256]{2,1,0:T(8,128)(2,1)S(1)}, bf16[2,112,256]{2,1,0:T(8,128)(2,1)S(1)}, u32[]{:S(2)}, u32[]{:S(2)}) collective-permute-start(bf16[2,112,256]{2,1,0:T(8,128)(2,1)S(1)} %get-tuple-element.26), channel_id=1, source_target_pairs={{8,0},{0,1},{12,2},{4,3},{9,4},{1,5},{13,6},{5,7},{10,8},{2,9},{14... | collective-permute-start | bytes 344072 | tf_op jit(solution)/shard_map/ppermute | solution.py:294
  19.1 11.0 %collective-permute-start.9 = (bf16[2,112,256]{2,1,0:T(8,128)(2,1)S(1)}, bf16[2,112,256]{2,1,0:T(8,128)(2,1)S(1)}, u32[]{:S(2)}, u32[]{:S(2)}) collective-permute-start(bf16[2,112,256]{2,1,0:T(8,128)(2,1)S(1)} %get-tuple-element.26), channel_id=1, source_target_pairs={{4,0},{12,1},{0,2},{8,3},{5,4},{13,5},{1,6},{9,7},{6,8},{14,9},{2,... | collective-permute-start | bytes 344072 | tf_op jit(solution)/shard_map/ppermute | solution.py:294
  22.7 7.4 %collective-permute-start.10 = (bf16[2,112,256]{2,1,0:T(8,128)(2,1)S(1)}, bf16[2,112,256]{2,1,0:T(8,128)(2,1)S(1)}, u32[]{:S(2)}, u32[]{:S(2)}) collective-permute-start(bf16[2,112,256]{2,1,0:T(8,128)(2,1)S(1)} %get-tuple-element.26), channel_id=1, source_target_pairs={{12,0},{4,1},{8,2},{0,3},{13,4},{5,5},{9,6},{1,7},{14,8},{6,9},{10... | collective-permute-start | bytes 344072 | tf_op jit(solution)/shard_map/ppermute | solution.py:294
  28.9 6.4 %collective-permute-start.5 = (f32[272,256]{1,0:T(8,128)S(1)}, f32[272,256]{1,0:T(8,128)S(1)}, u32[]{:S(2)}, u32[]{:S(2)}) collective-permute-start(f32[272,256]{1,0:T(8,128)S(1)} %get-tuple-element.24), channel_id=1, source_target_pairs={{0,4},{4,0},{8,12},{12,8},{1,5},{5,1},{9,13},{13,9},{2,6},{6,2},{1... | collective-permute-start | bytes 835592 | tf_op jit(solution)/shard_map/ppermute | solution.py:273
  32.5 2.8 %collective-permute-start.12 = (f32[272,256]{1,0:T(8,128)S(1)}, f32[272,256]{1,0:T(8,128)S(1)}, u32[]{:S(2)}, u32[]{:S(2)}) collective-permute-start(f32[272,256]{1,0:T(8,128)S(1)} %get-tuple-element.32), channel_id=1, source_target_pairs={{0,4},{4,0},{8,12},{12,8},{1,5},{5,1},{9,13},{13,9},{2,6},{6,2},{1... | collective-permute-start | bytes 835592 | tf_op jit(solution)/shard_map/ppermute | solution.py:273
  32.6 6.4 %collective-permute-start.4 = (f32[272,256]{1,0:T(8,128)S(1)}, f32[272,256]{1,0:T(8,128)S(1)}, u32[]{:S(2)}, u32[]{:S(2)}) collective-permute-start(f32[272,256]{1,0:T(8,128)S(1)} %get-tuple-element.21), channel_id=1, source_target_pairs={{0,4},{4,0},{8,12},{12,8},{1,5},{5,1},{9,13},{13,9},{2,6},{6,2},{1... | collective-permute-start | bytes 835592 | tf_op jit(solution)/shard_map/ppermute | solution.py:273
  35.1 3.9 %collective-permute-start.11 = (f32[272,256]{1,0:T(8,128)S(1)}, f32[272,256]{1,0:T(8,128)S(1)}, u32[]{:S(2)}, u32[]{:S(2)}) collective-permute-start(f32[272,256]{1,0:T(8,128)S(1)} %get-tuple-element.29), channel_id=1, source_target_pairs={{0,4},{4,0},{8,12},{12,8},{1,5},{5,1},{9,13},{13,9},{2,6},{6,2},{1... | collective-permute-start | bytes 835592 | tf_op jit(solution)/shard_map/ppermute | solution.py:273
  35.7 7.6 %collective-permute-start.6 = (f16[272,256]{1,0:T(8,128)(2,1)S(1)}, f16[272,256]{1,0:T(8,128)(2,1)S(1)}, u32[]{:S(2)}, u32[]{:S(2)}) collective-permute-start(f16[272,256]{1,0:T(8,128)(2,1)S(1)} %pad_maximum_fusion), channel_id=1, source_target_pairs={{0,8},{4,12},{8,0},{12,4},{1,9},{5,13},{9,1},{13,5},{2,10},{6,14},... | collective-permute-start | bytes 417800 | tf_op jit(solution)/shard_map/ppermute | solution.py:273
  38.9 7.1 %collective-permute-start.13 = (f16[272,256]{1,0:T(8,128)(2,1)S(1)}, f16[272,256]{1,0:T(8,128)(2,1)S(1)}, u32[]{:S(2)}, u32[]{:S(2)}) collective-permute-start(f16[272,256]{1,0:T(8,128)(2,1)S(1)} %pad_maximum_fusion.1), channel_id=1, source_target_pairs={{0,8},{4,12},{8,0},{12,4},{1,9},{5,13},{9,1},{13,5},{2,10},{6,14},... | collective-permute-start | bytes 417800 | tf_op jit(solution)/shard_map/ppermute | solution.py:273

commit v4 on v3

--- a/solution.py
+++ b/solution.py
@@ -10,6 +10,7 @@
 NY = 16
 NZ = 16
 CUTS = (0, 9, 16)
+STEPS = [[(True, (1, 0))], [(False, (1,))], [(False, (0,))]]
 HEAD = 16
 LOWEST, SPAN = 14.0, 29.0
 VMEM_LIMIT = 16 * 2**20
@@ -25,6 +26,53 @@
     for bit in range(bits):
         out = out | (((value >> bit) & 1) << (bits - 1 - bit))
     return out
+
+
+def paired(index):
+    return index > 0
+
+
+def rounds_of(index, nc):
+    return nc // 2 if paired(index) else nc
+
+
+def sender(index, chan, round_index, ns, nc):
+    masks = ns // 2 if paired(index) else ns
+    mask, jump = round_index % masks, round_index // masks
+    source = reversed_bits(chan % ns, bit_count(ns)) ^ (2 * mask if paired(index) else mask)
+    return source, (jump + chan // ns) % (nc // ns)
+
+
+def pair_kernel(own_ref, mate_ref, out_ref):
+    depth = own_ref.shape[0]
+    core = lax.axis_index("space") % 2
+    out_ref[pl.ds(depth * core, depth)] = own_ref[...]
+    out_ref[pl.ds(depth * (1 - core), depth)] = mate_ref[...]
+
+
+def pair(own, mate):
+    depth, cells, count = own.shape
+    return pl.pallas_call(
+        pair_kernel,
+        out_shape=jax.ShapeDtypeStruct((2 * depth, cells, count), own.dtype),
+        in_specs=[IN_VMEM] * 2,
+        out_specs=IN_VMEM,
+        compiler_params=pltpu.CompilerParams(vmem_limit_bytes=VMEM_LIMIT // 2),
+        name="pair",
+    )(own, mate)
+
+
+def sent_parts(block, index, ns, nc):
+    payload = pair(block, swapped(block, 0, ns)) if paired(index) else block
+    parts = []
+    for round_index in range(rounds_of(index, nc)):
+        pairs = []
+        for s in range(ns):
+            for z in range(nc):
+                source, turn = sender(index, z, round_index, ns, nc)
+                pairs.append((source * nc + s * (nc // ns) + turn, s * nc + z))
+        parts.append(lax.ppermute(payload, ("space", "chan"), pairs))
+    return parts
 
 
 def transpose_kernel(cuts, fields_ref, *out_refs):
@@ -76,14 +124,12 @@
 def fill_window(plan, part_refs, window_ref):
     ns, nc, cuts, index = plan
     repeats = nc // ns
-    bits = bit_count(ns)
     low, high = cuts[index], cuts[index + 1]
     first = max(low - 1, 0)
     last = high if high == NY else high - 1
     top = first - 1
-    older_refs, newer_refs = part_refs[:-nc], part_refs[-nc:]
-    depth = newer_refs[0].shape[0]
-    count = newer_refs[0].shape[2]
+    depth = (window_ref.shape[0] - 2) // ns
+    count = part_refs[0].shape[2]
     taken = repeats * count
     planes = ns * depth
     chan = lax.axis_index("chan")
@@ -113,19 +159,25 @@
                 else:
                     pl.when(turn == slot)(store)
 
-    for round_index in range(nc):
-        mask, jump = round_index % ns, round_index // ns
-        source = reversed_bits((chan % ns) ^ mask, bits)
-        turn = (jump + chan // ns) % repeats
-        for plane in range(depth):
-            where = 1 + source * depth + plane
-            if index:
-                begin = max(top, 0)
-                older = older_refs[round_index]
-                put(older[plane, (begin - cuts[index - 1]) * NZ :, :], begin, where, turn)
-            put(newer_refs[round_index][plane], low, where, turn)
-
-def add_up(plan, far, weight_ref, window_ref, mate_ref, keep_ref):
+    count_new = rounds_of(index, nc)
+    sets = [(index, part_refs[-count_new:])]
+    if index:
+        sets.append((index - 1, part_refs[:-count_new]))
+    for index_of, refs in sets:
+        skipped = max(top - cuts[index_of], 0)
+        for round_index, part_ref in enumerate(refs):
+            source, turn = sender(index_of, chan, round_index, ns, nc)
+            begin = (source // 2 * 2 if paired(index_of) else source) * depth
+            for plane in range(part_ref.shape[0]):
+                put(
+                    part_ref[plane, skipped * NZ :, :],
+                    cuts[index_of] + skipped,
+                    1 + begin + plane,
+                    turn,
+                )
+
+
+def add_up(plan, far, cores, weight_ref, window_ref, out_refs):
     ns, nc, cuts, index = plan
     depth = (window_ref.shape[0] - 2) // ns
     cells = window_ref.shape[1] - 2 * NZ
@@ -133,16 +185,17 @@
     groups = ns // 4
     for order in range(groups):
         mask = 2 * (groups - 1 - order + (groups if far else 0))
-        owners = [space ^ (mask + 1), space ^ mask]
         total = None
         for pair in range(9):
             a, b = divmod(pair, 3)
             left = jnp.concatenate(
                 [
                     window_ref[
-                        pl.ds(depth * owner + a, depth), b * NZ : b * NZ + cells, :
+                        pl.ds(depth * (space ^ (mask + core)) + a, depth),
+                        b * NZ : b * NZ + cells,
+                        :,
                     ].reshape(depth * cells, -1)
-                    for owner in owners
+                    for core in cores
                 ],
                 axis=0,
             )
@@ -152,51 +205,48 @@
             )
             total = product if total is None else total + product
         begin, rows = HEAD + order * depth * cells, depth * cells
-        mate_ref[begin : begin + rows] = total[:rows]
-        keep_ref[begin : begin + rows] = total[rows:]
-    for ref in (mate_ref, keep_ref):
+        for at, ref in enumerate(out_refs):
+            ref[begin : begin + rows] = total[at * rows : (at + 1) * rows]
+    for ref in out_refs:
         peak = jnp.max(jnp.abs(ref[HEAD:]), axis=0, keepdims=True)
         ref[:HEAD] = jnp.broadcast_to(peak, (HEAD, ref.shape[1]))
 
 
-def first_kernel(plan, token_ref, weight_ref, *refs):
-    *part_refs, mate_ref, keep_ref, window_ref = refs
+def first_kernel(plan, jobs, token_ref, weight_ref, *refs):
+    *refs, window_ref = refs
+    count = sum(len(cores) for _, cores in jobs)
+    part_refs, out_refs = refs[:-count], refs[-count:]
     fill_window(plan, part_refs, window_ref)
-    add_up(plan, True, weight_ref, window_ref, mate_ref, keep_ref)
-
-
-def second_kernel(plan, token_ref, weight_ref, window_ref, mate_ref, keep_ref):
-    add_up(plan, False, weight_ref, window_ref, mate_ref, keep_ref)
-
-
-def both_kernel(plan, token_ref, weight_ref, *refs):
-    *part_refs, far_mate, far_keep, near_mate, near_keep, window_ref = refs
-    fill_window(plan, part_refs, window_ref)
-    add_up(plan, True, weight_ref, window_ref, far_mate, far_keep)
-    add_up(plan, False, weight_ref, window_ref, near_mate, near_keep)
-
-
-def partial_sums(token, older, newer, weights, plan, at_once):
+    for far, cores in jobs:
+        add_up(plan, far, cores, weight_ref, window_ref, out_refs[: len(cores)])
+        out_refs = out_refs[len(cores) :]
+
+
+def later_kernel(plan, jobs, token_ref, weight_ref, window_ref, *out_refs):
+    for far, cores in jobs:
+        add_up(plan, far, cores, weight_ref, window_ref, out_refs)
+
+
+def partial_sums(token, older, newer, weights, depth, plan, at_once):
     ns, nc, cuts, index = plan
     low, high = cuts[index], cuts[index + 1]
     first = max(low - 1, 0)
     last = high if high == NY else high - 1
-    depth = newer[0].shape[0]
     owned, taken = weights.shape[1:]
     cells = (last - first) * NZ
     sums = jax.ShapeDtypeStruct((HEAD + ns // 4 * depth * cells, owned), jnp.float32)
     window = (ns * depth + 2, cells + 2 * NZ, 3 * taken)
 
-    def call(kernel, inputs, out_shape, scratch_shapes):
+    def call(kernel, jobs, inputs, out_shape, scratch_shapes, token=token):
         return pl.pallas_call(
-            functools.partial(kernel, plan),
+            functools.partial(kernel, plan, jobs),
             out_shape=out_shape,
             in_specs=[pl.BlockSpec(memory_space=pl.ANY)] + [IN_VMEM] * (1 + len(inputs)),
             out_specs=[IN_VMEM] * len(out_shape),
             scratch_shapes=scratch_shapes,
             compiler_params=pltpu.CompilerParams(vmem_limit_bytes=VMEM_LIMIT),
             cost_estimate=pl.CostEstimate(
-                flops=27 * len(out_shape) // 2 * ns * depth * cells * owned * taken,
+                flops=27 * 2 * sum(len(cores) for _, cores in jobs) * ns // 4 * depth * cells * owned * taken,
                 bytes_accessed=2 * weights.size,
                 transcendentals=0,
             ),
@@ -205,15 +255,24 @@
 
     parts = [*older, *newer]
     if at_once:
+        jobs = [(True, (1, 0)), (False, (1, 0))]
         far_mate, far_keep, near_mate, near_keep = call(
-            both_kernel, parts, [sums] * 4, [pltpu.VMEM(window, weights.dtype)]
+            first_kernel, jobs, parts, [sums] * 4, [pltpu.VMEM(window, weights.dtype)]
         )
-    else:
-        far_mate, far_keep, filled = call(
-            first_kernel, parts, [sums] * 2 + [jax.ShapeDtypeStruct(window, weights.dtype)], []
-        )
-        near_mate, near_keep = call(second_kernel, [filled], [sums] * 2, [])
-    return (far_mate, far_keep), (near_mate, near_keep)
+        return far_mate, far_keep, near_mate, lambda token: near_keep
+    results = []
+    for jobs in STEPS[:-1]:
+        count = sum(len(cores) for _, cores in jobs)
+        if not results:
+            filled = jax.ShapeDtypeStruct(window, weights.dtype)
+            *results, filled = call(first_kernel, jobs, parts, [sums] * count + [filled], [])
+        else:
+            results += call(later_kernel, jobs, [filled], [sums] * count, [])
+
+    def last(token):
+        return call(later_kernel, STEPS[-1], [filled], [sums], [], token)[0]
+
+    return *results, last
 
 
 def finish_kernel(counts, *refs):
@@ -280,32 +339,27 @@
     depth = fields.shape[1]
     blocks = by_cell(fields, CUTS)
     token = hold(blocks[0], conv_weight)
-    received = []
-    for index, block in enumerate(blocks):
-        arrived = []
-        for round_index in range(nc):
-            mask, jump = round_index % ns, round_index // ns
-            pairs = []
-            for s in range(ns):
-                for z in range(nc):
-                    source = reversed_bits((z % ns) ^ mask, bits)
-                    turn = (jump + z // ns) % repeats
-                    pairs.append((source * nc + s * repeats + turn, s * nc + z))
-            arrived.append(lax.ppermute(block, ("space", "chan"), pairs))
-        received.append(arrived)
+    received = [sent_parts(block, index, ns, nc) for index, block in enumerate(blocks)]
     groups = []
     for index, newer in enumerate(received):
         older = received[index - 1] if index else []
         plan = (ns, nc, CUTS, index)
-        far, near = partial_sums(token, older, newer, conv_weight, plan, index == 0)
-        token, mate = lax.optimization_barrier((token, far[0]))
-        far = (mate, far[1])
-        far, near = [keep + swapped(mate, 0, ns) for mate, keep in (far, near)]
+        far_mate, far_keep, near_mate, last = partial_sums(
+            token, older, newer, conv_weight, depth, plan, index == 0
+        )
+        token, far_mate = lax.optimization_barrier((token, far_mate))
+        far, after = far_keep + swapped(far_mate, 0, ns), token
+        if bits == 2:
+            sent = coded(far)
+            after, sent = lax.optimization_barrier((token, sent))
+        near = last(after) + swapped(near_mate, 0, ns)
         for bit in range(bits - 1, 1, -1):
             total = near + swapped(far, bit, ns)
             middle = HEAD + (total.shape[0] - HEAD) // 2
             far, near = total[:middle], jnp.concatenate([total[:HEAD], total[middle:]])
-        groups.append([near[HEAD:], decoded(swapped(coded(far), 1, ns))])
+        if bits > 2:
+            sent = coded(far)
+        groups.append([near[HEAD:], decoded(swapped(sent, 1, ns))])
     return finish(groups, fields.shape[1], fields.dtype)
 
 

time: 47.7 us -> 46.6 us (0.977)
  waiting for transfers between devices: 6.8 us -> 5.61 us
    ppermute x8 -> x6, starting transfers between devices: 21.3 us -> 16.3 us  [sent_parts(): parts.append(lax.ppermute(payload, ('space', 'chan'), pairs))]
    ppermute x6 -> x7, starting transfers between devices: 5.12 us -> 9.99 us  [swapped(): return lax.ppermute(value, 'space', [(i, i ^ 1 << bit) for i in range(ns)])]
    ppermute x6 -> x7, waiting for transfers between devices: 6.78 us -> 5.48 us  [swapped(): return lax.ppermute(value, 'space', [(i, i ^ 1 << bit) for i in range(ns)])]
    pallas_call x3 -> x5, Pallas kernels: 8.62 us -> 8.85 us  [the longest x4 8.83 us: call(): pl.pallas_call(functools.partial(kernel, plan, jobs), out_shape=out_shape...]
  transfers between devices with their start and end apart: 14 -> 13, of which waited for: 2 -> 3; matrix products, arithmetic and copies ran while one was open for 1% -> 1% of each run, Pallas kernels for 18% -> 19%
where the time goes in v4:
time: 46.6 us; the launch traced here: 46.4 us
  starting transfers between devices  26.3 us (56%)
  Pallas kernels  10.5 us (23%)
  waiting for transfers between devices  5.61 us (12%)
  local copies, waits for them, and re-layouts  2.95 us (6%)
  other arithmetic  0.77 us (2%)
    ppermute x6, starting transfers between devices, sent_parts(): parts.append(lax.ppermute(payload, ('space', 'chan'), pairs))  16.3 us
    ppermute x7, starting transfers between devices, swapped(): return lax.ppermute(value, 'space', [(i, i ^ 1 << bit) for i in range(ns)])  9.99 us
    pallas_call x4, Pallas kernels, call(): pl.pallas_call(functools.partial(kernel, plan, jobs), out_shape=out_shape...  8.83 us
    ppermute x7, waiting for transfers between devices, swapped(): return lax.ppermute(value, 'space', [(i, i ^ 1 << bit) for i in range(ns)])  5.48 us
    unnamed x6, local copies, waits for them, and re-layouts  2.95 us
    pallas_call x1, Pallas kernels, finish(): pl.pallas_call(functools.partial(finish_kernel, [len(pieces) for pieces i...  1.33 us
  transfers between devices with their start and end apart: 13, of which 3 were waited for; matrix products, arithmetic and copies ran while one was open for 1% of the time, Pallas kernels for 19%

profile of v4, /device:TPU:0, one launch (start us, length us, event | category | flops | bytes accessed | tf_op | source)
XLA Modules:
  0.0 46.4 jit_solution(3029375845416246226)
XLA Ops:
  0.0 0.0 copy-start.2
  0.0 0.9 %copy-done.2 = bf16[256,2,256]{2,1,0:T(2,128)(2,1)S(1)} copy-done((bf16[256,2,256]{2,1,0:T(2,128)(2,1)S(1)}, bf16[256,2,256]{2,1,0:T(2,128)(2,1)}, u32[]{:S(2)}) %copy-start.2) | copy-done | bytes 262168
  1.0 0.3 by_cell.1
  1.3 0.7 %collective-permute-start = (bf16[2,144,256]{2,1,0:T(8,128)(2,1)S(1)}, bf16[2,144,256]{2,1,0:T(8,128)(2,1)S(1)}, u32[]{:S(2)}, u32[]{:S(2)}) collective-permute-start(bf16[2,144,256]{2,1,0:T(8,128)(2,1)S(1)} %get-tuple-element.21.block_ref), channel_id=1, source_target_pairs={{0,0},{8,1},{4,2},{12,3},{1,4},{9,5},{5,6},{13,7},{2,8},{10,9},{6,... | collective-permute-start | bytes 442376 | tf_op jit(solution)/shard_map/ppermute | solution.py:74
  2.0 6.6 %collective-permute-start.1 = (bf16[2,144,256]{2,1,0:T(8,128)(2,1)S(1)}, bf16[2,144,256]{2,1,0:T(8,128)(2,1)S(1)}, u32[]{:S(2)}, u32[]{:S(2)}) collective-permute-start(bf16[2,144,256]{2,1,0:T(8,128)(2,1)S(1)} %get-tuple-element.21.block_ref), channel_id=1, source_target_pairs={{4,0},{12,1},{0,2},{8,3},{5,4},{13,5},{1,6},{9,7},{6,8},{14,9},{2,... | collective-permute-start | bytes 442376 | tf_op jit(solution)/shard_map/ppermute | solution.py:74
  8.6 0.5 %collective-permute-start.2 = (bf16[2,144,256]{2,1,0:T(8,128)(2,1)S(1)}, bf16[2,144,256]{2,1,0:T(8,128)(2,1)S(1)}, u32[]{:S(2)}, u32[]{:S(2)}) collective-permute-start(bf16[2,144,256]{2,1,0:T(8,128)(2,1)S(1)} %get-tuple-element.21.block_ref), channel_id=1, source_target_pairs={{8,0},{0,1},{12,2},{4,3},{9,4},{1,5},{13,6},{5,7},{10,8},{2,9},{14... | collective-permute-start | bytes 442376 | tf_op jit(solution)/shard_map/ppermute | solution.py:74
  9.1 4.2 %collective-permute-start.3 = (bf16[2,144,256]{2,1,0:T(8,128)(2,1)S(1)}, bf16[2,144,256]{2,1,0:T(8,128)(2,1)S(1)}, u32[]{:S(2)}, u32[]{:S(2)}) collective-permute-start(bf16[2,144,256]{2,1,0:T(8,128)(2,1)S(1)} %get-tuple-element.21.block_ref), channel_id=1, source_target_pairs={{12,0},{4,1},{8,2},{0,3},{13,4},{5,5},{9,6},{1,7},{14,8},{6,9},{10... | collective-permute-start | bytes 442376 | tf_op jit(solution)/shard_map/ppermute | solution.py:74
  13.3 0.1 collective-permute-start.7
  13.4 0.0 copy-start
  13.4 2.0 %copy-done = bf16[27,256,256]{2,1,0:T(8,128)(2,1)S(1)} copy-done((bf16[27,256,256]{2,1,0:T(8,128)(2,1)S(1)}, bf16[27,256,256]{2,1,0:T(8,128)(2,1)}, u32[]{:S(2)}) %copy-start) | copy-done | bytes 3538968
  15.4 0.0 copy-start.1
  15.4 0.0 collective-permute-done.7.mate_ref
  15.4 0.8 %collective-permute-start.8 = (bf16[4,112,256]{2,1,0:T(8,128)(2,1)S(1)}, bf16[4,112,256]{2,1,0:T(8,128)(2,1)S(1)}, u32[]{:S(2)}, u32[]{:S(2)}) collective-permute-start(bf16[4,112,256]{2,1,0:T(8,128)(2,1)S(1)} %pair.1), channel_id=1, source_target_pairs={{0,0},{8,1},{4,2},{12,3},{1,4},{9,5},{5,6},{13,7},{2,8},{10,9},{6,... | collective-permute-start | bytes 688136 | tf_op jit(solution)/shard_map/ppermute | solution.py:74
  16.2 0.0 collective-permute-done.refs_0_
  16.2 3.5 %collective-permute-start.9 = (bf16[4,112,256]{2,1,0:T(8,128)(2,1)S(1)}, bf16[4,112,256]{2,1,0:T(8,128)(2,1)S(1)}, u32[]{:S(2)}, u32[]{:S(2)}) collective-permute-start(bf16[4,112,256]{2,1,0:T(8,128)(2,1)S(1)} %pair.1), channel_id=1, source_target_pairs={{8,0},{0,1},{12,2},{4,3},{9,4},{1,5},{13,6},{5,7},{10,8},{2,9},{14... | collective-permute-start | bytes 688136 | tf_op jit(solution)/shard_map/ppermute | solution.py:74
  19.8 0.0 collective-permute-done.1.refs_1_
  19.8 0.0 collective-permute-done.2.refs_2_
  19.8 0.0 collective-permute-done.3.refs_3_
  19.8 0.0 copy-done.1
  19.8 4.3 %partial_sums.4 = (f32[272,256]{1,0:T(8,128)S(1)}, f32[272,256]{1,0:T(8,128)S(1)}, f32[272,256]{1,0:T(8,128)S(1)}, f32[272,256]{1,0:T(8,128)S(1)}) custom-call(f32[8,128]{1,0:T(8,128)S(1)} %hold.1.token_ref, bf16[27,256,256]{2,1,0:T(8,128)(2,1)S(1)} %copy-done.1, bf16[2,144,256]{2,1,0:T(8,128)(2,1)S(1)} %collective-permute-done.refs_0_, ...), custom_call_target="tpu_custom_call" | custom-call | flops 3623878656 | bytes 3538944 | tf_op jit(solution)/shard_map/partial_sums/pallas_call | solution.py:241
  24.1 3.6 %collective-permute-start.4 = (f32[272,256]{1,0:T(8,128)S(1)}, f32[272,256]{1,0:T(8,128)S(1)}, u32[]{:S(2)}, u32[]{:S(2)}) collective-permute-start(f32[272,256]{1,0:T(8,128)S(1)} %get-tuple-element.23), channel_id=1, source_target_pairs={{0,4},{4,0},{8,12},{12,8},{1,5},{5,1},{9,13},{13,9},{2,6},{6,2},{1... | collective-permute-start | bytes 835592 | tf_op jit(solution)/shard_map/ppermute | solution.py:332
  27.6 0.1 collective-permute-start.5
  27.7 0.0 collective-permute-done.8.refs_4_
  27.7 0.1 collective-permute-done.9.refs_5_
  27.8 2.3 %partial_sums.5 = (f32[272,256]{1,0:T(8,128)S(1)}, f32[272,256]{1,0:T(8,128)S(1)}, bf16[10,160,768]{2,1,0:T(8,128)(2,1)S(1)}) custom-call(f32[8,128]{1,0:T(8,128)S(1)} %hold.1.token_ref, bf16[27,256,256]{2,1,0:T(8,128)(2,1)S(1)} %copy-done.1, bf16[2,144,256]{2,1,0:T(8,128)(2,1)S(1)} %collective-permute-done.refs_0_, ...), custom_call_target="tpu_custom_call" | custom-call | flops 1811939328 | bytes 3538944 | tf_op jit(solution)/shard_map/partial_sums/pallas_call | solution.py:241
  30.2 0.4 collective-permute-start.10
  30.5 1.1 %partial_sums.7 = f32[272,256]{1,0:T(8,128)S(1)} custom-call(f32[8,128]{1,0:T(8,128)S(1)} %hold.1.token_ref, bf16[27,256,256]{2,1,0:T(8,128)(2,1)S(1)} %copy-done.1, bf16[10,160,768]{2,1,0:T(8,128)(2,1)S(1)} %get-tuple-element.35.window_ref), custom_call_target="tpu_custom_call" | custom-call | flops 905969664 | bytes 3538944 | tf_op jit(solution)/shard_map/partial_sums/pallas_call | solution.py:241
  31.7 0.3 collective-permute-start.11
  31.9 0.0 collective-permute-done.5
  32.0 0.0 collective-permute-done.4
  32.0 0.0 collective-permute-done.10
  32.1 0.1 select_convert_fusion
  32.2 0.1 fusion.8
  32.3 0.1 fusion.9
  32.4 0.1 pad_maximum_fusion
  32.5 5.6 %collective-permute-start.6 = (f16[272,256]{1,0:T(8,128)(2,1)S(1)}, f16[272,256]{1,0:T(8,128)(2,1)S(1)}, u32[]{:S(2)}, u32[]{:S(2)}) collective-permute-start(f16[272,256]{1,0:T(8,128)(2,1)S(1)} %get-tuple-element.28), channel_id=1, source_target_pairs={{0,8},{4,12},{8,0},{12,4},{1,9},{5,13},{9,1},{13,5},{2,10},{6,14},... | collective-permute-start | bytes 417800 | tf_op jit(solution)/shard_map/ppermute | solution.py:332
  38.1 0.1 collective-permute-start.12
  38.1 1.1 %partial_sums.6 = f32[272,256]{1,0:T(8,128)S(1)} custom-call(f32[8,128]{1,0:T(8,128)S(1)} %hold.1.token_ref, bf16[27,256,256]{2,1,0:T(8,128)(2,1)S(1)} %copy-done.1, bf16[10,160,768]{2,1,0:T(8,128)(2,1)S(1)} %get-tuple-element.35.window_ref), custom_call_target="tpu_custom_call" | custom-call | flops 905969664 | bytes 3538944 | tf_op jit(solution)/shard_map/partial_sums/pallas_call | solution.py:241
  39.3 0.0 collective-permute-done.11
  39.3 3.2 %collective-permute-done.6 = f16[272,256]{1,0:T(8,128)(2,1)S(1)} collective-permute-done((f16[272,256]{1,0:T(8,128)(2,1)S(1)}, f16[272,256]{1,0:T(8,128)(2,1)S(1)}, u32[]{:S(2)}, u32[]{:S(2)}) %collective-permute-start.6) | collective-permute-done | bytes 139296 | tf_op jit(solution)/shard_map/ppermute | solution.py:332
  42.6 0.1 negate_select_fusion.2.refs_1_
  42.7 2.3 %collective-permute-done.12 = f16[272,256]{1,0:T(8,128)(2,1)S(1)} collective-permute-done((f16[272,256]{1,0:T(8,128)(2,1)S(1)}, f16[272,256]{1,0:T(8,128)(2,1)S(1)}, u32[]{:S(2)}, u32[]{:S(2)}) %collective-permute-start.12) | collective-permute-done | bytes 139296 | tf_op jit(solution)/shard_map/ppermute | solution.py:332
  44.9 0.1 negate_select_fusion.refs_3_
  45.0 1.3 %finish.1 = bf16[256,2,256]{2,1,0:T(2,128)(2,1)} custom-call(f32[256,256]{1,0:T(8,128)S(1)} %slice_add_fusion.1.refs_0_, f32[256,256]{1,0:T(8,128)S(1)} %negate_select_fusion.2.refs_1_, f32[256,256]{1,0:T(8,128)S(1)} %slice_add_fusion.refs_2_, f32[256,256]{1,0:T(8,128)S(1)} %negate_select_fusion.refs_3_), custom_call_target="tpu_custom_call" | custom-call | tf_op jit(solution)/shard_map/finish/pallas_call | solution.py:298
  (11 shorter events, 0.2 us)
Async XLA Ops:
  0.0 0.9 %copy-start.2 = (bf16[256,2,256]{2,1,0:T(2,128)(2,1)S(1)}, bf16[256,2,256]{2,1,0:T(2,128)(2,1)}, u32[]{:S(2)}) copy-start(bf16[256,2,256]{2,1,0:T(2,128)(2,1)} %fields_ref.1) | copy-start | bytes 786436
  1.3 14.9 %collective-permute-start = (bf16[2,144,256]{2,1,0:T(8,128)(2,1)S(1)}, bf16[2,144,256]{2,1,0:T(8,128)(2,1)S(1)}, u32[]{:S(2)}, u32[]{:S(2)}) collective-permute-start(bf16[2,144,256]{2,1,0:T(8,128)(2,1)S(1)} %get-tuple-element.21.block_ref), channel_id=1, source_target_pairs={{0,0},{8,1},{4,2},{12,3},{1,4},{9,5},{5,6},{13,7},{2,8},{10,9},{6,... | collective-permute-start | bytes 442376 | tf_op jit(solution)/shard_map/ppermute | solution.py:74
  2.0 17.8 %collective-permute-start.1 = (bf16[2,144,256]{2,1,0:T(8,128)(2,1)S(1)}, bf16[2,144,256]{2,1,0:T(8,128)(2,1)S(1)}, u32[]{:S(2)}, u32[]{:S(2)}) collective-permute-start(bf16[2,144,256]{2,1,0:T(8,128)(2,1)S(1)} %get-tuple-element.21.block_ref), channel_id=1, source_target_pairs={{4,0},{12,1},{0,2},{8,3},{5,4},{13,5},{1,6},{9,7},{6,8},{14,9},{2,... | collective-permute-start | bytes 442376 | tf_op jit(solution)/shard_map/ppermute | solution.py:74
  8.6 11.2 %collective-permute-start.2 = (bf16[2,144,256]{2,1,0:T(8,128)(2,1)S(1)}, bf16[2,144,256]{2,1,0:T(8,128)(2,1)S(1)}, u32[]{:S(2)}, u32[]{:S(2)}) collective-permute-start(bf16[2,144,256]{2,1,0:T(8,128)(2,1)S(1)} %get-tuple-element.21.block_ref), channel_id=1, source_target_pairs={{8,0},{0,1},{12,2},{4,3},{9,4},{1,5},{13,6},{5,7},{10,8},{2,9},{14... | collective-permute-start | bytes 442376 | tf_op jit(solution)/shard_map/ppermute | solution.py:74
  9.1 10.7 %collective-permute-start.3 = (bf16[2,144,256]{2,1,0:T(8,128)(2,1)S(1)}, bf16[2,144,256]{2,1,0:T(8,128)(2,1)S(1)}, u32[]{:S(2)}, u32[]{:S(2)}) collective-permute-start(bf16[2,144,256]{2,1,0:T(8,128)(2,1)S(1)} %get-tuple-element.21.block_ref), channel_id=1, source_target_pairs={{12,0},{4,1},{8,2},{0,3},{13,4},{5,5},{9,6},{1,7},{14,8},{6,9},{10... | collective-permute-start | bytes 442376 | tf_op jit(solution)/shard_map/ppermute | solution.py:74
  13.3 2.1 %collective-permute-start.7 = (bf16[2,112,256]{2,1,0:T(8,128)(2,1)S(1)}, bf16[2,112,256]{2,1,0:T(8,128)(2,1)S(1)}, u32[]{:S(2)}, u32[]{:S(2)}) collective-permute-start(bf16[2,112,256]{2,1,0:T(8,128)(2,1)S(1)} %get-tuple-element.29.own_ref), channel_id=1, source_target_pairs={{0,4},{4,0},{8,12},{12,8},{1,5},{5,1},{9,13},{13,9},{2,6},{6,2},{1... | collective-permute-start | bytes 344072 | tf_op jit(solution)/shard_map/ppermute | solution.py:332
  13.4 2.0 %copy-start = (bf16[27,256,256]{2,1,0:T(8,128)(2,1)S(1)}, bf16[27,256,256]{2,1,0:T(8,128)(2,1)}, u32[]{:S(2)}) copy-start(bf16[27,256,256]{2,1,0:T(8,128)(2,1)} %weight_ref.9) | copy-start | bytes 10616836
  15.4 4.4 %copy-start.1 = (bf16[27,256,256]{2,1,0:T(8,128)(2,1)S(1)}, bf16[27,256,256]{2,1,0:T(8,128)(2,1)}, u32[]{:S(2)}) copy-start(bf16[27,256,256]{2,1,0:T(8,128)(2,1)} %weight_ref.9) | copy-start | bytes 10616836
  15.4 12.3 %collective-permute-start.8 = (bf16[4,112,256]{2,1,0:T(8,128)(2,1)S(1)}, bf16[4,112,256]{2,1,0:T(8,128)(2,1)S(1)}, u32[]{:S(2)}, u32[]{:S(2)}) collective-permute-start(bf16[4,112,256]{2,1,0:T(8,128)(2,1)S(1)} %pair.1), channel_id=1, source_target_pairs={{0,0},{8,1},{4,2},{12,3},{1,4},{9,5},{5,6},{13,7},{2,8},{10,9},{6,... | collective-permute-start | bytes 688136 | tf_op jit(solution)/shard_map/ppermute | solution.py:74
  16.2 11.6 %collective-permute-start.9 = (bf16[4,112,256]{2,1,0:T(8,128)(2,1)S(1)}, bf16[4,112,256]{2,1,0:T(8,128)(2,1)S(1)}, u32[]{:S(2)}, u32[]{:S(2)}) collective-permute-start(bf16[4,112,256]{2,1,0:T(8,128)(2,1)S(1)} %pair.1), channel_id=1, source_target_pairs={{8,0},{0,1},{12,2},{4,3},{9,4},{1,5},{13,6},{5,7},{10,8},{2,9},{14... | collective-permute-start | bytes 688136 | tf_op jit(solution)/shard_map/ppermute | solution.py:74
  24.1 7.9 %collective-permute-start.4 = (f32[272,256]{1,0:T(8,128)S(1)}, f32[272,256]{1,0:T(8,128)S(1)}, u32[]{:S(2)}, u32[]{:S(2)}) collective-permute-start(f32[272,256]{1,0:T(8,128)S(1)} %get-tuple-element.23), channel_id=1, source_target_pairs={{0,4},{4,0},{8,12},{12,8},{1,5},{5,1},{9,13},{13,9},{2,6},{6,2},{1... | collective-permute-start | bytes 835592 | tf_op jit(solution)/shard_map/ppermute | solution.py:332
  27.6 4.3 %collective-permute-start.5 = (f32[272,256]{1,0:T(8,128)S(1)}, f32[272,256]{1,0:T(8,128)S(1)}, u32[]{:S(2)}, u32[]{:S(2)}) collective-permute-start(f32[272,256]{1,0:T(8,128)S(1)} %get-tuple-element.27), channel_id=1, source_target_pairs={{0,4},{4,0},{8,12},{12,8},{1,5},{5,1},{9,13},{13,9},{2,6},{6,2},{1... | collective-permute-start | bytes 835592 | tf_op jit(solution)/shard_map/ppermute | solution.py:332
  30.2 1.9 %collective-permute-start.10 = (f32[272,256]{1,0:T(8,128)S(1)}, f32[272,256]{1,0:T(8,128)S(1)}, u32[]{:S(2)}, u32[]{:S(2)}) collective-permute-start(f32[272,256]{1,0:T(8,128)S(1)} %get-tuple-element.33), channel_id=1, source_target_pairs={{0,4},{4,0},{8,12},{12,8},{1,5},{5,1},{9,13},{13,9},{2,6},{6,2},{1... | collective-permute-start | bytes 835592 | tf_op jit(solution)/shard_map/ppermute | solution.py:332
  31.7 7.6 %collective-permute-start.11 = (f32[272,256]{1,0:T(8,128)S(1)}, f32[272,256]{1,0:T(8,128)S(1)}, u32[]{:S(2)}, u32[]{:S(2)}) collective-permute-start(f32[272,256]{1,0:T(8,128)S(1)} %partial_sums.7), channel_id=1, source_target_pairs={{0,4},{4,0},{8,12},{12,8},{1,5},{5,1},{9,13},{13,9},{2,6},{6,2},{1... | collective-permute-start | bytes 835592 | tf_op jit(solution)/shard_map/ppermute | solution.py:332
  32.5 10.0 %collective-permute-start.6 = (f16[272,256]{1,0:T(8,128)(2,1)S(1)}, f16[272,256]{1,0:T(8,128)(2,1)S(1)}, u32[]{:S(2)}, u32[]{:S(2)}) collective-permute-start(f16[272,256]{1,0:T(8,128)(2,1)S(1)} %get-tuple-element.28), channel_id=1, source_target_pairs={{0,8},{4,12},{8,0},{12,4},{1,9},{5,13},{9,1},{13,5},{2,10},{6,14},... | collective-permute-start | bytes 417800 | tf_op jit(solution)/shard_map/ppermute | solution.py:332
  38.1 6.8 %collective-permute-start.12 = (f16[272,256]{1,0:T(8,128)(2,1)S(1)}, f16[272,256]{1,0:T(8,128)(2,1)S(1)}, u32[]{:S(2)}, u32[]{:S(2)}) collective-permute-start(f16[272,256]{1,0:T(8,128)(2,1)S(1)} %get-tuple-element.36), channel_id=1, source_target_pairs={{0,8},{4,12},{8,0},{12,4},{1,9},{5,13},{9,1},{13,5},{2,10},{6,14},... | collective-permute-start | bytes 417800 | tf_op jit(solution)/shard_map/ppermute | solution.py:332

commit v5 on v4

--- a/solution.py
+++ b/solution.py
@@ -10,7 +10,7 @@
 NY = 16
 NZ = 16
 CUTS = (0, 9, 16)
-STEPS = [[(True, (1, 0))], [(False, (1,))], [(False, (0,))]]
+STEPS = [[(True, (1,))], [(True, (0,)), (False, (1,))], [(False, (0,))]]
 HEAD = 16
 LOWEST, SPAN = 14.0, 29.0
 VMEM_LIMIT = 16 * 2**20
@@ -224,7 +224,8 @@
 
 def later_kernel(plan, jobs, token_ref, weight_ref, window_ref, *out_refs):
     for far, cores in jobs:
-        add_up(plan, far, cores, weight_ref, window_ref, out_refs)
+        add_up(plan, far, cores, weight_ref, window_ref, out_refs[: len(cores)])
+        out_refs = out_refs[len(cores) :]
 
 
 def partial_sums(token, older, newer, weights, depth, plan, at_once):

time: 46.6 us -> 46.6 us (level)
  no operation moved by 1% of the time
where the time goes in v5:
time: 46.6 us; the launch traced here: 46.4 us
  starting transfers between devices  26.3 us (56%)
  Pallas kernels  10.5 us (23%)
  waiting for transfers between devices  5.61 us (12%)
  local copies, waits for them, and re-layouts  2.95 us (6%)
  other arithmetic  0.76 us (2%)
    ppermute x6, starting transfers between devices, sent_parts(): parts.append(lax.ppermute(payload, ('space', 'chan'), pairs))  16.3 us
    ppermute x7, starting transfers between devices, swapped(): return lax.ppermute(value, 'space', [(i, i ^ 1 << bit) for i in range(ns)])  9.99 us
    pallas_call x4, Pallas kernels, call(): pl.pallas_call(functools.partial(kernel, plan, jobs), out_shape=out_shape...  8.82 us
    ppermute x7, waiting for transfers between devices, swapped(): return lax.ppermute(value, 'space', [(i, i ^ 1 << bit) for i in range(ns)])  5.48 us
    unnamed x6, local copies, waits for them, and re-layouts  2.95 us
    pallas_call x1, Pallas kernels, finish(): pl.pallas_call(functools.partial(finish_kernel, [len(pieces) for pieces i...  1.33 us
  transfers between devices with their start and end apart: 13, of which 3 were waited for; matrix products, arithmetic and copies ran while one was open for 1% of the time, Pallas kernels for 19%

profile of v5, /device:TPU:0, one launch (start us, length us, event | category | flops | bytes accessed | tf_op | source)
XLA Modules:
  0.0 46.4 jit_solution(9612523439963666393)
XLA Ops:
  0.0 0.0 copy-start.2
  0.0 0.9 %copy-done.2 = bf16[256,2,256]{2,1,0:T(2,128)(2,1)S(1)} copy-done((bf16[256,2,256]{2,1,0:T(2,128)(2,1)S(1)}, bf16[256,2,256]{2,1,0:T(2,128)(2,1)}, u32[]{:S(2)}) %copy-start.2) | copy-done | bytes 262168
  1.0 0.3 by_cell.1
  1.3 0.7 %collective-permute-start = (bf16[2,144,256]{2,1,0:T(8,128)(2,1)S(1)}, bf16[2,144,256]{2,1,0:T(8,128)(2,1)S(1)}, u32[]{:S(2)}, u32[]{:S(2)}) collective-permute-start(bf16[2,144,256]{2,1,0:T(8,128)(2,1)S(1)} %get-tuple-element.22.block_ref), channel_id=1, source_target_pairs={{0,0},{8,1},{4,2},{12,3},{1,4},{9,5},{5,6},{13,7},{2,8},{10,9},{6,... | collective-permute-start | bytes 442376 | tf_op jit(solution)/shard_map/ppermute | solution.py:74
  2.0 6.6 %collective-permute-start.1 = (bf16[2,144,256]{2,1,0:T(8,128)(2,1)S(1)}, bf16[2,144,256]{2,1,0:T(8,128)(2,1)S(1)}, u32[]{:S(2)}, u32[]{:S(2)}) collective-permute-start(bf16[2,144,256]{2,1,0:T(8,128)(2,1)S(1)} %get-tuple-element.22.block_ref), channel_id=1, source_target_pairs={{4,0},{12,1},{0,2},{8,3},{5,4},{13,5},{1,6},{9,7},{6,8},{14,9},{2,... | collective-permute-start | bytes 442376 | tf_op jit(solution)/shard_map/ppermute | solution.py:74
  8.6 0.5 %collective-permute-start.2 = (bf16[2,144,256]{2,1,0:T(8,128)(2,1)S(1)}, bf16[2,144,256]{2,1,0:T(8,128)(2,1)S(1)}, u32[]{:S(2)}, u32[]{:S(2)}) collective-permute-start(bf16[2,144,256]{2,1,0:T(8,128)(2,1)S(1)} %get-tuple-element.22.block_ref), channel_id=1, source_target_pairs={{8,0},{0,1},{12,2},{4,3},{9,4},{1,5},{13,6},{5,7},{10,8},{2,9},{14... | collective-permute-start | bytes 442376 | tf_op jit(solution)/shard_map/ppermute | solution.py:74
  9.1 4.2 %collective-permute-start.3 = (bf16[2,144,256]{2,1,0:T(8,128)(2,1)S(1)}, bf16[2,144,256]{2,1,0:T(8,128)(2,1)S(1)}, u32[]{:S(2)}, u32[]{:S(2)}) collective-permute-start(bf16[2,144,256]{2,1,0:T(8,128)(2,1)S(1)} %get-tuple-element.22.block_ref), channel_id=1, source_target_pairs={{12,0},{4,1},{8,2},{0,3},{13,4},{5,5},{9,6},{1,7},{14,8},{6,9},{10... | collective-permute-start | bytes 442376 | tf_op jit(solution)/shard_map/ppermute | solution.py:74
  13.3 0.1 collective-permute-start.7
  13.4 0.0 copy-start
  13.4 2.0 %copy-done = bf16[27,256,256]{2,1,0:T(8,128)(2,1)S(1)} copy-done((bf16[27,256,256]{2,1,0:T(8,128)(2,1)S(1)}, bf16[27,256,256]{2,1,0:T(8,128)(2,1)}, u32[]{:S(2)}) %copy-start) | copy-done | bytes 3538968
  15.4 0.0 copy-start.1
  15.4 0.0 collective-permute-done.7.mate_ref
  15.4 0.8 %collective-permute-start.8 = (bf16[4,112,256]{2,1,0:T(8,128)(2,1)S(1)}, bf16[4,112,256]{2,1,0:T(8,128)(2,1)S(1)}, u32[]{:S(2)}, u32[]{:S(2)}) collective-permute-start(bf16[4,112,256]{2,1,0:T(8,128)(2,1)S(1)} %pair.1), channel_id=1, source_target_pairs={{0,0},{8,1},{4,2},{12,3},{1,4},{9,5},{5,6},{13,7},{2,8},{10,9},{6,... | collective-permute-start | bytes 688136 | tf_op jit(solution)/shard_map/ppermute | solution.py:74
  16.2 0.0 collective-permute-done.refs_0_
  16.2 3.5 %collective-permute-start.9 = (bf16[4,112,256]{2,1,0:T(8,128)(2,1)S(1)}, bf16[4,112,256]{2,1,0:T(8,128)(2,1)S(1)}, u32[]{:S(2)}, u32[]{:S(2)}) collective-permute-start(bf16[4,112,256]{2,1,0:T(8,128)(2,1)S(1)} %pair.1), channel_id=1, source_target_pairs={{8,0},{0,1},{12,2},{4,3},{9,4},{1,5},{13,6},{5,7},{10,8},{2,9},{14... | collective-permute-start | bytes 688136 | tf_op jit(solution)/shard_map/ppermute | solution.py:74
  19.8 0.0 collective-permute-done.1.refs_1_
  19.8 0.0 collective-permute-done.2.refs_2_
  19.8 0.0 collective-permute-done.3.refs_3_
  19.8 0.0 copy-done.1
  19.8 4.3 %partial_sums.4 = (f32[272,256]{1,0:T(8,128)S(1)}, f32[272,256]{1,0:T(8,128)S(1)}, f32[272,256]{1,0:T(8,128)S(1)}, f32[272,256]{1,0:T(8,128)S(1)}) custom-call(f32[8,128]{1,0:T(8,128)S(1)} %hold.1.token_ref, bf16[27,256,256]{2,1,0:T(8,128)(2,1)S(1)} %copy-done.1, bf16[2,144,256]{2,1,0:T(8,128)(2,1)S(1)} %collective-permute-done.refs_0_, ...), custom_call_target="tpu_custom_call" | custom-call | flops 3623878656 | bytes 3538944 | tf_op jit(solution)/shard_map/partial_sums/pallas_call | solution.py:242
  24.1 3.6 %collective-permute-start.4 = (f32[272,256]{1,0:T(8,128)S(1)}, f32[272,256]{1,0:T(8,128)S(1)}, u32[]{:S(2)}, u32[]{:S(2)}) collective-permute-start(f32[272,256]{1,0:T(8,128)S(1)} %get-tuple-element.24), channel_id=1, source_target_pairs={{0,4},{4,0},{8,12},{12,8},{1,5},{5,1},{9,13},{13,9},{2,6},{6,2},{1... | collective-permute-start | bytes 835592 | tf_op jit(solution)/shard_map/ppermute | solution.py:333
  27.6 0.1 collective-permute-start.5
  27.7 0.0 collective-permute-done.8.refs_4_
  27.7 0.1 collective-permute-done.9.refs_5_
  27.8 1.4 %partial_sums.5 = (f32[272,256]{1,0:T(8,128)S(1)}, bf16[10,160,768]{2,1,0:T(8,128)(2,1)S(1)}) custom-call(f32[8,128]{1,0:T(8,128)S(1)} %hold.1.token_ref, bf16[27,256,256]{2,1,0:T(8,128)(2,1)S(1)} %copy-done.1, bf16[2,144,256]{2,1,0:T(8,128)(2,1)S(1)} %collective-permute-done.refs_0_, bf16[2,144,256]{2,1,0:T(8,128)(2,1)S(1)} %collective-permute-done.1.refs_1_, ...), custom_call_target="tpu_custom_call" | custom-call | flops 905969664 | bytes 3538944 | tf_op jit(solution)/shard_map/partial_sums/pallas_call | solution.py:242
  29.3 0.4 collective-permute-start.10
  29.6 2.0 %partial_sums.6 = (f32[272,256]{1,0:T(8,128)S(1)}, f32[272,256]{1,0:T(8,128)S(1)}) custom-call(f32[8,128]{1,0:T(8,128)S(1)} %hold.1.token_ref, bf16[27,256,256]{2,1,0:T(8,128)(2,1)S(1)} %copy-done.1, bf16[10,160,768]{2,1,0:T(8,128)(2,1)S(1)} %get-tuple-element.33.window_ref), custom_call_target="tpu_custom_call" | custom-call | flops 1811939328 | bytes 3538944 | tf_op jit(solution)/shard_map/partial_sums/pallas_call | solution.py:242
  31.7 0.3 collective-permute-start.11
  31.9 0.0 collective-permute-done.5
  32.0 0.0 collective-permute-done.4
  32.0 0.0 collective-permute-done.10
  32.1 0.1 select_convert_fusion
  32.2 0.1 fusion.8
  32.3 0.1 fusion.9
  32.4 0.1 pad_maximum_fusion
  32.5 5.6 %collective-permute-start.6 = (f16[272,256]{1,0:T(8,128)(2,1)S(1)}, f16[272,256]{1,0:T(8,128)(2,1)S(1)}, u32[]{:S(2)}, u32[]{:S(2)}) collective-permute-start(f16[272,256]{1,0:T(8,128)(2,1)S(1)} %get-tuple-element.29), channel_id=1, source_target_pairs={{0,8},{4,12},{8,0},{12,4},{1,9},{5,13},{9,1},{13,5},{2,10},{6,14},... | collective-permute-start | bytes 417800 | tf_op jit(solution)/shard_map/ppermute | solution.py:333
  38.1 0.1 collective-permute-start.12
  38.1 1.1 %partial_sums.7 = f32[272,256]{1,0:T(8,128)S(1)} custom-call(f32[8,128]{1,0:T(8,128)S(1)} %hold.1.token_ref, bf16[27,256,256]{2,1,0:T(8,128)(2,1)S(1)} %copy-done.1, bf16[10,160,768]{2,1,0:T(8,128)(2,1)S(1)} %get-tuple-element.33.window_ref), custom_call_target="tpu_custom_call" | custom-call | flops 905969664 | bytes 3538944 | tf_op jit(solution)/shard_map/partial_sums/pallas_call | solution.py:242
  39.3 0.0 collective-permute-done.11
  39.3 3.2 %collective-permute-done.6 = f16[272,256]{1,0:T(8,128)(2,1)S(1)} collective-permute-done((f16[272,256]{1,0:T(8,128)(2,1)S(1)}, f16[272,256]{1,0:T(8,128)(2,1)S(1)}, u32[]{:S(2)}, u32[]{:S(2)}) %collective-permute-start.6) | collective-permute-done | bytes 139296 | tf_op jit(solution)/shard_map/ppermute | solution.py:333
  42.6 0.1 negate_select_fusion.2.refs_1_
  42.7 2.3 %collective-permute-done.12 = f16[272,256]{1,0:T(8,128)(2,1)S(1)} collective-permute-done((f16[272,256]{1,0:T(8,128)(2,1)S(1)}, f16[272,256]{1,0:T(8,128)(2,1)S(1)}, u32[]{:S(2)}, u32[]{:S(2)}) %collective-permute-start.12) | collective-permute-done | bytes 139296 | tf_op jit(solution)/shard_map/ppermute | solution.py:333
  44.9 0.1 negate_select_fusion.refs_3_
  45.0 1.3 %finish.1 = bf16[256,2,256]{2,1,0:T(2,128)(2,1)} custom-call(f32[256,256]{1,0:T(8,128)S(1)} %slice_add_fusion.1.refs_0_, f32[256,256]{1,0:T(8,128)S(1)} %negate_select_fusion.2.refs_1_, f32[256,256]{1,0:T(8,128)S(1)} %slice_add_fusion.refs_2_, f32[256,256]{1,0:T(8,128)S(1)} %negate_select_fusion.refs_3_), custom_call_target="tpu_custom_call" | custom-call | tf_op jit(solution)/shard_map/finish/pallas_call | solution.py:299
  (11 shorter events, 0.2 us)
Async XLA Ops:
  0.0 0.9 %copy-start.2 = (bf16[256,2,256]{2,1,0:T(2,128)(2,1)S(1)}, bf16[256,2,256]{2,1,0:T(2,128)(2,1)}, u32[]{:S(2)}) copy-start(bf16[256,2,256]{2,1,0:T(2,128)(2,1)} %fields_ref.1) | copy-start | bytes 786436
  1.3 14.9 %collective-permute-start = (bf16[2,144,256]{2,1,0:T(8,128)(2,1)S(1)}, bf16[2,144,256]{2,1,0:T(8,128)(2,1)S(1)}, u32[]{:S(2)}, u32[]{:S(2)}) collective-permute-start(bf16[2,144,256]{2,1,0:T(8,128)(2,1)S(1)} %get-tuple-element.22.block_ref), channel_id=1, source_target_pairs={{0,0},{8,1},{4,2},{12,3},{1,4},{9,5},{5,6},{13,7},{2,8},{10,9},{6,... | collective-permute-start | bytes 442376 | tf_op jit(solution)/shard_map/ppermute | solution.py:74
  2.0 17.8 %collective-permute-start.1 = (bf16[2,144,256]{2,1,0:T(8,128)(2,1)S(1)}, bf16[2,144,256]{2,1,0:T(8,128)(2,1)S(1)}, u32[]{:S(2)}, u32[]{:S(2)}) collective-permute-start(bf16[2,144,256]{2,1,0:T(8,128)(2,1)S(1)} %get-tuple-element.22.block_ref), channel_id=1, source_target_pairs={{4,0},{12,1},{0,2},{8,3},{5,4},{13,5},{1,6},{9,7},{6,8},{14,9},{2,... | collective-permute-start | bytes 442376 | tf_op jit(solution)/shard_map/ppermute | solution.py:74
  8.6 11.2 %collective-permute-start.2 = (bf16[2,144,256]{2,1,0:T(8,128)(2,1)S(1)}, bf16[2,144,256]{2,1,0:T(8,128)(2,1)S(1)}, u32[]{:S(2)}, u32[]{:S(2)}) collective-permute-start(bf16[2,144,256]{2,1,0:T(8,128)(2,1)S(1)} %get-tuple-element.22.block_ref), channel_id=1, source_target_pairs={{8,0},{0,1},{12,2},{4,3},{9,4},{1,5},{13,6},{5,7},{10,8},{2,9},{14... | collective-permute-start | bytes 442376 | tf_op jit(solution)/shard_map/ppermute | solution.py:74
  9.1 10.7 %collective-permute-start.3 = (bf16[2,144,256]{2,1,0:T(8,128)(2,1)S(1)}, bf16[2,144,256]{2,1,0:T(8,128)(2,1)S(1)}, u32[]{:S(2)}, u32[]{:S(2)}) collective-permute-start(bf16[2,144,256]{2,1,0:T(8,128)(2,1)S(1)} %get-tuple-element.22.block_ref), channel_id=1, source_target_pairs={{12,0},{4,1},{8,2},{0,3},{13,4},{5,5},{9,6},{1,7},{14,8},{6,9},{10... | collective-permute-start | bytes 442376 | tf_op jit(solution)/shard_map/ppermute | solution.py:74
  13.3 2.1 %collective-permute-start.7 = (bf16[2,112,256]{2,1,0:T(8,128)(2,1)S(1)}, bf16[2,112,256]{2,1,0:T(8,128)(2,1)S(1)}, u32[]{:S(2)}, u32[]{:S(2)}) collective-permute-start(bf16[2,112,256]{2,1,0:T(8,128)(2,1)S(1)} %get-tuple-element.30.own_ref), channel_id=1, source_target_pairs={{0,4},{4,0},{8,12},{12,8},{1,5},{5,1},{9,13},{13,9},{2,6},{6,2},{1... | collective-permute-start | bytes 344072 | tf_op jit(solution)/shard_map/ppermute | solution.py:333
  13.4 2.0 %copy-start = (bf16[27,256,256]{2,1,0:T(8,128)(2,1)S(1)}, bf16[27,256,256]{2,1,0:T(8,128)(2,1)}, u32[]{:S(2)}) copy-start(bf16[27,256,256]{2,1,0:T(8,128)(2,1)} %weight_ref.9) | copy-start | bytes 10616836
  15.4 4.4 %copy-start.1 = (bf16[27,256,256]{2,1,0:T(8,128)(2,1)S(1)}, bf16[27,256,256]{2,1,0:T(8,128)(2,1)}, u32[]{:S(2)}) copy-start(bf16[27,256,256]{2,1,0:T(8,128)(2,1)} %weight_ref.9) | copy-start | bytes 10616836
  15.4 12.3 %collective-permute-start.8 = (bf16[4,112,256]{2,1,0:T(8,128)(2,1)S(1)}, bf16[4,112,256]{2,1,0:T(8,128)(2,1)S(1)}, u32[]{:S(2)}, u32[]{:S(2)}) collective-permute-start(bf16[4,112,256]{2,1,0:T(8,128)(2,1)S(1)} %pair.1), channel_id=1, source_target_pairs={{0,0},{8,1},{4,2},{12,3},{1,4},{9,5},{5,6},{13,7},{2,8},{10,9},{6,... | collective-permute-start | bytes 688136 | tf_op jit(solution)/shard_map/ppermute | solution.py:74
  16.2 11.6 %collective-permute-start.9 = (bf16[4,112,256]{2,1,0:T(8,128)(2,1)S(1)}, bf16[4,112,256]{2,1,0:T(8,128)(2,1)S(1)}, u32[]{:S(2)}, u32[]{:S(2)}) collective-permute-start(bf16[4,112,256]{2,1,0:T(8,128)(2,1)S(1)} %pair.1), channel_id=1, source_target_pairs={{8,0},{0,1},{12,2},{4,3},{9,4},{1,5},{13,6},{5,7},{10,8},{2,9},{14... | collective-permute-start | bytes 688136 | tf_op jit(solution)/shard_map/ppermute | solution.py:74
  24.1 7.9 %collective-permute-start.4 = (f32[272,256]{1,0:T(8,128)S(1)}, f32[272,256]{1,0:T(8,128)S(1)}, u32[]{:S(2)}, u32[]{:S(2)}) collective-permute-start(f32[272,256]{1,0:T(8,128)S(1)} %get-tuple-element.24), channel_id=1, source_target_pairs={{0,4},{4,0},{8,12},{12,8},{1,5},{5,1},{9,13},{13,9},{2,6},{6,2},{1... | collective-permute-start | bytes 835592 | tf_op jit(solution)/shard_map/ppermute | solution.py:333
  27.6 4.3 %collective-permute-start.5 = (f32[272,256]{1,0:T(8,128)S(1)}, f32[272,256]{1,0:T(8,128)S(1)}, u32[]{:S(2)}, u32[]{:S(2)}) collective-permute-start(f32[272,256]{1,0:T(8,128)S(1)} %get-tuple-element.28), channel_id=1, source_target_pairs={{0,4},{4,0},{8,12},{12,8},{1,5},{5,1},{9,13},{13,9},{2,6},{6,2},{1... | collective-permute-start | bytes 835592 | tf_op jit(solution)/shard_map/ppermute | solution.py:333
  29.3 2.8 %collective-permute-start.10 = (f32[272,256]{1,0:T(8,128)S(1)}, f32[272,256]{1,0:T(8,128)S(1)}, u32[]{:S(2)}, u32[]{:S(2)}) collective-permute-start(f32[272,256]{1,0:T(8,128)S(1)} %get-tuple-element.35), channel_id=1, source_target_pairs={{0,4},{4,0},{8,12},{12,8},{1,5},{5,1},{9,13},{13,9},{2,6},{6,2},{1... | collective-permute-start | bytes 835592 | tf_op jit(solution)/shard_map/ppermute | solution.py:333
  31.7 7.6 %collective-permute-start.11 = (f32[272,256]{1,0:T(8,128)S(1)}, f32[272,256]{1,0:T(8,128)S(1)}, u32[]{:S(2)}, u32[]{:S(2)}) collective-permute-start(f32[272,256]{1,0:T(8,128)S(1)} %get-tuple-element.37), channel_id=1, source_target_pairs={{0,4},{4,0},{8,12},{12,8},{1,5},{5,1},{9,13},{13,9},{2,6},{6,2},{1... | collective-permute-start | bytes 835592 | tf_op jit(solution)/shard_map/ppermute | solution.py:333
  32.5 10.0 %collective-permute-start.6 = (f16[272,256]{1,0:T(8,128)(2,1)S(1)}, f16[272,256]{1,0:T(8,128)(2,1)S(1)}, u32[]{:S(2)}, u32[]{:S(2)}) collective-permute-start(f16[272,256]{1,0:T(8,128)(2,1)S(1)} %get-tuple-element.29), channel_id=1, source_target_pairs={{0,8},{4,12},{8,0},{12,4},{1,9},{5,13},{9,1},{13,5},{2,10},{6,14},... | collective-permute-start | bytes 417800 | tf_op jit(solution)/shard_map/ppermute | solution.py:333
  38.1 6.8 %collective-permute-start.12 = (f16[272,256]{1,0:T(8,128)(2,1)S(1)}, f16[272,256]{1,0:T(8,128)(2,1)S(1)}, u32[]{:S(2)}, u32[]{:S(2)}) collective-permute-start(f16[272,256]{1,0:T(8,128)(2,1)S(1)} %get-tuple-element.38), channel_id=1, source_target_pairs={{0,8},{4,12},{8,0},{12,4},{1,9},{5,13},{9,1},{13,5},{2,10},{6,14},... | collective-permute-start | bytes 417800 | tf_op jit(solution)/shard_map/ppermute | solution.py:333

commit v6 on v5

--- a/solution.py
+++ b/solution.py
@@ -29,7 +29,7 @@
 
 
 def paired(index):
-    return index > 0
+    return index >= 0
 
 
 def rounds_of(index, nc):

time: 46.6 us -> 48.4 us (1.039)
  waiting for transfers between devices: 5.61 us -> 7.21 us
    ppermute x7 -> x8, starting transfers between devices: 9.99 us -> 17.8 us  [swapped(): return lax.ppermute(value, 'space', [(i, i ^ 1 << bit) for i in range(ns)])]
    ppermute x6 -> x4, starting transfers between devices: 16.3 us -> 8.78 us  [sent_parts(): parts.append(lax.ppermute(payload, ('space', 'chan'), pairs))]
    ppermute x7 -> x8, waiting for transfers between devices: 5.48 us -> 6.84 us  [swapped(): return lax.ppermute(value, 'space', [(i, i ^ 1 << bit) for i in range(ns)])]
  transfers between devices with their start and end apart: 13 -> 12, of which waited for: 3 -> 4; matrix products, arithmetic and copies ran while one was open for 1% -> 1% of each run, Pallas kernels for 19% -> 18%
where the time goes in v6:
time: 48.4 us; the launch traced here: 48.2 us
  starting transfers between devices  26.5 us (55%)
  Pallas kernels  10.5 us (22%)
  waiting for transfers between devices  7.21 us (15%)
  local copies, waits for them, and re-layouts  2.95 us (6%)
  other arithmetic  0.77 us (2%)
    ppermute x8, starting transfers between devices, swapped(): return lax.ppermute(value, 'space', [(i, i ^ 1 << bit) for i in range(ns)])  17.8 us
    pallas_call x4, Pallas kernels, call(): pl.pallas_call(functools.partial(kernel, plan, jobs), out_shape=out_shape...  8.81 us
    ppermute x4, starting transfers between devices, sent_parts(): parts.append(lax.ppermute(payload, ('space', 'chan'), pairs))  8.78 us
    ppermute x8, waiting for transfers between devices, swapped(): return lax.ppermute(value, 'space', [(i, i ^ 1 << bit) for i in range(ns)])  6.84 us
    unnamed x6, local copies, waits for them, and re-layouts  2.95 us
    pallas_call x1, Pallas kernels, finish(): pl.pallas_call(functools.partial(finish_kernel, [len(pieces) for pieces i...  1.33 us
  transfers between devices with their start and end apart: 12, of which 4 were waited for; matrix products, arithmetic and copies ran while one was open for 1% of the time, Pallas kernels for 18%

profile of v6, /device:TPU:0, one launch (start us, length us, event | category | flops | bytes accessed | tf_op | source)
XLA Modules:
  0.0 48.2 jit_solution(13443574765951895594)
XLA Ops:
  0.0 0.0 copy-start.2
  0.0 0.9 %copy-done.2 = bf16[256,2,256]{2,1,0:T(2,128)(2,1)S(1)} copy-done((bf16[256,2,256]{2,1,0:T(2,128)(2,1)S(1)}, bf16[256,2,256]{2,1,0:T(2,128)(2,1)}, u32[]{:S(2)}) %copy-start.2) | copy-done | bytes 262168
  1.0 0.3 by_cell.1
  1.3 0.5 %collective-permute-start = (bf16[2,144,256]{2,1,0:T(8,128)(2,1)S(1)}, bf16[2,144,256]{2,1,0:T(8,128)(2,1)S(1)}, u32[]{:S(2)}, u32[]{:S(2)}) collective-permute-start(bf16[2,144,256]{2,1,0:T(8,128)(2,1)S(1)} %get-tuple-element.22.block_ref.own_ref), channel_id=1, source_target_pairs={{0,4},{4,0},{8,12},{12,8},{1,5},{5,1},{9,13},{13,9},{2,6},{6,2},{1... | collective-permute-start | bytes 442376 | tf_op jit(solution)/shard_map/ppermute | solution.py:333
  1.8 1.0 %collective-permute-done.mate_ref = bf16[2,144,256]{2,1,0:T(8,128)(2,1)S(1)} collective-permute-done((bf16[2,144,256]{2,1,0:T(8,128)(2,1)S(1)}, bf16[2,144,256]{2,1,0:T(8,128)(2,1)S(1)}, u32[]{:S(2)}, u32[]{:S(2)}) %collective-permute-start) | collective-permute-done | bytes 147488 | tf_op jit(solution)/shard_map/ppermute | solution.py:333
  2.9 0.7 %collective-permute-start.1 = (bf16[4,144,256]{2,1,0:T(8,128)(2,1)S(1)}, bf16[4,144,256]{2,1,0:T(8,128)(2,1)S(1)}, u32[]{:S(2)}, u32[]{:S(2)}) collective-permute-start(bf16[4,144,256]{2,1,0:T(8,128)(2,1)S(1)} %pair.2), channel_id=1, source_target_pairs={{0,0},{8,1},{4,2},{12,3},{1,4},{9,5},{5,6},{13,7},{2,8},{10,9},{6,... | collective-permute-start | bytes 884744 | tf_op jit(solution)/shard_map/ppermute | solution.py:74
  3.5 4.2 %collective-permute-start.2 = (bf16[4,144,256]{2,1,0:T(8,128)(2,1)S(1)}, bf16[4,144,256]{2,1,0:T(8,128)(2,1)S(1)}, u32[]{:S(2)}, u32[]{:S(2)}) collective-permute-start(bf16[4,144,256]{2,1,0:T(8,128)(2,1)S(1)} %pair.2), channel_id=1, source_target_pairs={{8,0},{0,1},{12,2},{4,3},{9,4},{1,5},{13,6},{5,7},{10,8},{2,9},{14... | collective-permute-start | bytes 884744 | tf_op jit(solution)/shard_map/ppermute | solution.py:74
  7.8 3.0 %collective-permute-start.6 = (bf16[2,112,256]{2,1,0:T(8,128)(2,1)S(1)}, bf16[2,112,256]{2,1,0:T(8,128)(2,1)S(1)}, u32[]{:S(2)}, u32[]{:S(2)}) collective-permute-start(bf16[2,112,256]{2,1,0:T(8,128)(2,1)S(1)} %get-tuple-element.30.own_ref), channel_id=1, source_target_pairs={{0,4},{4,0},{8,12},{12,8},{1,5},{5,1},{9,13},{13,9},{2,6},{6,2},{1... | collective-permute-start | bytes 344072 | tf_op jit(solution)/shard_map/ppermute | solution.py:333
  10.8 0.0 copy-start
  10.8 2.0 %copy-done = bf16[27,256,256]{2,1,0:T(8,128)(2,1)S(1)} copy-done((bf16[27,256,256]{2,1,0:T(8,128)(2,1)S(1)}, bf16[27,256,256]{2,1,0:T(8,128)(2,1)}, u32[]{:S(2)}) %copy-start) | copy-done | bytes 3538968
  12.8 0.0 copy-start.1
  12.8 0.0 collective-permute-done.6.mate_ref
  12.9 0.8 %collective-permute-start.7 = (bf16[4,112,256]{2,1,0:T(8,128)(2,1)S(1)}, bf16[4,112,256]{2,1,0:T(8,128)(2,1)S(1)}, u32[]{:S(2)}, u32[]{:S(2)}) collective-permute-start(bf16[4,112,256]{2,1,0:T(8,128)(2,1)S(1)} %pair.3), channel_id=1, source_target_pairs={{0,0},{8,1},{4,2},{12,3},{1,4},{9,5},{5,6},{13,7},{2,8},{10,9},{6,... | collective-permute-start | bytes 688136 | tf_op jit(solution)/shard_map/ppermute | solution.py:74
  13.7 3.1 %collective-permute-start.8 = (bf16[4,112,256]{2,1,0:T(8,128)(2,1)S(1)}, bf16[4,112,256]{2,1,0:T(8,128)(2,1)S(1)}, u32[]{:S(2)}, u32[]{:S(2)}) collective-permute-start(bf16[4,112,256]{2,1,0:T(8,128)(2,1)S(1)} %pair.3), channel_id=1, source_target_pairs={{8,0},{0,1},{12,2},{4,3},{9,4},{1,5},{13,6},{5,7},{10,8},{2,9},{14... | collective-permute-start | bytes 688136 | tf_op jit(solution)/shard_map/ppermute | solution.py:74
  16.7 0.0 collective-permute-done.1.refs_0_
  16.7 0.4 collective-permute-done.2.refs_1_
  17.1 0.0 copy-done.1
  17.1 4.2 %partial_sums.4 = (f32[272,256]{1,0:T(8,128)S(1)}, f32[272,256]{1,0:T(8,128)S(1)}, f32[272,256]{1,0:T(8,128)S(1)}, f32[272,256]{1,0:T(8,128)S(1)}) custom-call(f32[8,128]{1,0:T(8,128)S(1)} %hold.1.token_ref, bf16[27,256,256]{2,1,0:T(8,128)(2,1)S(1)} %copy-done.1, bf16[4,144,256]{2,1,0:T(8,128)(2,1)S(1)} %collective-permute-done.1.refs_0_, ...), custom_call_target="tpu_custom_call" | custom-call | flops 3623878656 | bytes 3538944 | tf_op jit(solution)/shard_map/partial_sums/pallas_call | solution.py:242
  21.3 1.9 %collective-permute-start.4 = (f32[272,256]{1,0:T(8,128)S(1)}, f32[272,256]{1,0:T(8,128)S(1)}, u32[]{:S(2)}, u32[]{:S(2)}) collective-permute-start(f32[272,256]{1,0:T(8,128)S(1)} %get-tuple-element.28), channel_id=1, source_target_pairs={{0,4},{4,0},{8,12},{12,8},{1,5},{5,1},{9,13},{13,9},{2,6},{6,2},{1... | collective-permute-start | bytes 835592 | tf_op jit(solution)/shard_map/ppermute | solution.py:333
  23.2 0.0 collective-permute-done.7.refs_2_
  23.2 0.0 collective-permute-done.8.refs_3_
  23.2 1.4 %partial_sums.5 = (f32[272,256]{1,0:T(8,128)S(1)}, bf16[10,160,768]{2,1,0:T(8,128)(2,1)S(1)}) custom-call(f32[8,128]{1,0:T(8,128)S(1)} %hold.1.token_ref, bf16[27,256,256]{2,1,0:T(8,128)(2,1)S(1)} %copy-done.1, bf16[4,144,256]{2,1,0:T(8,128)(2,1)S(1)} %collective-permute-done.1.refs_0_, bf16[4,144,256]{2,1,0:T(8,128)(2,1)S(1)} %collective-permute-done.2.refs_1_, ...), custom_call_target="tpu_custom_call" | custom-call | flops 905969664 | bytes 3538944 | tf_op jit(solution)/shard_map/partial_sums/pallas_call | solution.py:242
  24.7 3.3 %collective-permute-start.9 = (f32[272,256]{1,0:T(8,128)S(1)}, f32[272,256]{1,0:T(8,128)S(1)}, u32[]{:S(2)}, u32[]{:S(2)}) collective-permute-start(f32[272,256]{1,0:T(8,128)S(1)} %get-tuple-element.35), channel_id=1, source_target_pairs={{0,4},{4,0},{8,12},{12,8},{1,5},{5,1},{9,13},{13,9},{2,6},{6,2},{1... | collective-permute-start | bytes 835592 | tf_op jit(solution)/shard_map/ppermute | solution.py:333
  28.0 0.1 collective-permute-start.3
  28.1 2.0 %partial_sums.6 = (f32[272,256]{1,0:T(8,128)S(1)}, f32[272,256]{1,0:T(8,128)S(1)}) custom-call(f32[8,128]{1,0:T(8,128)S(1)} %hold.1.token_ref, bf16[27,256,256]{2,1,0:T(8,128)(2,1)S(1)} %copy-done.1, bf16[10,160,768]{2,1,0:T(8,128)(2,1)S(1)} %get-tuple-element.33.window_ref), custom_call_target="tpu_custom_call" | custom-call | flops 1811939328 | bytes 3538944 | tf_op jit(solution)/shard_map/partial_sums/pallas_call | solution.py:242
  30.1 0.5 %collective-permute-start.10 = (f32[272,256]{1,0:T(8,128)S(1)}, f32[272,256]{1,0:T(8,128)S(1)}, u32[]{:S(2)}, u32[]{:S(2)}) collective-permute-start(f32[272,256]{1,0:T(8,128)S(1)} %get-tuple-element.37), channel_id=1, source_target_pairs={{0,4},{4,0},{8,12},{12,8},{1,5},{5,1},{9,13},{13,9},{2,6},{6,2},{1... | collective-permute-start | bytes 835592 | tf_op jit(solution)/shard_map/ppermute | solution.py:333
  30.6 0.0 collective-permute-done.4
  30.6 0.0 collective-permute-done.9
  30.7 0.1 select_convert_fusion
  30.8 0.1 fusion.8
  30.9 0.1 fusion.9
  31.0 0.1 pad_maximum_fusion
  31.1 8.4 %collective-permute-start.5 = (f16[272,256]{1,0:T(8,128)(2,1)S(1)}, f16[272,256]{1,0:T(8,128)(2,1)S(1)}, u32[]{:S(2)}, u32[]{:S(2)}) collective-permute-start(f16[272,256]{1,0:T(8,128)(2,1)S(1)} %get-tuple-element.29), channel_id=1, source_target_pairs={{0,8},{4,12},{8,0},{12,4},{1,9},{5,13},{9,1},{13,5},{2,10},{6,14},... | collective-permute-start | bytes 417800 | tf_op jit(solution)/shard_map/ppermute | solution.py:333
  39.5 1.1 %partial_sums.7 = f32[272,256]{1,0:T(8,128)S(1)} custom-call(f32[8,128]{1,0:T(8,128)S(1)} %hold.1.token_ref, bf16[27,256,256]{2,1,0:T(8,128)(2,1)S(1)} %copy-done.1, bf16[10,160,768]{2,1,0:T(8,128)(2,1)S(1)} %get-tuple-element.33.window_ref), custom_call_target="tpu_custom_call" | custom-call | flops 905969664 | bytes 3538944 | tf_op jit(solution)/shard_map/partial_sums/pallas_call | solution.py:242
  40.6 0.1 collective-permute-start.11
  40.7 0.0 collective-permute-done.3
  40.7 0.0 collective-permute-done.10
  40.8 3.2 %collective-permute-done.5 = f16[272,256]{1,0:T(8,128)(2,1)S(1)} collective-permute-done((f16[272,256]{1,0:T(8,128)(2,1)S(1)}, f16[272,256]{1,0:T(8,128)(2,1)S(1)}, u32[]{:S(2)}, u32[]{:S(2)}) %collective-permute-start.5) | collective-permute-done | bytes 139296 | tf_op jit(solution)/shard_map/ppermute | solution.py:333
  44.0 0.1 negate_select_fusion.2.refs_1_
  44.1 2.6 %collective-permute-done.11 = f16[272,256]{1,0:T(8,128)(2,1)S(1)} collective-permute-done((f16[272,256]{1,0:T(8,128)(2,1)S(1)}, f16[272,256]{1,0:T(8,128)(2,1)S(1)}, u32[]{:S(2)}, u32[]{:S(2)}) %collective-permute-start.11) | collective-permute-done | bytes 139296 | tf_op jit(solution)/shard_map/ppermute | solution.py:333
  46.7 0.1 negate_select_fusion.refs_3_
  46.8 1.3 %finish.1 = bf16[256,2,256]{2,1,0:T(2,128)(2,1)} custom-call(f32[256,256]{1,0:T(8,128)S(1)} %slice_add_fusion.1.refs_0_, f32[256,256]{1,0:T(8,128)S(1)} %negate_select_fusion.2.refs_1_, f32[256,256]{1,0:T(8,128)S(1)} %slice_add_fusion.refs_2_, f32[256,256]{1,0:T(8,128)S(1)} %negate_select_fusion.refs_3_), custom_call_target="tpu_custom_call" | custom-call | tf_op jit(solution)/shard_map/finish/pallas_call | solution.py:299
  (12 shorter events, 0.3 us)
Async XLA Ops:
  0.0 0.9 %copy-start.2 = (bf16[256,2,256]{2,1,0:T(2,128)(2,1)S(1)}, bf16[256,2,256]{2,1,0:T(2,128)(2,1)}, u32[]{:S(2)}) copy-start(bf16[256,2,256]{2,1,0:T(2,128)(2,1)} %fields_ref.1) | copy-start | bytes 786436
  1.3 1.5 %collective-permute-start = (bf16[2,144,256]{2,1,0:T(8,128)(2,1)S(1)}, bf16[2,144,256]{2,1,0:T(8,128)(2,1)S(1)}, u32[]{:S(2)}, u32[]{:S(2)}) collective-permute-start(bf16[2,144,256]{2,1,0:T(8,128)(2,1)S(1)} %get-tuple-element.22.block_ref.own_ref), channel_id=1, source_target_pairs={{0,4},{4,0},{8,12},{12,8},{1,5},{5,1},{9,13},{13,9},{2,6},{6,2},{1... | collective-permute-start | bytes 442376 | tf_op jit(solution)/shard_map/ppermute | solution.py:333
  2.9 13.9 %collective-permute-start.1 = (bf16[4,144,256]{2,1,0:T(8,128)(2,1)S(1)}, bf16[4,144,256]{2,1,0:T(8,128)(2,1)S(1)}, u32[]{:S(2)}, u32[]{:S(2)}) collective-permute-start(bf16[4,144,256]{2,1,0:T(8,128)(2,1)S(1)} %pair.2), channel_id=1, source_target_pairs={{0,0},{8,1},{4,2},{12,3},{1,4},{9,5},{5,6},{13,7},{2,8},{10,9},{6,... | collective-permute-start | bytes 884744 | tf_op jit(solution)/shard_map/ppermute | solution.py:74
  3.5 13.5 %collective-permute-start.2 = (bf16[4,144,256]{2,1,0:T(8,128)(2,1)S(1)}, bf16[4,144,256]{2,1,0:T(8,128)(2,1)S(1)}, u32[]{:S(2)}, u32[]{:S(2)}) collective-permute-start(bf16[4,144,256]{2,1,0:T(8,128)(2,1)S(1)} %pair.2), channel_id=1, source_target_pairs={{8,0},{0,1},{12,2},{4,3},{9,4},{1,5},{13,6},{5,7},{10,8},{2,9},{14... | collective-permute-start | bytes 884744 | tf_op jit(solution)/shard_map/ppermute | solution.py:74
  7.8 5.0 %collective-permute-start.6 = (bf16[2,112,256]{2,1,0:T(8,128)(2,1)S(1)}, bf16[2,112,256]{2,1,0:T(8,128)(2,1)S(1)}, u32[]{:S(2)}, u32[]{:S(2)}) collective-permute-start(bf16[2,112,256]{2,1,0:T(8,128)(2,1)S(1)} %get-tuple-element.30.own_ref), channel_id=1, source_target_pairs={{0,4},{4,0},{8,12},{12,8},{1,5},{5,1},{9,13},{13,9},{2,6},{6,2},{1... | collective-permute-start | bytes 344072 | tf_op jit(solution)/shard_map/ppermute | solution.py:333
  10.8 2.0 %copy-start = (bf16[27,256,256]{2,1,0:T(8,128)(2,1)S(1)}, bf16[27,256,256]{2,1,0:T(8,128)(2,1)}, u32[]{:S(2)}) copy-start(bf16[27,256,256]{2,1,0:T(8,128)(2,1)} %weight_ref.9) | copy-start | bytes 10616836
  12.8 4.3 %copy-start.1 = (bf16[27,256,256]{2,1,0:T(8,128)(2,1)S(1)}, bf16[27,256,256]{2,1,0:T(8,128)(2,1)}, u32[]{:S(2)}) copy-start(bf16[27,256,256]{2,1,0:T(8,128)(2,1)} %weight_ref.9) | copy-start | bytes 10616836
  12.9 10.4 %collective-permute-start.7 = (bf16[4,112,256]{2,1,0:T(8,128)(2,1)S(1)}, bf16[4,112,256]{2,1,0:T(8,128)(2,1)S(1)}, u32[]{:S(2)}, u32[]{:S(2)}) collective-permute-start(bf16[4,112,256]{2,1,0:T(8,128)(2,1)S(1)} %pair.3), channel_id=1, source_target_pairs={{0,0},{8,1},{4,2},{12,3},{1,4},{9,5},{5,6},{13,7},{2,8},{10,9},{6,... | collective-permute-start | bytes 688136 | tf_op jit(solution)/shard_map/ppermute | solution.py:74
  13.7 9.6 %collective-permute-start.8 = (bf16[4,112,256]{2,1,0:T(8,128)(2,1)S(1)}, bf16[4,112,256]{2,1,0:T(8,128)(2,1)S(1)}, u32[]{:S(2)}, u32[]{:S(2)}) collective-permute-start(bf16[4,112,256]{2,1,0:T(8,128)(2,1)S(1)} %pair.3), channel_id=1, source_target_pairs={{8,0},{0,1},{12,2},{4,3},{9,4},{1,5},{13,6},{5,7},{10,8},{2,9},{14... | collective-permute-start | bytes 688136 | tf_op jit(solution)/shard_map/ppermute | solution.py:74
  21.3 9.2 %collective-permute-start.4 = (f32[272,256]{1,0:T(8,128)S(1)}, f32[272,256]{1,0:T(8,128)S(1)}, u32[]{:S(2)}, u32[]{:S(2)}) collective-permute-start(f32[272,256]{1,0:T(8,128)S(1)} %get-tuple-element.28), channel_id=1, source_target_pairs={{0,4},{4,0},{8,12},{12,8},{1,5},{5,1},{9,13},{13,9},{2,6},{6,2},{1... | collective-permute-start | bytes 835592 | tf_op jit(solution)/shard_map/ppermute | solution.py:333
  24.7 6.0 %collective-permute-start.9 = (f32[272,256]{1,0:T(8,128)S(1)}, f32[272,256]{1,0:T(8,128)S(1)}, u32[]{:S(2)}, u32[]{:S(2)}) collective-permute-start(f32[272,256]{1,0:T(8,128)S(1)} %get-tuple-element.35), channel_id=1, source_target_pairs={{0,4},{4,0},{8,12},{12,8},{1,5},{5,1},{9,13},{13,9},{2,6},{6,2},{1... | collective-permute-start | bytes 835592 | tf_op jit(solution)/shard_map/ppermute | solution.py:333
  28.0 12.7 %collective-permute-start.3 = (f32[272,256]{1,0:T(8,128)S(1)}, f32[272,256]{1,0:T(8,128)S(1)}, u32[]{:S(2)}, u32[]{:S(2)}) collective-permute-start(f32[272,256]{1,0:T(8,128)S(1)} %get-tuple-element.24), channel_id=1, source_target_pairs={{0,4},{4,0},{8,12},{12,8},{1,5},{5,1},{9,13},{13,9},{2,6},{6,2},{1... | collective-permute-start | bytes 835592 | tf_op jit(solution)/shard_map/ppermute | solution.py:333
  30.1 10.7 %collective-permute-start.10 = (f32[272,256]{1,0:T(8,128)S(1)}, f32[272,256]{1,0:T(8,128)S(1)}, u32[]{:S(2)}, u32[]{:S(2)}) collective-permute-start(f32[272,256]{1,0:T(8,128)S(1)} %get-tuple-element.37), channel_id=1, source_target_pairs={{0,4},{4,0},{8,12},{12,8},{1,5},{5,1},{9,13},{13,9},{2,6},{6,2},{1... | collective-permute-start | bytes 835592 | tf_op jit(solution)/shard_map/ppermute | solution.py:333
  31.1 12.9 %collective-permute-start.5 = (f16[272,256]{1,0:T(8,128)(2,1)S(1)}, f16[272,256]{1,0:T(8,128)(2,1)S(1)}, u32[]{:S(2)}, u32[]{:S(2)}) collective-permute-start(f16[272,256]{1,0:T(8,128)(2,1)S(1)} %get-tuple-element.29), channel_id=1, source_target_pairs={{0,8},{4,12},{8,0},{12,4},{1,9},{5,13},{9,1},{13,5},{2,10},{6,14},... | collective-permute-start | bytes 417800 | tf_op jit(solution)/shard_map/ppermute | solution.py:333
  40.6 6.1 %collective-permute-start.11 = (f16[272,256]{1,0:T(8,128)(2,1)S(1)}, f16[272,256]{1,0:T(8,128)(2,1)S(1)}, u32[]{:S(2)}, u32[]{:S(2)}) collective-permute-start(f16[272,256]{1,0:T(8,128)(2,1)S(1)} %get-tuple-element.38), channel_id=1, source_target_pairs={{0,8},{4,12},{8,0},{12,4},{1,9},{5,13},{9,1},{13,5},{2,10},{6,14},... | collective-permute-start | bytes 417800 | tf_op jit(solution)/shard_map/ppermute | solution.py:333
